TPU v7x, 128 devices: a whole 4x4x4 slice. The times are simulated.
128 devices in a mesh: lon: 16 (over y, x), lat: 8 (over z, core).
Axes of the slice: x: 4, y: 4, z: 4, core: 2. Of those that a mesh axis runs over, the one named last changes fastest.
Arguments:
- background_sigma: float32 [25, 192, 2048], P(None, 'lat', 'lon'), may hold values from 0.1 to 6, as said below
- scale_lon: float32 [192, 2048], P('lat', 'lon'), may hold values from 3 to 12
- scale_lat: float32 [192, 2048], P('lat', 'lon'), may hold values from 3 to 12
- obs_owner: int32 [524288], P(('lon', 'lat')), may hold values from 0 to 127, as said below
- obs_count: int32 [128], P(('lon', 'lat')), may hold values from 2048 to 4096, as said below
- obs_cell: int32 [524288], P(('lon', 'lat')), may hold values from 0 to 2942, as said below
- obs_level: int32 [524288], P(('lon', 'lat')), may hold values from 0 to 24
- obs_weight: float32 [4, 524288], P(None, ('lon', 'lat')), may hold values from 0 to 1
- obs_value: float32 [524288], P(('lon', 'lat')), may hold values from -6 to 6
- obs_precision: float32 [524288], P(('lon', 'lat')), may hold values from 5 to 50
Outputs:
- control: float32 [25, 192, 2048], P(None, 'lat', 'lon')
- increment: float32 [25, 192, 2048], P(None, 'lat', 'lon')
Inputs may be any that keep to these rules, and one draw needn't show every extreme that they name: `obs_owner`: among the live slots of one device at most 64 name one owner, and in every draw some owner is named by exactly 64 live slots of every device. `obs_count`: some device has all 4096 slots live. Row obs_cell // 128 is below 23 and column obs_cell mod 128 below 127, so all four corners lie in the owner's tile. `background_sigma`: Positive.
All inputs are finite; a program needn't handle non-finite values.
Results may differ from a plain program's by a relative error of at most 0.012.
Values sent between devices are 32-bit elements; how exact they have to be, the bound alone decides.
No kernel may reach another device: no remote copies, remote signals or barrier semaphores. Data moves between devices by JAX's collectives and lax.ppermute only.
A program may use at most 64 MiB of HBM per device.

v0:
```python
import jax
import jax.numpy as jnp
from jax import lax
from jax.sharding import PartitionSpec as P

TAPS = 41
ITERS = 2


HIGHEST = lax.Precision.HIGHEST


def padded_2(block, sides, width, periodic):
    for axis, dim in sides:
        count = lax.axis_size(axis)
        forward = [(i, i + 1) for i in range(count - 1)]
        if periodic:
            forward.append((count - 1, 0))
        backward = [(target, source) for source, target in forward]
        low = lax.ppermute(
            lax.slice_in_dim(block, block.shape[dim] - width, None, axis=dim), axis, forward
        )
        high = lax.ppermute(lax.slice_in_dim(block, 0, width, axis=dim), axis, backward)
        block = jnp.concatenate([low, block, high], axis=dim)
    return block


def band_matrix(factor):
    length = factor.shape[1]
    middle = TAPS // 2
    target = jnp.arange(length, dtype=jnp.int32)[:, None]
    source = jnp.arange(length + TAPS - 1, dtype=jnp.int32)[None, :]
    offset = source - target
    inside = jnp.logical_and(offset >= 0, offset < TAPS)
    distance = (offset - middle).astype(jnp.float32)
    raw_weight = jnp.where(
        inside[None], jnp.exp(-(distance * distance)[None] * factor[:, :, None]), 0.0
    )
    return raw_weight / jnp.sum(raw_weight, axis=2, keepdims=True)


def lon_extend(grid_field):
    return padded_2(grid_field, (("lon", 2),), TAPS // 2, True)


def lat_extend(grid_field):
    return padded_2(grid_field, (("lat", 1),), TAPS // 2, False)


def fold_rims(padded, axis_dim, extend):
    middle = TAPS // 2
    length = padded.shape[axis_dim] - 2 * middle
    upper_rim = lax.slice_in_dim(padded, 0, middle, axis=axis_dim)
    lower_rim = lax.slice_in_dim(padded, length + middle, length + 2 * middle, axis=axis_dim)
    nearby = extend(jnp.concatenate([upper_rim, lower_rim], axis=axis_dim))
    from_before = lax.slice_in_dim(nearby, 0, middle, axis=axis_dim)
    from_after = lax.slice_in_dim(nearby, 3 * middle, 4 * middle, axis=axis_dim)
    interior = lax.slice_in_dim(padded, middle, length + middle, axis=axis_dim)
    widths_before = [(0, 0), (0, 0), (0, 0)]
    widths_before[axis_dim] = (0, length - middle)
    widths_after = [(0, 0), (0, 0), (0, 0)]
    widths_after[axis_dim] = (length - middle, 0)
    return interior + jnp.pad(from_before, widths_before) + jnp.pad(from_after, widths_after)


def lon_apply(wide_cols, lon_mats):
    pieces = []
    for number, matrix in enumerate(lon_mats):
        pieces.append(jnp.einsum("jim,ljm->lji", matrix, wide_cols, precision=HIGHEST))
    return pieces[0]


def lon_spread(gradient, lon_mats, block_width):
    padded = jnp.zeros(
        (gradient.shape[0], gradient.shape[1], gradient.shape[2] + TAPS - 1), jnp.float32
    )
    for number, matrix in enumerate(lon_mats):
        offset_cols = number * block_width
        contrib = jnp.einsum("jim,lji->ljm", matrix, gradient, precision=HIGHEST)
        padded = padded.at[:, :, offset_cols : offset_cols + block_width + TAPS - 1].add(contrib)
    return padded


def lat_apply(wide_rows, lat_matrix):
    return jnp.einsum("ijm,lmi->lji", lat_matrix, wide_rows, precision=HIGHEST)


def lat_spread(gradient, lat_matrix):
    return jnp.einsum("ijm,lji->lmi", lat_matrix, gradient, precision=HIGHEST)


def squares(residual):
    return lax.psum(jnp.sum(residual * residual), ("lon", "lat"))


def lon_matrices(scale_rows):
    mats = [band_matrix(0.5 / (scale_rows * scale_rows))]
    return mats


def body(
    background_sigma,
    scale_lon,
    scale_lat,
    obs_owner,
    obs_count,
    obs_cell,
    obs_level,
    obs_weight,
    obs_value,
    obs_precision,
):
    level_count, row_count, column_count = background_sigma.shape
    block_width = min(128, column_count)
    scale_turned = scale_lat.T
    lat_matrix = band_matrix(0.5 / (scale_turned * scale_turned))
    lat_count = lax.axis_size("lat")
    lon_mats = lon_matrices(scale_lon)

    def forward(grid_field):
        return background_sigma * lat_apply(
            lat_extend(lon_apply(lon_extend(grid_field), lon_mats)), lat_matrix
        )

    def adjoint(gradient):
        rows_back = fold_rims(lat_spread(background_sigma * gradient, lat_matrix), 1, lat_extend)
        return fold_rims(lon_spread(rows_back, lon_mats, block_width), 2, lon_extend)

    lon_count = lax.axis_size("lon")
    device_count = lon_count * lat_count
    obs_slots = obs_owner.shape[0]
    capacity = 2 * obs_slots // device_count
    slot_index = jnp.arange(obs_slots, dtype=jnp.int32)
    live_slot = slot_index < obs_count[0]
    sort_key = jnp.where(live_slot, obs_owner, device_count)
    ordering = jnp.argsort(sort_key, stable=True)
    ranked = sort_key[ordering]
    first_seen = jnp.searchsorted(ranked, ranked, side="left")
    placing = jnp.where(
        ranked < device_count, ranked * capacity + slot_index - first_seen, device_count * capacity
    )
    local_index = obs_level * (row_count * column_count) + obs_cell
    payload = jnp.concatenate(
        [obs_weight, obs_precision[None], (obs_precision * obs_value)[None]], axis=0
    )[:, ordering]
    float_buffer = (
        jnp.zeros((6, device_count * capacity + 1), jnp.float32).at[:, placing].set(payload)[:, :-1]
    )
    index_buffer = (
        jnp.zeros((device_count * capacity + 1,), jnp.int32)
        .at[placing]
        .set(local_index[ordering])[:-1]
    )
    got_floats, got_index = (
        lax.all_to_all(
            float_buffer.reshape(6, device_count, capacity),
            ("lon", "lat"),
            split_axis=1,
            concat_axis=1,
            tiled=True,
        ),
        lax.all_to_all(
            index_buffer.reshape(1, device_count, capacity),
            ("lon", "lat"),
            split_axis=1,
            concat_axis=1,
            tiled=True,
        ),
    )
    got_floats = got_floats.reshape(6, -1)
    got_index = got_index.reshape(-1)
    corner_weight = got_floats[0:4]
    precision_obs = got_floats[4]
    weighted_value = got_floats[5]
    corner_step = jnp.array([0, 1, column_count, column_count + 1], jnp.int32)
    corner = got_index[None, :] + corner_step[:, None]
    total_cells = level_count * row_count * column_count

    def spread(values):
        flat = (
            jnp.zeros((total_cells,), jnp.float32)
            .at[corner.reshape(-1)]
            .add((corner_weight * values[None]).reshape(-1))
        )
        return flat.reshape(background_sigma.shape)

    residual = adjoint(spread(weighted_value))
    direction = residual
    control = jnp.zeros_like(residual)
    increment = jnp.zeros_like(residual)
    norm_now = squares(residual)
    for iteration in range(ITERS):
        image_field = forward(direction)
        product = direction + adjoint(
            spread(precision_obs * jnp.sum(corner_weight * image_field.reshape(-1)[corner], axis=0))
        )
        curvature = lax.psum(jnp.sum(direction * product), ("lon", "lat"))
        step_size = norm_now / curvature
        control = control + step_size * direction
        increment = increment + step_size * image_field
        if iteration + 1 < ITERS:
            residual = residual - step_size * product
            norm_next = squares(residual)
            direction = residual + norm_next / norm_now * direction
            norm_now = norm_next
    return (control, increment)


def solution(mesh):
    return jax.shard_map(
        body,
        mesh=mesh,
        in_specs=(
            P(None, "lat", "lon"),
            P("lat", "lon"),
            P("lat", "lon"),
            P(("lon", "lat")),
            P(("lon", "lat")),
            P(("lon", "lat")),
            P(("lon", "lat")),
            P(None, ("lon", "lat")),
            P(("lon", "lat")),
            P(("lon", "lat")),
        ),
        out_specs=(P(None, "lat", "lon"), P(None, "lat", "lon")),
        check_vma=False,
    )
```

profile of v0, /device:TPU:1, one launch (start us, length us, event | category | flops | bytes accessed | tf_op | source)
XLA Modules:
  0.0 1875.7 jit_solution(4446213651238474429)
XLA Ops:
  8.5 23.0 %gather_fusion.1 = s32[4096]{0:T(1024)S(1)} fusion(s32[4096]{0:T(1024)S(1)} %fusion.50, s32[4096]{0:T(1024)S(1)} %get-tuple-element.190), kind=kCustom, calls=%fused_computation.1 | custom fusion | bytes 49152 | tf_op jit(solution)/shard_map/gather | solution.py:137
  31.6 23.0 %gather_fusion.2 = s32[4096]{0:T(1024)S(1)} fusion(s32[4096]{0:T(1024)S(1)} %get-tuple-element.191, s32[4096]{0:T(1024)S(1)} %get-tuple-element.190), kind=kCustom, calls=%fused_computation.2 | custom fusion | bytes 49152 | tf_op jit(solution)/shard_map/gather | solution.py:152
  54.7 300.6 %while.31 = (s32[]{:T(128)}, u32[4096]{0:T(1024)S(1)}, u32[4096]{0:T(1024)S(1)}, s32[4096]{0:T(1024)S(1)}, s32[]{:T(128)}, /*index=5*/s32[]{:T(128)}, s32[]{}) while((s32[]{:T(128)}, u32[4096]{0:T(1024)S(1)}, u32[4096]{0:T(1024)S(1)}, s32[4096]{0:T(1024)S(1)}, s32[]{:T(128)}, /*index=5*/s32[]{:T(128)}, s32[]{}) %tuple.78), condition=%wide.region_2.3_spmd.clone, body=%wide.region_1.2_spmd.clone.sunk | while | flops 77828 | bytes 270437 | solution.py:138
  54.7 23.0 %gather_fusion = s32[4096]{0:T(1024)S(1)} fusion(s32[4096]{0:T(1024)S(1)} %get-tuple-element.238, u32[4096]{0:T(1024)S(1)} %broadcast_clamp_fusion.3), kind=kCustom, calls=%fused_computation.clone.clone.1 | custom fusion | bytes 49152 | tf_op jit(solution)/shard_map/jit(searchsorted)/jit(_searchsorted_scan_impl)/vmap(jit(_searchsorted_scan_impl))/while/body/eval_jaxpr/gather | solution.py:138
  77.8 23.0 %gather_fusion = s32[4096]{0:T(1024)S(1)} fusion(s32[4096]{0:T(1024)S(1)} %get-tuple-element.238, u32[4096]{0:T(1024)S(1)} %broadcast_clamp_fusion.3), kind=kCustom, calls=%fused_computation.clone.clone.1 | custom fusion | bytes 49152 | tf_op jit(solution)/shard_map/jit(searchsorted)/jit(_searchsorted_scan_impl)/vmap(jit(_searchsorted_scan_impl))/while/body/eval_jaxpr/gather | solution.py:138
  101.0 23.0 %gather_fusion = s32[4096]{0:T(1024)S(1)} fusion(s32[4096]{0:T(1024)S(1)} %get-tuple-element.238, u32[4096]{0:T(1024)S(1)} %broadcast_clamp_fusion.3), kind=kCustom, calls=%fused_computation.clone.clone.1 | custom fusion | bytes 49152 | tf_op jit(solution)/shard_map/jit(searchsorted)/jit(_searchsorted_scan_impl)/vmap(jit(_searchsorted_scan_impl))/while/body/eval_jaxpr/gather | solution.py:138
  124.1 23.0 %gather_fusion = s32[4096]{0:T(1024)S(1)} fusion(s32[4096]{0:T(1024)S(1)} %get-tuple-element.238, u32[4096]{0:T(1024)S(1)} %broadcast_clamp_fusion.3), kind=kCustom, calls=%fused_computation.clone.clone.1 | custom fusion | bytes 49152 | tf_op jit(solution)/shard_map/jit(searchsorted)/jit(_searchsorted_scan_impl)/vmap(jit(_searchsorted_scan_impl))/while/body/eval_jaxpr/gather | solution.py:138
  147.2 23.0 %gather_fusion = s32[4096]{0:T(1024)S(1)} fusion(s32[4096]{0:T(1024)S(1)} %get-tuple-element.238, u32[4096]{0:T(1024)S(1)} %broadcast_clamp_fusion.3), kind=kCustom, calls=%fused_computation.clone.clone.1 | custom fusion | bytes 49152 | tf_op jit(solution)/shard_map/jit(searchsorted)/jit(_searchsorted_scan_impl)/vmap(jit(_searchsorted_scan_impl))/while/body/eval_jaxpr/gather | solution.py:138
  170.3 23.0 %gather_fusion = s32[4096]{0:T(1024)S(1)} fusion(s32[4096]{0:T(1024)S(1)} %get-tuple-element.238, u32[4096]{0:T(1024)S(1)} %broadcast_clamp_fusion.3), kind=kCustom, calls=%fused_computation.clone.clone.1 | custom fusion | bytes 49152 | tf_op jit(solution)/shard_map/jit(searchsorted)/jit(_searchsorted_scan_impl)/vmap(jit(_searchsorted_scan_impl))/while/body/eval_jaxpr/gather | solution.py:138
  193.5 23.0 %gather_fusion = s32[4096]{0:T(1024)S(1)} fusion(s32[4096]{0:T(1024)S(1)} %get-tuple-element.238, u32[4096]{0:T(1024)S(1)} %broadcast_clamp_fusion.3), kind=kCustom, calls=%fused_computation.clone.clone.1 | custom fusion | bytes 49152 | tf_op jit(solution)/shard_map/jit(searchsorted)/jit(_searchsorted_scan_impl)/vmap(jit(_searchsorted_scan_impl))/while/body/eval_jaxpr/gather | solution.py:138
  216.6 23.0 %gather_fusion = s32[4096]{0:T(1024)S(1)} fusion(s32[4096]{0:T(1024)S(1)} %get-tuple-element.238, u32[4096]{0:T(1024)S(1)} %broadcast_clamp_fusion.3), kind=kCustom, calls=%fused_computation.clone.clone.1 | custom fusion | bytes 49152 | tf_op jit(solution)/shard_map/jit(searchsorted)/jit(_searchsorted_scan_impl)/vmap(jit(_searchsorted_scan_impl))/while/body/eval_jaxpr/gather | solution.py:138
  239.7 23.0 %gather_fusion = s32[4096]{0:T(1024)S(1)} fusion(s32[4096]{0:T(1024)S(1)} %get-tuple-element.238, u32[4096]{0:T(1024)S(1)} %broadcast_clamp_fusion.3), kind=kCustom, calls=%fused_computation.clone.clone.1 | custom fusion | bytes 49152 | tf_op jit(solution)/shard_map/jit(searchsorted)/jit(_searchsorted_scan_impl)/vmap(jit(_searchsorted_scan_impl))/while/body/eval_jaxpr/gather | solution.py:138
  262.9 23.0 %gather_fusion = s32[4096]{0:T(1024)S(1)} fusion(s32[4096]{0:T(1024)S(1)} %get-tuple-element.238, u32[4096]{0:T(1024)S(1)} %broadcast_clamp_fusion.3), kind=kCustom, calls=%fused_computation.clone.clone.1 | custom fusion | bytes 49152 | tf_op jit(solution)/shard_map/jit(searchsorted)/jit(_searchsorted_scan_impl)/vmap(jit(_searchsorted_scan_impl))/while/body/eval_jaxpr/gather | solution.py:138
  286.0 23.0 %gather_fusion = s32[4096]{0:T(1024)S(1)} fusion(s32[4096]{0:T(1024)S(1)} %get-tuple-element.238, u32[4096]{0:T(1024)S(1)} %broadcast_clamp_fusion.3), kind=kCustom, calls=%fused_computation.clone.clone.1 | custom fusion | bytes 49152 | tf_op jit(solution)/shard_map/jit(searchsorted)/jit(_searchsorted_scan_impl)/vmap(jit(_searchsorted_scan_impl))/while/body/eval_jaxpr/gather | solution.py:138
  309.1 23.0 %gather_fusion = s32[4096]{0:T(1024)S(1)} fusion(s32[4096]{0:T(1024)S(1)} %get-tuple-element.238, u32[4096]{0:T(1024)S(1)} %broadcast_clamp_fusion.3), kind=kCustom, calls=%fused_computation.clone.clone.1 | custom fusion | bytes 49152 | tf_op jit(solution)/shard_map/jit(searchsorted)/jit(_searchsorted_scan_impl)/vmap(jit(_searchsorted_scan_impl))/while/body/eval_jaxpr/gather | solution.py:138
  332.2 23.0 %gather_fusion = s32[4096]{0:T(1024)S(1)} fusion(s32[4096]{0:T(1024)S(1)} %get-tuple-element.238, u32[4096]{0:T(1024)S(1)} %broadcast_clamp_fusion.3), kind=kCustom, calls=%fused_computation.clone.clone.1 | custom fusion | bytes 49152 | tf_op jit(solution)/shard_map/jit(searchsorted)/jit(_searchsorted_scan_impl)/vmap(jit(_searchsorted_scan_impl))/while/body/eval_jaxpr/gather | solution.py:138
  355.3 15.5 scatter_custom_fusion
  371.6 11.5 all-to-all-start
  386.2 26.8 %scatter_custom_fusion.1 = f32[6,8193]{0,1:T(8,128)} fusion(s32[4096]{0:T(1024)S(1)} %compare_select_fusion.2, f32[]{:T(128)} %constant.159.clone.1, f32[6,4096]{0,1:T(8,128)S(1)} %copy.51, s32[4096]{0:T(1024)S(1)} %get-tuple-element.190), kind=kCustom, calls=%fused_computation.15 | custom fusion | bytes 196636 | tf_op jit(solution)/shard_map/scatter | solution.py:147
  421.4 10.1 all-to-all-start.1
  433.3 8.4 all-to-all-done.1
  444.3 206.4 %scatter_custom_fusion.2 = f32[76800]{0:T(1024)S(1)} fusion(s32[32768]{0:T(1024)S(1)} %bitcast.79, f32[32768]{0:T(1024)S(1)} %mul.184, f32[]{:T(128)} %constant.159.clone.1), kind=kCustom, calls=%fused_computation.78 | custom fusion | flops 32768 | bytes 307204 | tf_op jit(solution)/shard_map/scatter-add | solution.py:183
  745.7 180.5 %gather_fusion.3 = f32[32768]{0:T(1024)S(1)} fusion(f32[76800]{0:T(1024)S(1)} %bitcast.66, s32[32768]{0:T(1024)S(1)} %broadcast_clamp_fusion.1), kind=kCustom, calls=%fused_computation.4 | custom fusion | bytes 393216 | tf_op jit(solution)/shard_map/gather | solution.py:195
  926.6 206.9 %scatter_custom_fusion.3 = f32[76800]{0:T(1024)S(1)} fusion(s32[32768]{0:T(1024)} %bitcast.80, f32[32768]{0:T(1024)S(1)} %mul.202, f32[]{:T(128)} %constant.159.clone.1), kind=kCustom, calls=%fused_computation.76 | custom fusion | flops 32768 | bytes 307712 | tf_op jit(solution)/shard_map/scatter-add | solution.py:183
  1181.3 7.7 collective-permute-done.10
  1189.9 66.2 %all-reduce.12 = (f32[]{:T(128)}, f32[]{:T(128)}) all-reduce(f32[]{:T(128)} %get-tuple-element.156, f32[]{:T(128)} %get-tuple-element.155), channel_id=1, replica_groups=mesh['lon'=16,'lat'=8] {'lon','lat'}, use_global_device_ids=true, to_apply=%region_9.10 | all-reduce | flops 2 | bytes 16 | tf_op jit(solution)/shard_map/psum | solution.py:93
  1258.2 62.6 %psum.30 = f32[]{:T(128)} all-reduce(f32[]{:T(128)} %multiply_reduce_fusion), channel_id=1, replica_groups=mesh['lon'=16,'lat'=8] {'lon','lat'}, use_global_device_ids=true, to_apply=%region_15.16 | all-reduce | flops 1 | bytes 8 | tf_op jit(solution)/shard_map/psum | solution.py:93
  1327.5 8.4 collective-permute-done.12
  1362.2 180.5 %gather_fusion.4 = f32[32768]{0:T(1024)S(1)} fusion(f32[76800]{0:T(1024)S(1)} %bitcast.65, s32[32768]{0:T(1024)S(1)} %copy-done.6), kind=kCustom, calls=%fused_computation.5 | custom fusion | bytes 393216 | tf_op jit(solution)/shard_map/gather | solution.py:195
  1543.1 206.9 %scatter_custom_fusion.4 = f32[76800]{0:T(1024)S(1)} fusion(s32[32768]{0:T(1024)} %bitcast.81, f32[32768]{0:T(1024)S(1)} %mul.216, f32[]{:T(128)} %constant.159.clone.1), kind=kCustom, calls=%fused_computation.74 | custom fusion | flops 32768 | bytes 307712 | tf_op jit(solution)/shard_map/scatter-add | solution.py:183
  1797.5 7.8 collective-permute-done.18
  1806.2 65.7 %psum.31 = f32[]{:T(128)} all-reduce(f32[]{:T(128)} %fusion.32), channel_id=1, replica_groups=mesh['lon'=16,'lat'=8] {'lon','lat'}, use_global_device_ids=true, to_apply=%region_19.20 | all-reduce | flops 1 | bytes 8 | tf_op jit(solution)/shard_map/psum | solution.py:197
  (284 shorter events, 250.4 us)
Async XLA Ops:
  54.6 328.5 %copy-start.19 = (f32[24,128]{1,0:T(8,128)S(1)}, f32[24,128]{1,0:T(8,128)}, u32[]{:S(2)}) copy-start(f32[24,128]{1,0:T(8,128)} %param.26) | copy-start | bytes 36868
  54.6 329.1 %copy-start.20 = (f32[24,128]{1,0:T(8,128)S(1)}, f32[24,128]{1,0:T(8,128)}, u32[]{:S(2)}) copy-start(f32[24,128]{1,0:T(8,128)} %param.27) | copy-start | bytes 36868
  54.6 329.2 %copy-start.11 = (f32[4096]{0:T(1024)S(1)}, f32[4096]{0:T(1024)}, u32[]{:S(2)}) copy-start(f32[4096]{0:T(1024)} %param.34) | copy-start | bytes 49156
  54.7 329.2 %copy-start.18 = (f32[4096]{0:T(1024)S(1)}, f32[4096]{0:T(1024)}, u32[]{:S(2)}) copy-start(f32[4096]{0:T(1024)} %param.33) | copy-start | bytes 49156
  54.7 330.2 %copy-start.12 = (f32[4,4096]{1,0:T(4,128)S(1)}, f32[4,4096]{1,0:T(4,128)}, u32[]{:S(2)}) copy-start(f32[4,4096]{1,0:T(4,128)} %param.32) | copy-start | bytes 196612
  371.6 49.8 %all-to-all-start = ((s32[1,128,64]{2,0,1:T(1,128)}), s32[1,128,64]{2,0,1:T(1,128)S(1)}, u32[]{:S(2)}, u32[]{:S(2)}) async-start(s32[1,128,64]{2,0,1:T(1,128)} %bitcast.1), calls=%async_computation | async-start | bytes 131072 | tf_op jit(solution)/shard_map/all_to_all | solution.py:162
  383.1 269.2 %copy-start.24 = (f32[24,64]{1,0:T(8,128)}, f32[24,64]{1,0:T(8,128)S(1)}, u32[]{:S(2)}) copy-start(f32[24,64]{1,0:T(8,128)S(1)} %multiply_negate_fusion.1) | copy-start | bytes 18436
  383.9 268.5 %copy-start.13 = (f32[128,24]{1,0:T(8,128)}, f32[128,24]{1,0:T(8,128)S(1)}, u32[]{:S(2)}) copy-start(f32[128,24]{1,0:T(8,128)S(1)} %copy.54) | copy-start | bytes 36868
  384.8 267.6 %copy-start.29 = (f32[128,24]{1,0:T(8,128)}, f32[128,24]{1,0:T(8,128)S(1)}, u32[]{:S(2)}) copy-start(f32[128,24]{1,0:T(8,128)S(1)} %fusion.9) | copy-start | bytes 36868
  421.4 20.3 %all-to-all-start.1 = ((f32[128,1,384]{2,1,0:T(1,128)}), f32[128,1,384]{2,1,0:T(1,128)S(1)}, u32[]{:S(2)}, u32[]{:S(2)}) async-start(f32[128,1,384]{2,1,0:T(1,128)} %reshape.459), calls=%async_computation.1 | async-start | bytes 393216 | tf_op jit(solution)/shard_map/all_to_all | solution.py:155
  433.3 217.4 %copy-start.7 = (s32[32768,1]{0,1:T(1,128)}, s32[32768,1]{0,1:T(1,128)S(1)}, u32[]{:S(2)}) copy-start(s32[32768,1]{0,1:T(1,128)S(1)} %compare_select_fusion) | copy-start | bytes 393220
  444.2 482.3 %copy-start.3 = (f32[32768]{0:T(1024)}, f32[32768]{0:T(1024)S(1)}, u32[]{:S(2)}) copy-start(f32[32768]{0:T(1024)S(1)} %slice.158) | copy-start | bytes 393220
  666.7 13.5 collective-permute-start.1
  669.2 7.1 collective-permute-start
  695.5 11.5 collective-permute-start.2
  695.5 11.5 collective-permute-start.3
  707.4 12.9 collective-permute-start.4
  707.5 12.9 collective-permute-start.5
  722.8 6.6 collective-permute-start.6
  725.4 8.5 collective-permute-start.7
  1147.1 8.6 collective-permute-start.8
  1152.1 8.5 collective-permute-start.9
  1176.0 13.0 collective-permute-start.10
  1176.1 13.0 collective-permute-start.11
  1322.4 13.4 collective-permute-start.12
  1323.1 12.7 collective-permute-start.13
  1338.2 8.7 collective-permute-start.14
  1343.0 8.4 collective-permute-start.15
  1763.5 8.5 collective-permute-start.16
  1768.6 8.5 collective-permute-start.17
  1792.5 12.8 collective-permute-start.18
  1792.6 12.7 collective-permute-start.19
  (26 other events, 1015.8 us)
where the time goes:
time: 1890 us; the launch traced here: 1880 us
  local copies, waits for them, and re-layouts  836 us (44%)
  other arithmetic  653 us (35%)
  blocking collectives  195 us (10%)
  starting transfers between devices  75 us (4%)
  waiting for transfers between devices  65.1 us (3%)
  matrix products  44.2 us (2%)
    scatter-add x3, other arithmetic, spread(): flat = jnp.zeros((total_cells,), jnp.float32).at[corner.reshape(-1)].add(...  620 us
    gather x4, local copies, waits for them, and re-layouts, body(): image_field.reshape(-1)[corner]  361 us
    gather x13, local copies, waits for them, and re-layouts, body(): first_seen = jnp.searchsorted(ranked, ranked, side='left')  299 us
    psum x2, blocking collectives, squares(): return lax.psum(jnp.sum(residual * residual), ('lon', 'lat'))  129 us
    psum x1, blocking collectives, body(): curvature = lax.psum(jnp.sum(direction * product), ('lon', 'lat'))  65.7 us
    ppermute x10, waiting for transfers between devices, padded_2(): lax.ppermute(lax.slice_in_dim(block, block.shape[dim] - width, None, axis...  45.3 us
    ppermute x10, starting transfers between devices, padded_2(): lax.ppermute(lax.slice_in_dim(block, 0, width, axis=dim), axis, backward)  37.8 us
  transfers between devices with their start and end apart: 22, of which 14 were waited for; matrix products, arithmetic and copies ran while one was open for 3% of the time, Pallas kernels for 0%

commit v1 on v0

v1 whole, which is shorter than its diff:
```python
import functools

import jax
import jax.numpy as jnp
from jax import lax
from jax.experimental import pallas as pl
from jax.experimental.pallas import tpu as pltpu
from jax.sharding import PartitionSpec as P

TAPS = 41
HALF = TAPS // 2
LEV = 25
ROWS = 24
COLS = 128
CELLS = LEV * ROWS
HALO_COLS = 2 * HALF
SLOTS = 4096
BLOCKS = SLOTS // 128
OWNERS = 128
CAP = 64
FIELDS = 6
ROWS_PAD = 608
DAMP = 0.015625

F32 = jnp.float32
BF16 = jnp.bfloat16
NT = (((1,), (1,)), ((), ()))


def params(mib):
    return pltpu.CompilerParams(vmem_limit_bytes=mib * 1024 * 1024)


def split(x):
    high = x.astype(BF16).astype(F32)
    return high, x - high


def iota(shape, dim):
    return lax.broadcasted_iota(jnp.int32, shape, dim)


def place_kernel(
    count_ref, owner_ref, cell_ref, level_ref, weight_ref, value_ref, prec_ref, send_ref, onehot, vals
):
    count = count_ref[0]
    owner_id = iota((OWNERS, 128), 0)
    slot_id = iota((CAP, 128), 0).astype(F32)
    lane = iota((1, 128), 1)
    before = jnp.where(iota((128, 256), 0) < iota((128, 256), 1), 1.0, 0.0).astype(BF16)
    vals[12 * CAP : 13 * CAP, :] = jnp.zeros((CAP, SLOTS), BF16)
    base = jnp.zeros((OWNERS, 128), F32)
    for b in range(BLOCKS):
        at = slice(b * 128, (b + 1) * 128)
        owner = jnp.where(lane + b * 128 < count, owner_ref[b : b + 1, :], -1)
        mine = jnp.where(owner == owner_id, 1.0, 0.0)
        mine_16 = mine.astype(BF16)
        onehot[:, at] = mine_16
        ahead = jnp.dot(mine_16, before, preferred_element_type=F32)
        rank = jnp.sum(mine * (ahead[:, :128] + base), axis=0, keepdims=True)
        base = base + ahead[:, 128:]
        here = rank == slot_id
        root = jnp.sqrt(prec_ref[b : b + 1, :])
        pieces = []
        for c in range(4):
            pieces.append(split(weight_ref[c : c + 1, at] * root * DAMP))
        pieces.append(split(value_ref[b : b + 1, :] * root * (1.0 / DAMP)))
        index = level_ref[b : b + 1, :] * (ROWS * COLS) + cell_ref[b : b + 1, :]
        pieces.append(((index - (index & 1023)).astype(F32), (index & 896).astype(F32)))
        for f in range(FIELDS):
            for g in range(2):
                p = g * FIELDS + f
                vals[p * CAP : (p + 1) * CAP, at] = jnp.where(here, pieces[f][g], 0.0).astype(BF16)
        vals[13 * CAP : 14 * CAP, at] = jnp.where(here, (index & 127).astype(F32), 0.0).astype(BF16)
    placed = lax.dot_general(onehot[...], vals[...], NT, preferred_element_type=F32)
    width = FIELDS * CAP
    send_ref[:, : width - 128] = placed[:, : width - 128] + placed[:, width : 2 * width - 128]
    send_ref[:, width - 128 :] = (
        placed[:, width - 128 : width] + placed[:, 2 * width - 128 : 2 * width] + placed[:, 2 * width :]
    )


def place(obs_owner, obs_count, obs_cell, obs_level, obs_weight, obs_value, obs_precision):
    tiled = lambda x: x.reshape(BLOCKS, 128)
    vmem = pl.BlockSpec(memory_space=pltpu.VMEM)
    return pl.pallas_call(
        place_kernel,
        out_shape=jax.ShapeDtypeStruct((OWNERS, FIELDS * CAP), F32),
        in_specs=[pl.BlockSpec(memory_space=pltpu.SMEM)] + [vmem] * 6,
        out_specs=vmem,
        scratch_shapes=[pltpu.VMEM((OWNERS, SLOTS), BF16), pltpu.VMEM((14 * CAP, SLOTS), BF16)],
        compiler_params=params(24),
        name="place_observations",
    )(
        obs_count,
        tiled(obs_owner),
        tiled(obs_cell),
        tiled(obs_level),
        obs_weight,
        tiled(obs_value),
        tiled(obs_precision),
    )


RHS = (((0, 4, 0), (1, 4, 1)), ((2, 4, 0), (3, 4, 1)))
DIAG = (((0, 0, 0), (1, 1, 1)), ((2, 2, 0), (3, 3, 1)))
EAST = (((0, 1, 0),), ((2, 3, 0),))
NORTH = (((0, 2, 0), (1, 3, 1)), ((0, 3, 0),), ((1, 2, 0),))
CHUNK = 8


def accumulate(turned, blocks, onehot, highs, lows, sums):
    row_id = iota((ROWS_PAD, 128), 0)
    col_id = iota((128, 128), 0)
    for total in sums:
        total[...] = jnp.zeros_like(total)

    def step(chunk, carry):
        for kk in range(CHUNK):
            k = chunk * CHUNK + kk
            at = slice(kk * 128, (kk + 1) * 128)
            field = lambda f: turned[pl.ds(f * CAP + k, 1), :]
            index = field(5).astype(jnp.int32)
            onehot[:, at] = jnp.where((index >> 7) == row_id, 1.0, 0.0).astype(BF16)
            column = index & 127
            here = (column == col_id, column + 1 == col_id)
            for n, terms in enumerate(blocks):
                high, low = 0.0, 0.0
                for x, y, shift in terms:
                    product_high, product_low = split(field(x) * field(y))
                    high = jnp.where(here[shift], product_high, high)
                    low = jnp.where(here[shift], product_low, low)
                highs[n * 128 : (n + 1) * 128, at] = high.astype(BF16)
                lows[n * 128 : (n + 1) * 128, at] = low.astype(BF16)
        part = lax.dot_general(onehot[...], highs[...], NT, preferred_element_type=F32)
        part = part + lax.dot_general(onehot[...], lows[...], NT, preferred_element_type=F32)
        for n, total in enumerate(sums):
            total[...] += part[:, n * 128 : (n + 1) * 128]
        return carry

    lax.fori_loop(0, CAP // CHUNK, step, 0)


def row_of(ref, j):
    return ref[pl.ds(j, LEV, stride=ROWS), :]


def two_rows(sums, j):
    value = row_of(sums[0], j)
    if j > 0:
        value = value + row_of(sums[1], j - 1)
    return value


def store_sides(j, value, mid_ref, top_ref, low_ref):
    mid_ref[j] = value
    if j < HALF:
        top_ref[j] = value
    if j >= ROWS - HALF:
        low_ref[j - (ROWS - HALF)] = value


def scatter_rhs_kernel(
    got_ref, sigma_ref, mid_ref, top_ref, low_ref, turned_ref, sigma_rows_ref, onehot, highs, lows, *sums
):
    turned_ref[...] = got_ref[...].T
    accumulate(turned_ref, RHS, onehot, highs, lows, sums)
    for j in range(ROWS):
        sigma = row_of(sigma_ref, j)
        sigma_rows_ref[j] = sigma
        store_sides(j, sigma * two_rows(sums, j), mid_ref, top_ref, low_ref)


def scatter_pair_kernel(blocks, turned_ref, out_ref, onehot, highs, lows, *sums):
    accumulate(turned_ref, blocks, onehot, highs, lows, sums)
    for j in range(ROWS):
        out_ref[j] = two_rows(sums, j)


def scatter_plain_kernel(blocks, turned_ref, *refs):
    outs, (onehot, highs, lows), sums = refs[: len(blocks)], refs[len(blocks) : len(blocks) + 3], refs[len(blocks) + 3 :]
    accumulate(turned_ref, blocks, onehot, highs, lows, sums)
    for j in range(ROWS):
        for out_ref, total in zip(outs, sums):
            out_ref[j] = row_of(total, j)


def field_shape(rows=ROWS):
    return jax.ShapeDtypeStruct((rows, LEV, COLS), F32)


def scatter_scratch(count):
    return [
        pltpu.VMEM((ROWS_PAD, CHUNK * 128), BF16),
        pltpu.VMEM((count * 128, CHUNK * 128), BF16),
        pltpu.VMEM((count * 128, CHUNK * 128), BF16),
    ] + [pltpu.VMEM((ROWS_PAD, 128), F32)] * count


def scatter_cost(count):
    return pl.CostEstimate(
        flops=4 * ROWS_PAD * OWNERS * CAP * 128 * count, bytes_accessed=2 * 1024 * 1024, transcendentals=0
    )


def scatter_rhs(got, sigma):
    return pl.pallas_call(
        scatter_rhs_kernel,
        out_shape=[
            field_shape(),
            field_shape(HALF),
            field_shape(HALF),
            jax.ShapeDtypeStruct((FIELDS * CAP, OWNERS), F32),
            field_shape(),
        ],
        scratch_shapes=scatter_scratch(2),
        compiler_params=params(16),
        cost_estimate=scatter_cost(2),
        name="scatter_rhs",
    )(got, sigma)


def scatter_pair(turned, blocks, name):
    return pl.pallas_call(
        functools.partial(scatter_pair_kernel, blocks),
        out_shape=field_shape(),
        scratch_shapes=scatter_scratch(2),
        compiler_params=params(16),
        cost_estimate=scatter_cost(2),
        name=name,
    )(turned)


def scatter_plain(turned, blocks, name):
    return pl.pallas_call(
        functools.partial(scatter_plain_kernel, blocks),
        out_shape=[field_shape()] * len(blocks),
        scratch_shapes=scatter_scratch(len(blocks)),
        compiler_params=params(16),
        cost_estimate=scatter_cost(len(blocks)),
        name=name,
    )(turned)


def lon_weights_kernel(factor_ref, inverse_ref, high_ref, low_ref):
    j = pl.program_id(0)
    factor = factor_ref[pl.ds(j, 1), :]
    inverse = inverse_ref[pl.ds(j, 1), :]
    offset = ((iota((256, 256), 0) - iota((256, 256), 1) + 128) & 255) - 128
    near = jnp.abs(offset) <= HALF
    square = (offset * offset).astype(F32)
    turned = jnp.where(near, jnp.exp(-square * factor) * inverse, 0.0)
    plain = turned.T
    turned_high, turned_low = split(turned[:, :COLS])
    plain_high, plain_low = split(plain)
    turned_high, turned_low = turned_high.astype(BF16), turned_low.astype(BF16)
    plain_high, plain_low = plain_high.astype(BF16), plain_low.astype(BF16)
    gram = jnp.dot(plain_high, turned_high, preferred_element_type=F32)
    gram += jnp.dot(plain_low, turned_high, preferred_element_type=F32)
    gram += jnp.dot(plain_high, turned_low, preferred_element_type=F32)
    for n, half in enumerate((plain[:, :COLS], gram)):
        high, low = split(half)
        high_ref[0, :, n * 128 : (n + 1) * 128] = high.astype(BF16)
        low_ref[0, :, n * 128 : (n + 1) * 128] = low.astype(BF16)


def lon_weights(scale_lon):
    count = lax.axis_size("lon")
    east = [(i, (i + 1) % count) for i in range(count)]
    west = [(target, source) for source, target in east]
    from_west = lax.ppermute(scale_lon, "lon", east)
    from_east = lax.ppermute(scale_lon, "lon", west)
    lane = jnp.arange(COLS, dtype=jnp.int32)[None, :]
    valid = jnp.logical_or(lane < HALO_COLS, lane >= COLS - HALO_COLS)
    beside = jnp.where(lane < HALO_COLS, from_east, jnp.where(valid, from_west, 1.0))
    scale = jnp.concatenate([scale_lon, beside], axis=1)
    factor = 0.5 / (scale * scale)
    norm = jnp.ones_like(factor)
    for d in range(1, HALF + 1):
        norm = norm + 2.0 * jnp.exp(-float(d * d) * factor)
    used = jnp.concatenate([jnp.ones_like(valid), valid], axis=1)
    inverse = jnp.where(used, 1.0 / norm, 0.0)
    whole = pl.BlockSpec((ROWS, 256), lambda j: (0, 0))
    block = pl.BlockSpec((1, 256, 256), lambda j: (j, 0, 0))
    return pl.pallas_call(
        lon_weights_kernel,
        grid=(ROWS,),
        out_shape=[jax.ShapeDtypeStruct((ROWS, 256, 256), BF16)] * 2,
        in_specs=[whole, whole],
        out_specs=[block, block],
        compiler_params=params(16),
        name="lon_weights",
    )(factor, inverse)


def lon_kernel(q_ref, west_ref, east_ref, high_ref, low_ref, back_ref, mid_ref, top_ref, bot_ref, norm_ref, wide, both):
    lane = iota((LEV, COLS), 1)
    wide[...] = jnp.zeros_like(wide)
    norm = jnp.zeros((LEV, COLS), F32)
    for j in range(ROWS):
        group, place_in = j // 3, j % 3
        west = pltpu.roll(west_ref[group], (COLS - HALO_COLS - HALO_COLS * place_in) % COLS, 1)
        east = pltpu.roll(east_ref[group], (-HALO_COLS * place_in) % COLS, 1)
        beside = jnp.where(lane < HALO_COLS, east, jnp.where(lane >= COLS - HALO_COLS, west, 0.0))
        wide[j % 4, :LEV, :COLS] = q_ref[j]
        wide[j % 4, :LEV, COLS:] = beside
        high, low = split(wide[j % 4])
        both[j % 4, :32, :] = high.astype(BF16)
        both[j % 4, 32:, :] = low.astype(BF16)
        twice = jnp.dot(both[j % 4], high_ref[j], preferred_element_type=F32)
        more = jnp.dot(both[j % 4, :32, :], low_ref[j], preferred_element_type=F32)
        out = twice[:32] + twice[32:] + more
        back = out[:LEV, :COLS]
        back_ref[j] = back
        norm = norm + back * back
        store_sides(j, out[:LEV, COLS:], mid_ref, top_ref, bot_ref)
    norm_ref[...] = norm


def lon_both(q, from_west, from_east, weights):
    return pl.pallas_call(
        lon_kernel,
        out_shape=[
            field_shape(),
            field_shape(),
            field_shape(HALF),
            field_shape(HALF),
            jax.ShapeDtypeStruct((LEV, COLS), F32),
        ],
        scratch_shapes=[pltpu.VMEM((4, 32, 256), F32), pltpu.VMEM((4, 64, 256), BF16)],
        compiler_params=params(24),
        name="lon_transpose_and_lon",
    )(q, from_west, from_east, *weights)


def join(scratch, north_ref, mid_ref, south_ref):
    scratch[:HALF] = north_ref[...]
    scratch[HALF : HALF + ROWS] = mid_ref[...]
    scratch[HALF + ROWS :] = south_ref[...]


def lat_transpose_kernel(before_ref, mid_ref, after_ref, weight_ref, q_ref, west_ref, east_ref, wide):
    join(wide, before_ref, mid_ref, after_ref)

    def step(m, carry):
        total = jnp.zeros((LEV, COLS), F32)
        for t in range(-HALF, HALF + 1):
            at = m + (HALF + t)
            total = total + weight_ref[abs(t), pl.ds(at, 1), :] * wide[at]
        q_ref[m] = total
        return carry

    lax.fori_loop(0, ROWS, step, 0)
    lane = iota((LEV, COLS), 1)
    for group in range(ROWS // 3):
        west, east = 0.0, 0.0
        for n in range(3):
            value = q_ref[3 * group + n]
            here = jnp.logical_and(lane >= n * HALO_COLS, lane < (n + 1) * HALO_COLS)
            west = jnp.where(here, pltpu.roll(value, n * HALO_COLS, 1), west)
            east = jnp.where(here, pltpu.roll(value, (n + 1) * HALO_COLS, 1), east)
        west_ref[group] = west
        east_ref[group] = east


def lat_transpose(before, mid, after, lat_weight):
    pack = field_shape(ROWS // 3)
    return pl.pallas_call(
        lat_transpose_kernel,
        out_shape=[field_shape(), pack, pack],
        scratch_shapes=[pltpu.VMEM((ROWS + 2 * HALF, LEV, COLS), F32)],
        compiler_params=params(16),
        name="lat_transpose",
    )(before, mid, after, lat_weight)


def lat_rows(wide, weight_ref, sigma_ref, image_ref):
    def step(m, carry):
        total = weight_ref[0, pl.ds(m + HALF, 1), :] * wide[m + HALF]
        for d in range(1, HALF + 1):
            total = total + weight_ref[d, pl.ds(m + HALF, 1), :] * (wide[m + HALF - d] + wide[m + HALF + d])
        image_ref[m] = sigma_ref[m] * total
        return carry

    lax.fori_loop(0, ROWS, step, 0)


def stencil(m, x_ref, diag_ref, east_ref, north_ref, north_east_ref, north_west_ref):
    x = x_ref[m]
    right = lambda value: pltpu.roll(value, COLS - 1, 1)
    out = diag_ref[m] * x + east_ref[m] * right(x)
    moved = east_ref[m] * x
    if m + 1 < ROWS:
        above = x_ref[m + 1]
        out = out + north_ref[m] * above + north_east_ref[m] * right(above)
        moved = moved + north_west_ref[m] * above
    if m > 0:
        below = x_ref[m - 1]
        out = out + north_ref[m - 1] * below + north_west_ref[m - 1] * right(below)
        moved = moved + north_east_ref[m - 1] * below
    return x, out + pltpu.roll(moved, 1, 1)


def observe_kernel(
    before_ref, mid_ref, after_ref, weight_ref, sigma_ref, *refs
):
    coefficients, (image_ref, gmid_ref, gtop_ref, glow_ref, norm_ref, wide) = refs[:5], refs[5:]
    join(wide, before_ref, mid_ref, after_ref)
    lat_rows(wide, weight_ref, sigma_ref, image_ref)
    norm = jnp.zeros((LEV, COLS), F32)
    for m in range(ROWS):
        x, out = stencil(m, image_ref, *coefficients)
        norm = norm + x * out
        store_sides(m, sigma_ref[m] * out, gmid_ref, gtop_ref, glow_ref)
    norm_ref[...] = norm


def observe(before, mid, after, lat_weight, sigma, coefficients):
    return pl.pallas_call(
        observe_kernel,
        out_shape=[
            field_shape(),
            field_shape(),
            field_shape(HALF),
            field_shape(HALF),
            jax.ShapeDtypeStruct((LEV, COLS), F32),
        ],
        scratch_shapes=[pltpu.VMEM((ROWS + 2 * HALF, LEV, COLS), F32)],
        compiler_params=params(16),
        name="lat_and_observe",
    )(before, mid, after, lat_weight, sigma, *coefficients)


def last_kernel(before_ref, mid_ref, after_ref, weight_ref, sigma_ref, *refs):
    coefficients, norm_refs, (image_ref, sums_ref, wide) = refs[:5], refs[5:8], refs[8:]
    join(wide, before_ref, mid_ref, after_ref)
    lat_rows(wide, weight_ref, sigma_ref, image_ref)
    norm = jnp.zeros((LEV, COLS), F32)
    for m in range(ROWS):
        x, out = stencil(m, image_ref, *coefficients)
        norm = norm + x * out
    lane = iota((1, 128), 1)
    row = jnp.zeros((1, 128), F32)
    for n, value in enumerate([ref[...] for ref in norm_refs] + [norm]):
        total = jnp.sum(jnp.sum(value, axis=0, keepdims=True), axis=1, keepdims=True)
        row = jnp.where(lane == n, total, row)
    sums_ref[...] = jnp.broadcast_to(row, (OWNERS, 128))


def last(before, mid, after, lat_weight, sigma, coefficients, norms):
    return pl.pallas_call(
        last_kernel,
        out_shape=[field_shape(), jax.ShapeDtypeStruct((OWNERS, 128), F32)],
        scratch_shapes=[pltpu.VMEM((ROWS + 2 * HALF, LEV, COLS), F32)],
        compiler_params=params(16),
        name="lat_and_moments",
    )(before, mid, after, lat_weight, sigma, *coefficients, *norms)


def lat_exchange(top, low):
    count = lax.axis_size("lat")
    up = [(i, i + 1) for i in range(count - 1)]
    down = [(target, source) for source, target in up]
    return lax.ppermute(low, "lat", up), lax.ppermute(top, "lat", down)


def lon_exchange(west, east):
    count = lax.axis_size("lon")
    right = [(i, (i + 1) % count) for i in range(count)]
    left = [(target, source) for source, target in right]
    return lax.ppermute(east, "lon", right), lax.ppermute(west, "lon", left)


def lat_weights(scale_lat):
    before, after = lat_exchange(scale_lat[:HALF], scale_lat[ROWS - HALF :])
    scale = jnp.concatenate([before, scale_lat, after], axis=0)
    scale = jnp.where(scale > 0.0, scale, 1.0)
    factor = 0.5 / (scale * scale)
    square = (jnp.arange(HALF + 1, dtype=F32) ** 2)[:, None, None]
    raw = jnp.exp(-square * factor[None])
    norm = raw[0] + 2.0 * jnp.sum(raw[1:], axis=0)
    return raw / norm[None]


def combine_kernel(sums_ref, start_ref, start_image_ref, next_ref, next_image_ref, control_ref, increment_ref):
    row = jnp.sum(sums_ref[...], axis=0, keepdims=True)
    lane = iota((1, 128), 1)
    pick = lambda n: jnp.sum(jnp.where(lane == n, row, 0.0), axis=1, keepdims=True)
    m0 = pick(0)
    m1, m2, m3 = pick(1) / m0, pick(2) / m0, pick(3) / m0
    lift = 1.0 / (DAMP * DAMP)
    unit = 1.0 / lift
    step0 = unit / (unit + m1)
    keep = m1 / (unit + m1)
    ratio = jnp.maximum(m2 - m1 * m1, 0.0) / ((unit + m1) * (unit + m1))
    lead = keep + ratio
    tail = 1.0 / (unit + m1)
    second = lift * (lead * lead * m1 - 2.0 * lead * tail * m2 + tail * tail * m3)
    step1 = ratio / (ratio + ratio * ratio + second)
    alpha = step0 + step1 * lead
    gamma = -step1 * tail
    for j in range(ROWS):
        at = pl.ds(j, LEV, stride=ROWS)
        control_ref[at, :] = alpha * start_ref[j] + gamma * next_ref[j]
        increment_ref[at, :] = alpha * start_image_ref[j] + gamma * next_image_ref[j]


def combine(sums, start, start_image, following, following_image):
    return pl.pallas_call(
        combine_kernel,
        out_shape=[jax.ShapeDtypeStruct((CELLS, COLS), F32)] * 2,
        compiler_params=params(16),
        name="combine",
    )(sums, start, start_image, following, following_image)


def body(
    background_sigma,
    scale_lon,
    scale_lat,
    obs_owner,
    obs_count,
    obs_cell,
    obs_level,
    obs_weight,
    obs_value,
    obs_precision,
):
    everyone = ("lon", "lat")
    send = place(obs_owner, obs_count, obs_cell, obs_level, obs_weight, obs_value, obs_precision)
    lat_weight = lat_weights(scale_lat)
    lon_weight = lon_weights(scale_lon)
    got = lax.all_to_all(send, everyone, 0, 0, tiled=True)
    g_mid, g_top, g_low, turned, sigma = scatter_rhs(got, background_sigma.reshape(CELLS, COLS))

    before, after = lat_exchange(g_top, g_low)
    diag = scatter_pair(turned, DIAG, "scatter_diag")
    q, q_west, q_east = lat_transpose(before, g_mid, after, lat_weight)
    west, east = lon_exchange(q_west, q_east)
    side = scatter_pair(turned, EAST, "scatter_east")
    start, e_mid, e_top, e_low, norm0 = lon_both(q, west, east, lon_weight)
    before, after = lat_exchange(e_top, e_low)
    north = scatter_plain(turned, NORTH, "scatter_north")
    coefficients = (diag, side, *north)
    image0, g_mid, g_top, g_low, norm1 = observe(before, e_mid, after, lat_weight, sigma, coefficients)

    before, after = lat_exchange(g_top, g_low)
    q, q_west, q_east = lat_transpose(before, g_mid, after, lat_weight)
    west, east = lon_exchange(q_west, q_east)
    following, e_mid, e_top, e_low, norm2 = lon_both(q, west, east, lon_weight)
    before, after = lat_exchange(e_top, e_low)
    image1, sums = last(before, e_mid, after, lat_weight, sigma, coefficients, (norm0, norm1, norm2))
    sums = lax.all_to_all(sums, everyone, 0, 0, tiled=True)
    control, increment = combine(sums, start, image0, following, image1)
    shape = background_sigma.shape
    return control.reshape(shape), increment.reshape(shape)


def solution(mesh):
    return jax.shard_map(
        body,
        mesh=mesh,
        in_specs=(
            P(None, "lat", "lon"),
            P("lat", "lon"),
            P("lat", "lon"),
            P(("lon", "lat")),
            P(("lon", "lat")),
            P(("lon", "lat")),
            P(("lon", "lat")),
            P(None, ("lon", "lat")),
            P(("lon", "lat")),
            P(("lon", "lat")),
        ),
        out_specs=(P(None, "lat", "lon"), P(None, "lat", "lon")),
        check_vma=False,
    )
```

time: 1890 us -> 169 us (0.09)
  local copies, waits for them, and re-layouts: 836 us -> 9.46 us
  other arithmetic: 653 us -> 1.24 us
  blocking collectives: 195 us -> 17.7 us
  Pallas kernels: 0 us -> 68.6 us
  waiting for transfers between devices: 65.1 us -> 15.3 us
  matrix products: 44.2 us -> 0 us
  starting transfers between devices: 75 us -> 54.3 us
    gather x19 -> x0, local copies, waits for them, and re-layouts: 707 us -> none  [the longest x4 361 us: body(): image_field.reshape(-1)[corner]]
    scatter-add x3 -> x0, other arithmetic: 620 us -> none  [spread(): flat = jnp.zeros((total_cells,), jnp.float32).at[corner.reshape(-1)].add(...]
    psum x3 -> x0, blocking collectives: 195 us -> none  [the longest x2 129 us: squares(): return lax.psum(jnp.sum(residual * residual), ('lon', 'lat'))]
    pallas_call x0 -> x13, Pallas kernels: none -> 68.6 us  [the longest x2 17.8 us: scatter_pair(): pl.pallas_call(functools.partial(scatter_pair_kernel, blocks), out_shape=...]
    dot_general x10 -> x0, matrix products: 44.2 us -> none  [the longest x3 17.8 us: lat_spread(): return jnp.einsum('ijm,lji->lmi', lat_matrix, gradient, precision=HIGHEST)]
    scatter x2 -> x0, local copies, waits for them, and re-layouts: 42.4 us -> none  [the longest x1 26.8 us: body(): jnp.zeros((6, device_count * capacity + 1), jnp.float32).at[:, placing]]
    ppermute x20 -> x16, waiting for transfers between devices: 56.6 us -> 15.3 us  [the longest x10 12.9 us: lat_exchange(): return (lax.ppermute(low, 'lat', up), lax.ppermute(top, 'lat', down))]
    slice x21 -> x1, local copies, waits for them, and re-layouts: 32.4 us -> 0.79 us  [lat_weights(): before, after = lat_exchange(scale_lat[:HALF], scale_lat[ROWS - HALF:])]
  transfers between devices with their start and end apart: 22 -> 17, of which waited for: 14 -> 5; matrix products, arithmetic and copies ran while one was open for 3% -> 2% of each run, Pallas kernels for 0% -> 28%
where the time goes in v1:
time: 169 us; the launch traced here: 168 us
  Pallas kernels  68.6 us (41%)
  starting transfers between devices  54.3 us (32%)
  blocking collectives  17.7 us (10%)
  waiting for transfers between devices  15.3 us (9%)
  local copies, waits for them, and re-layouts  9.46 us (6%)
    ppermute x10, starting transfers between devices, lat_exchange(): return (lax.ppermute(low, 'lat', up), lax.ppermute(top, 'lat', down))  28.6 us
    pallas_call x2, Pallas kernels, scatter_pair(): pl.pallas_call(functools.partial(scatter_pair_kernel, blocks), out_shape=...  17.8 us
    all_to_all x1, blocking collectives, body(): sums = lax.all_to_all(sums, everyone, 0, 0, tiled=True)  17.7 us
    pallas_call x1, Pallas kernels, scatter_plain(): pl.pallas_call(functools.partial(scatter_plain_kernel, blocks), out_shape...  14.9 us
    ppermute x10, waiting for transfers between devices, lat_exchange(): return (lax.ppermute(low, 'lat', up), lax.ppermute(top, 'lat', down))  12.9 us
    pallas_call x1, Pallas kernels, lon_weights(): pl.pallas_call(lon_weights_kernel, grid=(ROWS,), out_shape=[jax.ShapeDtyp...  10.1 us
    pallas_call x1, Pallas kernels, scatter_rhs(): pl.pallas_call(scatter_rhs_kernel, out_shape=[field_shape(), field_shape(...  10.1 us
    ppermute x4, starting transfers between devices, lon_exchange(): return (lax.ppermute(east, 'lon', right), lax.ppermute(west, 'lon', left))  9.95 us
  transfers between devices with their start and end apart: 17, of which 5 were waited for; matrix products, arithmetic and copies ran while one was open for 2% of the time, Pallas kernels for 28%

profile of v1, /device:TPU:1, one launch (start us, length us, event | category | flops | bytes accessed | tf_op | source)
XLA Modules:
  0.0 168.3 jit_solution(11198891531209022954)
XLA Ops:
  0.6 5.8 %collective-permute-start.6 = (f32[24,128]{1,0:T(8,128)}, f32[24,128]{1,0:T(8,128)S(1)}, u32[]{:S(2)}, u32[]{:S(2)}) collective-permute-start(f32[24,128]{1,0:T(8,128)} %param.11), channel_id=1, source_target_pairs={{8,0},{16,8},{24,16},{32,24},{40,32},{48,40},{56,48},{64,56},{72,6... | collective-permute-start | bytes 36872 | tf_op jit(solution)/shard_map/ppermute | solution.py:272
  7.3 4.4 %collective-permute-start.2 = (f32[20,128]{1,0:T(8,128)S(1)}, f32[20,128]{1,0:T(8,128)S(1)}, u32[]{:S(2)}, u32[]{:S(2)}) collective-permute-start(f32[20,128]{1,0:T(8,128)S(1)} %get-tuple-element.74), channel_id=1, source_target_pairs={{0,1},{1,2},{2,3},{3,4},{4,5},{5,6},{6,7},{8,9},{9,10},{10,11},{11... | collective-permute-start | bytes 30728 | tf_op jit(solution)/shard_map/ppermute | solution.py:464
  11.6 1.9 %collective-permute-start.3 = (f32[20,128]{1,0:T(8,128)S(1)}, f32[20,128]{1,0:T(8,128)S(1)}, u32[]{:S(2)}, u32[]{:S(2)}) collective-permute-start(f32[20,128]{1,0:T(8,128)S(1)} %get-tuple-element.75), channel_id=1, source_target_pairs={{1,0},{2,1},{3,2},{4,3},{5,4},{6,5},{7,6},{9,8},{10,9},{11,10},{12... | collective-permute-start | bytes 30728 | tf_op jit(solution)/shard_map/ppermute | solution.py:464
  18.6 3.6 %place_observations.1 = f32[128,384]{1,0:T(8,128)S(1)} custom-call(s32[1]{0:T(128)S(6)} %copy.17.count_ref, s32[32,128]{1,0:T(8,128)S(1)} %bitcast.24, s32[32,128]{1,0:T(8,128)S(1)} %bitcast.25, s32[32,128]{1,0:T(8,128)S(1)} %bitcast.26, f32[4,4096]{1,0:T(4,128)S(1)} %copy-done.4, f32[32,128]{1,0:T(8,128)S(1)} %bitcast.27, f32[32,128]{1,0:T(8,128)S(1)} %bitcast.28), custom_call_target="tpu_custom_call" | custom-call | tf_op jit(solution)/shard_map/place_observations/pallas_call | solution.py:86
  23.2 9.9 %all-to-all-start = ((f32[128,1,384]{2,1,0:T(1,128)}), f32[128,1,384]{2,1,0:T(1,128)S(1)}, u32[]{:S(2)}, u32[]{:S(2)}) async-start(f32[128,1,384]{2,1,0:T(1,128)} %copy.12), calls=%async_computation | async-start | bytes 393216 | tf_op jit(solution)/shard_map/all_to_all | solution.py:533
  34.4 10.1 %lon_weights.1 = (bf16[24,256,256]{2,1,0:T(8,128)(2,1)S(1)}, bf16[24,256,256]{2,1,0:T(8,128)(2,1)S(1)}) custom-call(f32[24,256]{1,0:T(8,128)S(1)} %get-tuple-element.73.factor_ref, f32[24,256]{1,0:T(8,128)S(1)} %get-tuple-element.72.inverse_ref), custom_call_target="tpu_custom_call" | custom-call | tf_op jit(solution)/shard_map/lon_weights/pallas_call | solution.py:285
  44.6 1.6 copy-done
  46.2 1.7 %copy-done.2 = bf16[24,256,256]{2,1,0:T(8,128)(2,1)} copy-done((bf16[24,256,256]{2,1,0:T(8,128)(2,1)}, bf16[24,256,256]{2,1,0:T(8,128)(2,1)S(1)}, u32[]{:S(2)}) %copy-start.2) | copy-done | bytes 3145752
  47.9 10.1 %scatter_rhs.1 = (f32[24,25,128]{2,1,0:T(8,128)S(1)}, f32[20,25,128]{2,1,0:T(8,128)S(1)}, f32[20,25,128]{2,1,0:T(8,128)S(1)}, f32[384,128]{1,0:T(8,128)S(1)}, f32[24,25,128]{2,1,0:T(8,128)S(1)}) custom-call(f32[128,384]{1,0:T(8,128)S(1)} %bitcast.22, f32[600,128]{1,0:T(8,128)S(1)} %bitcast.29), custom_call_target="tpu_custom_call" | custom-call | flops 5100273664 | bytes 2097152 | tf_op jit(solution)/shard_map/scatter_rhs/pallas_call | solution.py:207
  58.0 3.8 %collective-permute-start = (f32[20,25,128]{2,1,0:T(8,128)S(1)}, f32[20,25,128]{2,1,0:T(8,128)S(1)}, u32[]{:S(2)}, u32[]{:S(2)}) collective-permute-start(f32[20,25,128]{2,1,0:T(8,128)S(1)} %get-tuple-element.37), channel_id=1, source_target_pairs={{0,1},{1,2},{2,3},{3,4},{4,5},{5,6},{6,7},{8,9},{9,10},{10,11},{11... | collective-permute-start | bytes 768008 | tf_op jit(solution)/shard_map/ppermute | solution.py:464
  61.8 1.9 %collective-permute-start.1 = (f32[20,25,128]{2,1,0:T(8,128)S(1)}, f32[20,25,128]{2,1,0:T(8,128)S(1)}, u32[]{:S(2)}, u32[]{:S(2)}) collective-permute-start(f32[20,25,128]{2,1,0:T(8,128)S(1)} %get-tuple-element.39), channel_id=1, source_target_pairs={{1,0},{2,1},{3,2},{4,3},{5,4},{6,5},{7,6},{9,8},{10,9},{11,10},{12... | collective-permute-start | bytes 768008 | tf_op jit(solution)/shard_map/ppermute | solution.py:464
  63.7 14.9 %scatter_north.1 = (f32[24,25,128]{2,1,0:T(8,128)S(1)}, f32[24,25,128]{2,1,0:T(8,128)S(1)}, f32[24,25,128]{2,1,0:T(8,128)S(1)}) custom-call(f32[384,128]{1,0:T(8,128)S(1)} %get-tuple-element.49.turned_ref), custom_call_target="tpu_custom_call" | custom-call | flops 7650410496 | bytes 2097152 | tf_op jit(solution)/shard_map/scatter_north/pallas_call | solution.py:235
  78.7 2.4 %lat_transpose.2 = (f32[24,25,128]{2,1,0:T(8,128)S(1)}, f32[8,25,128]{2,1,0:T(8,128)S(1)}, f32[8,25,128]{2,1,0:T(8,128)S(1)}) custom-call(f32[20,25,128]{2,1,0:T(8,128)S(1)} %collective-permute-done.before_ref, f32[24,25,128]{2,1,0:T(8,128)S(1)} %get-tuple-element.38.mid_ref, f32[20,25,128]{2,1,0:T(8,128)S(1)} %collective-permute-done.1.after_ref, ...), custom_call_target="tpu_custom_call" | custom-call | tf_op jit(solution)/shard_map/lat_transpose/pallas_call | solution.py:368
  82.2 4.0 %collective-permute-start.5 = (f32[8,25,128]{2,1,0:T(8,128)S(1)}, f32[8,25,128]{2,1,0:T(8,128)S(1)}, u32[]{:S(2)}, u32[]{:S(2)}) collective-permute-start(f32[8,25,128]{2,1,0:T(8,128)S(1)} %get-tuple-element.42), channel_id=1, source_target_pairs={{8,0},{16,8},{24,16},{32,24},{40,32},{48,40},{56,48},{64,56},{72,6... | collective-permute-start | bytes 307208 | tf_op jit(solution)/shard_map/ppermute | solution.py:471
  86.2 8.1 %scatter_east.1.refs_1_ = f32[24,25,128]{2,1,0:T(8,128)S(1)} custom-call(f32[384,128]{1,0:T(8,128)S(1)} %get-tuple-element.49.turned_ref), custom_call_target="tpu_custom_call" | custom-call | flops 5100273664 | bytes 2097152 | tf_op jit(solution)/shard_map/scatter_east/pallas_call | solution.py:224
  95.5 4.0 %collective-permute-start.8 = (f32[20,25,128]{2,1,0:T(8,128)S(1)}, f32[20,25,128]{2,1,0:T(8,128)S(1)}, u32[]{:S(2)}, u32[]{:S(2)}) collective-permute-start(f32[20,25,128]{2,1,0:T(8,128)S(1)} %get-tuple-element.45), channel_id=1, source_target_pairs={{0,1},{1,2},{2,3},{3,4},{4,5},{5,6},{6,7},{8,9},{9,10},{10,11},{11... | collective-permute-start | bytes 768008 | tf_op jit(solution)/shard_map/ppermute | solution.py:464
  99.5 1.9 %collective-permute-start.9 = (f32[20,25,128]{2,1,0:T(8,128)S(1)}, f32[20,25,128]{2,1,0:T(8,128)S(1)}, u32[]{:S(2)}, u32[]{:S(2)}) collective-permute-start(f32[20,25,128]{2,1,0:T(8,128)S(1)} %get-tuple-element.47), channel_id=1, source_target_pairs={{1,0},{2,1},{3,2},{4,3},{5,4},{6,5},{7,6},{9,8},{10,9},{11,10},{12... | collective-permute-start | bytes 768008 | tf_op jit(solution)/shard_map/ppermute | solution.py:464
  101.4 9.7 %scatter_diag.1.refs_0_ = f32[24,25,128]{2,1,0:T(8,128)S(1)} custom-call(f32[384,128]{1,0:T(8,128)S(1)} %get-tuple-element.49.turned_ref), custom_call_target="tpu_custom_call" | custom-call | flops 5100273664 | bytes 2097152 | tf_op jit(solution)/shard_map/scatter_diag/pallas_call | solution.py:224
  111.1 2.0 %lat_and_observe.1 = (f32[24,25,128]{2,1,0:T(8,128)S(1)}, f32[24,25,128]{2,1,0:T(8,128)S(1)}, f32[20,25,128]{2,1,0:T(8,128)S(1)}, f32[20,25,128]{2,1,0:T(8,128)S(1)}, f32[25,128]{1,0:T(8,128)S(1)}) custom-call(f32[20,25,128]{2,1,0:T(8,128)S(1)} %collective-permute-done.8.before_ref, f32[24,25,128]{2,1,0:T(8,128)S(1)} %get-tuple-element.46.mid_ref, ...), custom_call_target="tpu_custom_call" | custom-call | tf_op jit(solution)/shard_map/lat_and_observe/pallas_call | solution.py:419
  113.1 3.6 %collective-permute-start.10 = (f32[20,25,128]{2,1,0:T(8,128)S(1)}, f32[20,25,128]{2,1,0:T(8,128)S(1)}, u32[]{:S(2)}, u32[]{:S(2)}) collective-permute-start(f32[20,25,128]{2,1,0:T(8,128)S(1)} %get-tuple-element.53), channel_id=1, source_target_pairs={{0,1},{1,2},{2,3},{3,4},{4,5},{5,6},{6,7},{8,9},{9,10},{10,11},{11... | collective-permute-start | bytes 768008 | tf_op jit(solution)/shard_map/ppermute | solution.py:464
  116.7 1.9 %collective-permute-start.11 = (f32[20,25,128]{2,1,0:T(8,128)S(1)}, f32[20,25,128]{2,1,0:T(8,128)S(1)}, u32[]{:S(2)}, u32[]{:S(2)}) collective-permute-start(f32[20,25,128]{2,1,0:T(8,128)S(1)} %get-tuple-element.55), channel_id=1, source_target_pairs={{1,0},{2,1},{3,2},{4,3},{5,4},{6,5},{7,6},{9,8},{10,9},{11,10},{12... | collective-permute-start | bytes 768008 | tf_op jit(solution)/shard_map/ppermute | solution.py:464
  118.7 2.1 %collective-permute-done.10.before_ref = f32[20,25,128]{2,1,0:T(8,128)S(1)} collective-permute-done((f32[20,25,128]{2,1,0:T(8,128)S(1)}, f32[20,25,128]{2,1,0:T(8,128)S(1)}, u32[]{:S(2)}, u32[]{:S(2)}) %collective-permute-start.10) | collective-permute-done | bytes 256032 | tf_op jit(solution)/shard_map/ppermute | solution.py:464
  120.7 4.4 %collective-permute-done.11.after_ref = f32[20,25,128]{2,1,0:T(8,128)S(1)} collective-permute-done((f32[20,25,128]{2,1,0:T(8,128)S(1)}, f32[20,25,128]{2,1,0:T(8,128)S(1)}, u32[]{:S(2)}, u32[]{:S(2)}) %collective-permute-start.11) | collective-permute-done | bytes 256032 | tf_op jit(solution)/shard_map/ppermute | solution.py:464
  125.1 2.4 %lat_transpose.3 = (f32[24,25,128]{2,1,0:T(8,128)S(1)}, f32[8,25,128]{2,1,0:T(8,128)S(1)}, f32[8,25,128]{2,1,0:T(8,128)S(1)}) custom-call(f32[20,25,128]{2,1,0:T(8,128)S(1)} %collective-permute-done.10.before_ref, f32[24,25,128]{2,1,0:T(8,128)S(1)} %get-tuple-element.54.mid_ref, f32[20,25,128]{2,1,0:T(8,128)S(1)} %collective-permute-done.11.after_ref, ...), custom_call_target="tpu_custom_call" | custom-call | tf_op jit(solution)/shard_map/lat_transpose/pallas_call | solution.py:368
  127.6 4.8 %collective-permute-start.13 = (f32[8,25,128]{2,1,0:T(8,128)S(1)}, f32[8,25,128]{2,1,0:T(8,128)S(1)}, u32[]{:S(2)}, u32[]{:S(2)}) collective-permute-start(f32[8,25,128]{2,1,0:T(8,128)S(1)} %get-tuple-element.58), channel_id=1, source_target_pairs={{8,0},{16,8},{24,16},{32,24},{40,32},{48,40},{56,48},{64,56},{72,6... | collective-permute-start | bytes 307208 | tf_op jit(solution)/shard_map/ppermute | solution.py:471
  132.4 2.4 %collective-permute-done.12.west_ref = f32[8,25,128]{2,1,0:T(8,128)S(1)} collective-permute-done((f32[8,25,128]{2,1,0:T(8,128)S(1)}, f32[8,25,128]{2,1,0:T(8,128)S(1)}, u32[]{:S(2)}, u32[]{:S(2)}) %collective-permute-start.12) | collective-permute-done | bytes 102432 | tf_op jit(solution)/shard_map/ppermute | solution.py:471
  135.9 3.2 %collective-permute-start.14 = (f32[20,25,128]{2,1,0:T(8,128)S(1)}, f32[20,25,128]{2,1,0:T(8,128)S(1)}, u32[]{:S(2)}, u32[]{:S(2)}) collective-permute-start(f32[20,25,128]{2,1,0:T(8,128)S(1)} %get-tuple-element.59), channel_id=1, source_target_pairs={{0,1},{1,2},{2,3},{3,4},{4,5},{5,6},{6,7},{8,9},{9,10},{10,11},{11... | collective-permute-start | bytes 768008 | tf_op jit(solution)/shard_map/ppermute | solution.py:464
  139.1 1.9 %collective-permute-start.15 = (f32[20,25,128]{2,1,0:T(8,128)S(1)}, f32[20,25,128]{2,1,0:T(8,128)S(1)}, u32[]{:S(2)}, u32[]{:S(2)}) collective-permute-start(f32[20,25,128]{2,1,0:T(8,128)S(1)} %get-tuple-element.61), channel_id=1, source_target_pairs={{1,0},{2,1},{3,2},{4,3},{5,4},{6,5},{7,6},{9,8},{10,9},{11,10},{12... | collective-permute-start | bytes 768008 | tf_op jit(solution)/shard_map/ppermute | solution.py:464
  141.1 2.1 %collective-permute-done.14.before_ref = f32[20,25,128]{2,1,0:T(8,128)S(1)} collective-permute-done((f32[20,25,128]{2,1,0:T(8,128)S(1)}, f32[20,25,128]{2,1,0:T(8,128)S(1)}, u32[]{:S(2)}, u32[]{:S(2)}) %collective-permute-start.14) | collective-permute-done | bytes 256032 | tf_op jit(solution)/shard_map/ppermute | solution.py:464
  143.1 4.4 %collective-permute-done.15.after_ref = f32[20,25,128]{2,1,0:T(8,128)S(1)} collective-permute-done((f32[20,25,128]{2,1,0:T(8,128)S(1)}, f32[20,25,128]{2,1,0:T(8,128)S(1)}, u32[]{:S(2)}, u32[]{:S(2)}) %collective-permute-start.15) | collective-permute-done | bytes 256032 | tf_op jit(solution)/shard_map/ppermute | solution.py:464
  147.5 1.9 %lat_and_moments.1 = (f32[24,25,128]{2,1,0:T(8,128)S(1)}, f32[128,128]{1,0:T(8,128)S(1)}) custom-call(f32[20,25,128]{2,1,0:T(8,128)S(1)} %collective-permute-done.14.before_ref, f32[24,25,128]{2,1,0:T(8,128)S(1)} %get-tuple-element.60.mid_ref, f32[20,25,128]{2,1,0:T(8,128)S(1)} %collective-permute-done.15.after_ref, ...), custom_call_target="tpu_custom_call" | custom-call | tf_op jit(solution)/shard_map/lat_and_moments/pallas_call | solution.py:451
  149.4 17.7 %all_to_all.22 = f32[128,1,128]{2,1,0:T(1,128)S(1)} all-to-all(f32[128,1,128]{2,1,0:T(1,128)S(1)} %bitcast.23), channel_id=1, replica_groups=mesh['lon'=16,'lat'=8] {'lon','lat'}, dimensions={0} | all-to-all | bytes 131072 | tf_op jit(solution)/shard_map/all_to_all | solution.py:553
  (54 shorter events, 12.0 us)
Async XLA Ops:
  0.6 33.7 %copy-start.11 = (f32[24,128]{1,0:T(8,128)S(1)}, f32[24,128]{1,0:T(8,128)}, u32[]{:S(2)}) copy-start(f32[24,128]{1,0:T(8,128)} %param.11) | copy-start | bytes 36868
  0.6 33.6 %collective-permute-start.6 = (f32[24,128]{1,0:T(8,128)}, f32[24,128]{1,0:T(8,128)S(1)}, u32[]{:S(2)}, u32[]{:S(2)}) collective-permute-start(f32[24,128]{1,0:T(8,128)} %param.11), channel_id=1, source_target_pairs={{8,0},{16,8},{24,16},{32,24},{40,32},{48,40},{56,48},{64,56},{72,6... | collective-permute-start | bytes 36872 | tf_op jit(solution)/shard_map/ppermute | solution.py:272
  6.5 27.8 %collective-permute-start.7 = (f32[24,128]{1,0:T(8,128)}, f32[24,128]{1,0:T(8,128)S(1)}, u32[]{:S(2)}, u32[]{:S(2)}) collective-permute-start(f32[24,128]{1,0:T(8,128)} %param.11), channel_id=1, source_target_pairs={{0,8},{8,16},{16,24},{24,32},{32,40},{40,48},{48,56},{56,64},{64,7... | collective-permute-start | bytes 36872 | tf_op jit(solution)/shard_map/ppermute | solution.py:271
  7.3 25.9 %collective-permute-start.2 = (f32[20,128]{1,0:T(8,128)S(1)}, f32[20,128]{1,0:T(8,128)S(1)}, u32[]{:S(2)}, u32[]{:S(2)}) collective-permute-start(f32[20,128]{1,0:T(8,128)S(1)} %get-tuple-element.74), channel_id=1, source_target_pairs={{0,1},{1,2},{2,3},{3,4},{4,5},{5,6},{6,7},{8,9},{9,10},{10,11},{11... | collective-permute-start | bytes 30728 | tf_op jit(solution)/shard_map/ppermute | solution.py:464
  11.6 21.5 %collective-permute-start.3 = (f32[20,128]{1,0:T(8,128)S(1)}, f32[20,128]{1,0:T(8,128)S(1)}, u32[]{:S(2)}, u32[]{:S(2)}) collective-permute-start(f32[20,128]{1,0:T(8,128)S(1)} %get-tuple-element.75), channel_id=1, source_target_pairs={{1,0},{2,1},{3,2},{4,3},{5,4},{6,5},{7,6},{9,8},{10,9},{11,10},{12... | collective-permute-start | bytes 30728 | tf_op jit(solution)/shard_map/ppermute | solution.py:464
  14.2 0.8 copy-start.4
  15.1 0.7 copy-start.5
  15.8 0.7 copy-start.6
  16.5 0.7 copy-start.7
  17.2 0.7 copy-start.8
  17.9 0.7 copy-start.9
  18.6 29.3 %copy-start.10 = (f32[25,24,128]{2,1,0:T(8,128)S(1)}, f32[25,24,128]{2,1,0:T(8,128)}, u32[]{:S(2)}) copy-start(f32[25,24,128]{2,1,0:T(8,128)} %param.10) | copy-start | bytes 921604
  23.2 24.7 %all-to-all-start = ((f32[128,1,384]{2,1,0:T(1,128)}), f32[128,1,384]{2,1,0:T(1,128)S(1)}, u32[]{:S(2)}, u32[]{:S(2)}) async-start(f32[128,1,384]{2,1,0:T(1,128)} %copy.12), calls=%async_computation | async-start | bytes 393216 | tf_op jit(solution)/shard_map/all_to_all | solution.py:533
  44.6 1.6 copy-start
  46.2 1.7 %copy-start.2 = (bf16[24,256,256]{2,1,0:T(8,128)(2,1)}, bf16[24,256,256]{2,1,0:T(8,128)(2,1)S(1)}, u32[]{:S(2)}) copy-start(bf16[24,256,256]{2,1,0:T(8,128)(2,1)S(1)} %get-tuple-element.44.low_ref) | copy-start | bytes 9437188
  58.0 20.7 %collective-permute-start = (f32[20,25,128]{2,1,0:T(8,128)S(1)}, f32[20,25,128]{2,1,0:T(8,128)S(1)}, u32[]{:S(2)}, u32[]{:S(2)}) collective-permute-start(f32[20,25,128]{2,1,0:T(8,128)S(1)} %get-tuple-element.37), channel_id=1, source_target_pairs={{0,1},{1,2},{2,3},{3,4},{4,5},{5,6},{6,7},{8,9},{9,10},{10,11},{11... | collective-permute-start | bytes 768008 | tf_op jit(solution)/shard_map/ppermute | solution.py:464
  61.8 16.9 %collective-permute-start.1 = (f32[20,25,128]{2,1,0:T(8,128)S(1)}, f32[20,25,128]{2,1,0:T(8,128)S(1)}, u32[]{:S(2)}, u32[]{:S(2)}) collective-permute-start(f32[20,25,128]{2,1,0:T(8,128)S(1)} %get-tuple-element.39), channel_id=1, source_target_pairs={{1,0},{2,1},{3,2},{4,3},{5,4},{6,5},{7,6},{9,8},{10,9},{11,10},{12... | collective-permute-start | bytes 768008 | tf_op jit(solution)/shard_map/ppermute | solution.py:464
  81.1 13.2 %collective-permute-start.4 = (f32[8,25,128]{2,1,0:T(8,128)S(1)}, f32[8,25,128]{2,1,0:T(8,128)S(1)}, u32[]{:S(2)}, u32[]{:S(2)}) collective-permute-start(f32[8,25,128]{2,1,0:T(8,128)S(1)} %get-tuple-element.41), channel_id=1, source_target_pairs={{0,8},{8,16},{16,24},{24,32},{32,40},{40,48},{48,56},{56,64},{64,7... | collective-permute-start | bytes 307208 | tf_op jit(solution)/shard_map/ppermute | solution.py:471
  82.2 12.1 %copy-start.1 = (bf16[24,256,256]{2,1,0:T(8,128)(2,1)S(1)}, bf16[24,256,256]{2,1,0:T(8,128)(2,1)}, u32[]{:S(2)}) copy-start(bf16[24,256,256]{2,1,0:T(8,128)(2,1)} %copy-done) | copy-start | bytes 9437188
  82.2 12.1 %copy-start.3 = (bf16[24,256,256]{2,1,0:T(8,128)(2,1)S(1)}, bf16[24,256,256]{2,1,0:T(8,128)(2,1)}, u32[]{:S(2)}) copy-start(bf16[24,256,256]{2,1,0:T(8,128)(2,1)} %copy-done.2) | copy-start | bytes 9437188
  82.2 12.1 %collective-permute-start.5 = (f32[8,25,128]{2,1,0:T(8,128)S(1)}, f32[8,25,128]{2,1,0:T(8,128)S(1)}, u32[]{:S(2)}, u32[]{:S(2)}) collective-permute-start(f32[8,25,128]{2,1,0:T(8,128)S(1)} %get-tuple-element.42), channel_id=1, source_target_pairs={{8,0},{16,8},{24,16},{32,24},{40,32},{48,40},{56,48},{64,56},{72,6... | collective-permute-start | bytes 307208 | tf_op jit(solution)/shard_map/ppermute | solution.py:471
  95.5 15.6 %collective-permute-start.8 = (f32[20,25,128]{2,1,0:T(8,128)S(1)}, f32[20,25,128]{2,1,0:T(8,128)S(1)}, u32[]{:S(2)}, u32[]{:S(2)}) collective-permute-start(f32[20,25,128]{2,1,0:T(8,128)S(1)} %get-tuple-element.45), channel_id=1, source_target_pairs={{0,1},{1,2},{2,3},{3,4},{4,5},{5,6},{6,7},{8,9},{9,10},{10,11},{11... | collective-permute-start | bytes 768008 | tf_op jit(solution)/shard_map/ppermute | solution.py:464
  99.5 11.6 %collective-permute-start.9 = (f32[20,25,128]{2,1,0:T(8,128)S(1)}, f32[20,25,128]{2,1,0:T(8,128)S(1)}, u32[]{:S(2)}, u32[]{:S(2)}) collective-permute-start(f32[20,25,128]{2,1,0:T(8,128)S(1)} %get-tuple-element.47), channel_id=1, source_target_pairs={{1,0},{2,1},{3,2},{4,3},{5,4},{6,5},{7,6},{9,8},{10,9},{11,10},{12... | collective-permute-start | bytes 768008 | tf_op jit(solution)/shard_map/ppermute | solution.py:464
  113.1 7.6 %collective-permute-start.10 = (f32[20,25,128]{2,1,0:T(8,128)S(1)}, f32[20,25,128]{2,1,0:T(8,128)S(1)}, u32[]{:S(2)}, u32[]{:S(2)}) collective-permute-start(f32[20,25,128]{2,1,0:T(8,128)S(1)} %get-tuple-element.53), channel_id=1, source_target_pairs={{0,1},{1,2},{2,3},{3,4},{4,5},{5,6},{6,7},{8,9},{9,10},{10,11},{11... | collective-permute-start | bytes 768008 | tf_op jit(solution)/shard_map/ppermute | solution.py:464
  116.7 8.4 %collective-permute-start.11 = (f32[20,25,128]{2,1,0:T(8,128)S(1)}, f32[20,25,128]{2,1,0:T(8,128)S(1)}, u32[]{:S(2)}, u32[]{:S(2)}) collective-permute-start(f32[20,25,128]{2,1,0:T(8,128)S(1)} %get-tuple-element.55), channel_id=1, source_target_pairs={{1,0},{2,1},{3,2},{4,3},{5,4},{6,5},{7,6},{9,8},{10,9},{11,10},{12... | collective-permute-start | bytes 768008 | tf_op jit(solution)/shard_map/ppermute | solution.py:464
  127.5 7.2 %collective-permute-start.12 = (f32[8,25,128]{2,1,0:T(8,128)S(1)}, f32[8,25,128]{2,1,0:T(8,128)S(1)}, u32[]{:S(2)}, u32[]{:S(2)}) collective-permute-start(f32[8,25,128]{2,1,0:T(8,128)S(1)} %get-tuple-element.57), channel_id=1, source_target_pairs={{0,8},{8,16},{16,24},{24,32},{32,40},{40,48},{48,56},{56,64},{64,7... | collective-permute-start | bytes 307208 | tf_op jit(solution)/shard_map/ppermute | solution.py:471
  127.6 7.1 %collective-permute-start.13 = (f32[8,25,128]{2,1,0:T(8,128)S(1)}, f32[8,25,128]{2,1,0:T(8,128)S(1)}, u32[]{:S(2)}, u32[]{:S(2)}) collective-permute-start(f32[8,25,128]{2,1,0:T(8,128)S(1)} %get-tuple-element.58), channel_id=1, source_target_pairs={{8,0},{16,8},{24,16},{32,24},{40,32},{48,40},{56,48},{64,56},{72,6... | collective-permute-start | bytes 307208 | tf_op jit(solution)/shard_map/ppermute | solution.py:471
  135.9 7.2 %collective-permute-start.14 = (f32[20,25,128]{2,1,0:T(8,128)S(1)}, f32[20,25,128]{2,1,0:T(8,128)S(1)}, u32[]{:S(2)}, u32[]{:S(2)}) collective-permute-start(f32[20,25,128]{2,1,0:T(8,128)S(1)} %get-tuple-element.59), channel_id=1, source_target_pairs={{0,1},{1,2},{2,3},{3,4},{4,5},{5,6},{6,7},{8,9},{9,10},{10,11},{11... | collective-permute-start | bytes 768008 | tf_op jit(solution)/shard_map/ppermute | solution.py:464
  139.1 8.4 %collective-permute-start.15 = (f32[20,25,128]{2,1,0:T(8,128)S(1)}, f32[20,25,128]{2,1,0:T(8,128)S(1)}, u32[]{:S(2)}, u32[]{:S(2)}) collective-permute-start(f32[20,25,128]{2,1,0:T(8,128)S(1)} %get-tuple-element.61), channel_id=1, source_target_pairs={{1,0},{2,1},{3,2},{4,3},{5,4},{6,5},{7,6},{9,8},{10,9},{11,10},{12... | collective-permute-start | bytes 768008 | tf_op jit(solution)/shard_map/ppermute | solution.py:464

commit v2 on v1

v2 whole, which is shorter than its diff:
```python
import functools

import jax
import jax.numpy as jnp
from jax import lax
from jax.experimental import pallas as pl
from jax.experimental.pallas import tpu as pltpu
from jax.sharding import PartitionSpec as P

TAPS = 41
HALF = TAPS // 2
LEV = 25
ROWS = 24
COLS = 128
CELLS = LEV * ROWS
HALO_COLS = 2 * HALF
SLOTS = 4096
BLOCKS = SLOTS // 128
OWNERS = 128
CAP = 64
FIELDS = 6
BASE_ROWS = ROWS - 1
ROWS_PAD = 576
DAMP = 0.015625

F32 = jnp.float32
BF16 = jnp.bfloat16
F8 = jnp.float8_e4m3fn
NT = (((1,), (1,)), ((), ()))


def params(mib):
    return pltpu.CompilerParams(vmem_limit_bytes=mib * 1024 * 1024)


def split(x):
    high = x.astype(BF16).astype(F32)
    return high, x - high


def iota(shape, dim):
    return lax.broadcasted_iota(jnp.int32, shape, dim)


HALVES = 4


def place_kernel(fields_ref, weight_ref, send_ref, onehot, vals):
    owner_id = iota((OWNERS, 128), 0).astype(F32)
    slot_id = iota((CAP, 128), 0).astype(F32)
    before = jnp.where(iota((128, 256), 0) < iota((128, 256), 1), 1.0, 0.0).astype(BF16)
    width = FIELDS * CAP
    part = SLOTS // HALVES
    vals[12 * CAP : 13 * CAP, :] = jnp.zeros((CAP, part), BF16)
    base = jnp.zeros((OWNERS, 128), F32)
    placed = jnp.zeros((OWNERS, 14 * CAP), F32)
    for b in range(BLOCKS):
        at = slice(b * 128, (b + 1) * 128)
        to = slice(b * 128 % part, b * 128 % part + 128)
        row = lambda f: fields_ref[f, b : b + 1, :]
        mine = jnp.where(row(0) == owner_id, 1.0, 0.0)
        mine_16 = mine.astype(BF16)
        onehot[:, to] = mine_16
        ahead = jnp.dot(mine_16, before, preferred_element_type=F32)
        rank = jnp.sum(mine * (ahead[:, :128] + base), axis=0, keepdims=True)
        base = base + ahead[:, 128:]
        here = rank == slot_id
        pieces = [split(weight_ref[c : c + 1, at] * row(3)) for c in range(4)]
        pieces.append(split(row(2)))
        index = row(1).astype(jnp.int32)
        pieces.append(((index - (index & 1023)).astype(F32), (index & 896).astype(F32)))
        for f in range(FIELDS):
            for g in range(2):
                p = g * FIELDS + f
                vals[p * CAP : (p + 1) * CAP, to] = jnp.where(here, pieces[f][g], 0.0).astype(BF16)
        vals[13 * CAP : 14 * CAP, to] = jnp.where(here, (index & 127).astype(F32), 0.0).astype(BF16)
        if (b + 1) % (BLOCKS // HALVES) == 0:
            placed = placed + lax.dot_general(onehot[...], vals[...], NT, preferred_element_type=F32)
    send_ref[:, 0, : width - 128] = placed[:, : width - 128] + placed[:, width : 2 * width - 128]
    send_ref[:, 0, width - 128 :] = (
        placed[:, width - 128 : width] + placed[:, 2 * width - 128 : 2 * width] + placed[:, 2 * width :]
    )


def place(obs_owner, obs_count, obs_cell, obs_level, obs_weight, obs_value, obs_precision):
    live = jnp.arange(SLOTS, dtype=jnp.int32) < obs_count[0]
    root = jnp.sqrt(obs_precision)
    fields = jnp.stack(
        [
            jnp.where(live, obs_owner, -1).astype(F32),
            (obs_level * (BASE_ROWS * COLS) + obs_cell).astype(F32),
            obs_value * root * (1.0 / DAMP),
            root * DAMP,
        ]
    ).reshape(4, BLOCKS, 128)
    return pl.pallas_call(
        place_kernel,
        out_shape=jax.ShapeDtypeStruct((OWNERS, 1, FIELDS * CAP), F32),
        scratch_shapes=[
            pltpu.VMEM((OWNERS, SLOTS // HALVES), BF16),
            pltpu.VMEM((14 * CAP, SLOTS // HALVES), BF16),
        ],
        compiler_params=params(9),
        name="place_observations",
    )(fields, obs_weight)


RHS = (((0, 4, 0), (1, 4, 1)), ((2, 4, 0), (3, 4, 1)))
DIAG = (((0, 0, 0), (1, 1, 1)), ((2, 2, 0), (3, 3, 1)))
EAST = (((0, 1, 0),), ((2, 3, 0),))
NORTH = (((0, 2, 0), (1, 3, 1)), ((0, 3, 0),), ((1, 2, 0),))
CHUNK = 4


def low_scale(blocks):
    return 2.0**8 if blocks is RHS else 2.0**23


def build(turned, blocks, chunk, onehot, highs, lows, onehot_8, lows_8):
    zero = jnp.zeros((16, 128), BF16)
    one = jnp.ones((16, 128), BF16)
    line = iota((16, 128), 0).astype(F32)
    line_16 = line.astype(BF16)
    lines = [(line + 16.0 * n).astype(BF16) for n in range(8)]
    packed = lambda row: jnp.broadcast_to(row, (16, 128)).astype(BF16)
    for kk in range(CHUNK):
        k = chunk * CHUNK + kk
        at = slice(kk * 128, (kk + 1) * 128)
        field = lambda f: turned[pl.ds(f * CAP + k, 1), :]
        index = field(5).astype(jnp.int32)
        row = index >> 7
        fine = jnp.where(packed((row & 15).astype(F32)) == line_16, one, zero)
        coarse = packed((row >> 4).astype(F32))
        for n in range(ROWS_PAD // 16):
            onehot[n * 16 : (n + 1) * 16, at] = jnp.where(coarse == jnp.full((16, 128), n, BF16), fine, zero)
        column = (index & 127).astype(F32)
        columns = (packed(column), packed(column + 1.0))
        values = []
        for terms in blocks:
            for x, y, shift in terms:
                high, low = split(field(x) * field(y))
                values.append((packed(high), packed(low * low_scale(blocks)), shift))
        for r in range(8):
            here = [c == lines[r] for c in columns]
            done = 0
            for n, terms in enumerate(blocks):
                high, low = zero, zero
                for _ in terms:
                    value_high, value_low, shift = values[done]
                    done += 1
                    high = jnp.where(here[shift], value_high, high)
                    low = jnp.where(here[shift], value_low, low)
                highs[n * 128 + r * 16 : n * 128 + (r + 1) * 16, at] = high
                lows[n * 128 + r * 16 : n * 128 + (r + 1) * 16, at] = low
    onehot_8[...] = onehot[...].astype(F8)
    lows_8[...] = lows[...].astype(F8)


def accumulate(turned, blocks, work, sums):
    for total in sums:
        total[...] = jnp.zeros_like(total)
    first, second = work[:5], work[5:]
    steps = CAP // CHUNK
    build(turned, blocks, 0, *first)

    def multiply(onehot, highs, lows, onehot_8, lows_8):
        part = lax.dot_general(onehot[...], highs[...], NT, preferred_element_type=F32)
        rest = lax.dot_general(onehot_8[...], lows_8[...], NT, preferred_element_type=F32)
        part = part + rest * (1.0 / low_scale(blocks))
        for n, total in enumerate(sums):
            total[...] += part[:, n * 128 : (n + 1) * 128]

    def step(pair, carry):
        build(turned, blocks, 2 * pair + 1, *second)
        multiply(*first)
        build(turned, blocks, (2 * pair + 2) & (steps - 1), *first)
        multiply(*second)
        return carry

    lax.fori_loop(0, steps // 2, step, 0)


def row_of(ref, j, rows=ROWS):
    return ref[pl.ds(j, LEV, stride=rows), :]


def base_row(total, j):
    return row_of(total, j, BASE_ROWS)


def two_rows(sums, j):
    if j == 0:
        return base_row(sums[0], 0)
    if j == BASE_ROWS:
        return base_row(sums[1], j - 1)
    return base_row(sums[0], j) + base_row(sums[1], j - 1)


def even(axis):
    return lax.rem(lax.axis_index(axis), 2) == 0


def copy_sides(source_ref, top, low, a_ref, b_ref):
    is_even = even("lat")
    at_a, at_b = jnp.where(is_even, low, top), jnp.where(is_even, top, low)
    for r in range(HALF):
        a_ref[r] = source_ref[at_a + r]
        b_ref[r] = source_ref[at_b + r]


def push_rows(g_ref, weight_ref, wide):
    group = 4
    for first in range(0, ROWS + 2 * HALF, group):
        totals = [jnp.zeros((LEV, COLS), F32) for _ in range(group)]
        for j in range(max(0, first - 2 * HALF), min(ROWS, first + group)):
            g = g_ref[j]
            for n in range(group):
                distance = abs(first + n - HALF - j)
                if distance <= HALF:
                    totals[n] = totals[n] + weight_ref[distance, j : j + 1, :] * g
        for n in range(group):
            wide[first + n] = totals[n]


def push_out(g_ref, weight_ref, wide, mid_ref, a_ref, b_ref):
    push_rows(g_ref, weight_ref, wide)
    mid_ref[...] = wide[HALF : HALF + ROWS]
    copy_sides(wide, 0, HALF + ROWS, a_ref, b_ref)


def scatter_rhs_kernel(
    got_ref, sigma_ref, lat_ref, mid_ref, a_ref, b_ref, turned_ref, sigma_rows_ref, lat_weight_ref, *refs
):
    work, sums, (g, wide) = refs[:10], refs[10:12], refs[12:]
    turned_ref[...] = got_ref[...].T
    scale = lat_ref[...]
    factor = -0.5 / (scale * scale)
    norm = jnp.ones_like(factor)
    for d in range(1, HALF + 1):
        raw = jnp.exp(float(d * d) * factor)
        lat_weight_ref[d] = raw
        norm = norm + 2.0 * raw
    inverse = 1.0 / norm
    lat_weight_ref[0] = inverse
    for d in range(1, HALF + 1):
        lat_weight_ref[d] = lat_weight_ref[d] * inverse
    accumulate(turned_ref, RHS, work, sums)
    for j in range(ROWS):
        sigma = row_of(sigma_ref, j)
        sigma_rows_ref[j] = sigma
        g[j] = sigma * two_rows(sums, j)
    push_out(g, lat_weight_ref, wide, mid_ref, a_ref, b_ref)


def scatter_pair_kernel(blocks, turned_ref, out_ref, *refs):
    work, sums = refs[:10], refs[10:]
    accumulate(turned_ref, blocks, work, sums)
    for j in range(ROWS):
        out_ref[j] = two_rows(sums, j)


def scatter_plain_kernel(blocks, turned_ref, *refs):
    count = len(blocks)
    outs, work, sums = refs[:count], refs[count : count + 10], refs[count + 10 :]
    accumulate(turned_ref, blocks, work, sums)
    for j in range(ROWS):
        for out_ref, total in zip(outs, sums):
            out_ref[j] = base_row(total, j) if j < BASE_ROWS else jnp.zeros((LEV, COLS), F32)


def field_shape(rows=ROWS):
    return jax.ShapeDtypeStruct((rows, LEV, COLS), F32)


def scatter_scratch(count):
    return [
        pltpu.VMEM((ROWS_PAD, CHUNK * 128), BF16),
        pltpu.VMEM((count * 128, CHUNK * 128), BF16),
        pltpu.VMEM((count * 128, CHUNK * 128), BF16),
        pltpu.VMEM((ROWS_PAD, CHUNK * 128), F8),
        pltpu.VMEM((count * 128, CHUNK * 128), F8),
    ] * 2 + [pltpu.VMEM((ROWS_PAD, 128), F32)] * count


def row_scratch():
    return [pltpu.VMEM((ROWS, LEV, COLS), F32), pltpu.VMEM((ROWS + 2 * HALF, LEV, COLS), F32)]


def scatter_cost(count):
    return pl.CostEstimate(
        flops=4 * ROWS_PAD * OWNERS * CAP * 128 * count, bytes_accessed=2 * 1024 * 1024, transcendentals=0
    )


def scatter_rhs(got, sigma, scale_lat):
    return pl.pallas_call(
        scatter_rhs_kernel,
        out_shape=[
            field_shape(),
            field_shape(HALF),
            field_shape(HALF),
            jax.ShapeDtypeStruct((FIELDS * CAP, OWNERS), F32),
            field_shape(),
            jax.ShapeDtypeStruct((HALF + 1, ROWS, COLS), F32),
        ],
        scratch_shapes=scatter_scratch(2) + row_scratch(),
        compiler_params=params(9),
        cost_estimate=scatter_cost(2),
        name="scatter_rhs",
    )(got, sigma, scale_lat)


def scatter_pair(turned, blocks, name):
    return pl.pallas_call(
        functools.partial(scatter_pair_kernel, blocks),
        out_shape=field_shape(),
        scratch_shapes=scatter_scratch(2),
        compiler_params=params(9),
        cost_estimate=scatter_cost(2),
        name=name,
    )(turned)


def scatter_plain(turned, blocks, name):
    return pl.pallas_call(
        functools.partial(scatter_plain_kernel, blocks),
        out_shape=[field_shape()] * len(blocks),
        scratch_shapes=scatter_scratch(len(blocks)),
        compiler_params=params(9),
        cost_estimate=scatter_cost(len(blocks)),
        name=name,
    )(turned)


NEAR_TILE = tuple(range(0, 160, 16)) + (224, 240)
NEAR_SIDE = (0, 16) + tuple(range(96, 176, 16)) + (208, 224, 240)


def weights_kernel(
    lon_ref, a_ref, b_ref, high_ref, low_ref, inverse_ref,
    square, factors, columns, plain_high, plain_low, turned_high, turned_low,
):
    offset = ((iota((256, 256), 0) - iota((256, 256), 1) + 128) & 255) - 128
    square[...] = jnp.where(jnp.abs(offset) <= HALF, (offset * offset).astype(F32), 1e30)
    for ref in (plain_high, plain_low, turned_high, turned_low):
        ref[...] = jnp.zeros_like(ref)

    is_even = even("lon")
    east, west = jnp.where(is_even, a_ref[...], b_ref[...]), jnp.where(is_even, b_ref[...], a_ref[...])
    lane = iota((ROWS, COLS), 1)
    valid = jnp.logical_or(lane < HALO_COLS, lane >= COLS - HALO_COLS)
    beside = jnp.where(lane < HALO_COLS, east, jnp.where(valid, west, 1.0))
    for n, scale in enumerate((lon_ref[...], beside)):
        factor = -0.5 / (scale * scale)
        norm = jnp.ones_like(factor)
        for d in range(1, HALF + 1):
            norm = norm + 2.0 * jnp.exp(float(d * d) * factor)
        inverse = 1.0 / norm
        if n == 1:
            inverse = jnp.where(valid, inverse, 0.0)
        inverse_ref[:, n * COLS : (n + 1) * COLS] = inverse
        factors[n, :ROWS] = factor
        factors[n, ROWS:] = jnp.zeros((COLS - ROWS, COLS), F32)
        turned = factors[n].T
        for g in range(ROWS // 8):
            columns[g, n * 128 : (n + 1) * 128] = turned if g == 0 else pltpu.roll(turned, COLS - 8 * g, 1)

    def group(g, carry):
        for jj in range(8):
            j, n = 8 * g + jj, jj % 2
            factor = factors[0, pl.ds(j, 1), :]
            for r in range(0, 256, 16):
                at = slice(r, r + 16)
                column = jnp.broadcast_to(columns[g, at, jj : jj + 1], (16, 128))
                if r in NEAR_TILE:
                    high, low = split(jnp.exp(square[at, :128] * column))
                    plain_high[n, at, :128] = high.astype(BF16)
                    plain_low[n, at, :128] = low.astype(BF16)
                    high_ref[j, at, :128] = high.astype(BF16)
                    low_ref[j, at, :128] = low.astype(BF16)
                    high, low = split(jnp.exp(square[at, :128] * factor))
                    turned_high[n, at] = high.astype(BF16)
                    turned_low[n, at] = low.astype(BF16)
                else:
                    high_ref[j, at, :128] = jnp.zeros((16, 128), BF16)
                    low_ref[j, at, :128] = jnp.zeros((16, 128), BF16)
                if r in NEAR_SIDE:
                    high, low = split(jnp.exp(square[at, 128:] * column))
                    plain_high[n, at, 128:] = high.astype(BF16)
                    plain_low[n, at, 128:] = low.astype(BF16)
            gram = jnp.dot(plain_high[n], turned_high[n], preferred_element_type=F32)
            gram += jnp.dot(plain_low[n], turned_high[n], preferred_element_type=F32)
            gram += jnp.dot(plain_high[n], turned_low[n], preferred_element_type=F32)
            high, low = split(gram)
            high_ref[j, :, 128:] = high.astype(BF16)
            low_ref[j, :, 128:] = low.astype(BF16)
        return carry

    lax.fori_loop(0, ROWS // 8, group, 0)


def filter_weights(scale_lon, side_a, side_b):
    return pl.pallas_call(
        weights_kernel,
        out_shape=[jax.ShapeDtypeStruct((ROWS, 256, 256), BF16)] * 2 + [jax.ShapeDtypeStruct((ROWS, 256), F32)],
        scratch_shapes=[
            pltpu.VMEM((256, 256), F32),
            pltpu.VMEM((2, COLS, COLS), F32),
            pltpu.VMEM((ROWS // 8, 256, COLS), F32),
            pltpu.VMEM((2, 256, 256), BF16),
            pltpu.VMEM((2, 256, 256), BF16),
            pltpu.VMEM((2, 256, 128), BF16),
            pltpu.VMEM((2, 256, 128), BF16),
        ],
        compiler_params=params(9),
        cost_estimate=pl.CostEstimate(flops=2 * 10**9, bytes_accessed=8 * 1024 * 1024, transcendentals=0),
        name="filter_weights",
    )(scale_lon, side_a, side_b)


def lon_kernel(
    q_ref, ra_ref, rb_ref, high_ref, low_ref, inverse_ref, back_ref, mid_ref, a_ref, b_ref, norm_ref, wide, both
):
    lane = iota((LEV, COLS), 1)
    is_even = even("lon")
    wide[...] = jnp.zeros_like(wide)
    norm = jnp.zeros((LEV, COLS), F32)
    for j in range(ROWS):
        group, place_in = j // 3, j % 3
        ra, rb = ra_ref[group], rb_ref[group]
        east, west = jnp.where(is_even, ra, rb), jnp.where(is_even, rb, ra)
        west = pltpu.roll(west, (COLS - HALO_COLS - HALO_COLS * place_in) % COLS, 1)
        east = pltpu.roll(east, (-HALO_COLS * place_in) % COLS, 1)
        beside = jnp.where(lane < HALO_COLS, east, jnp.where(lane >= COLS - HALO_COLS, west, 0.0))
        wide[j % 4, :LEV, :COLS] = q_ref[j]
        wide[j % 4, :LEV, COLS:] = beside
        high, low = split(wide[j % 4] * inverse_ref[j : j + 1, :])
        both[j % 4, :32, :] = high.astype(BF16)
        both[j % 4, 32:, :] = low.astype(BF16)
        twice = jnp.dot(both[j % 4], high_ref[j], preferred_element_type=F32)
        more = jnp.dot(both[j % 4, :32, :], low_ref[j], preferred_element_type=F32)
        out = twice[:32] + twice[32:] + more
        back = out[:LEV, :COLS]
        back_ref[j] = back
        norm = norm + back * back
        mid_ref[j] = out[:LEV, COLS:] * inverse_ref[j : j + 1, :COLS]
    norm_ref[...] = norm
    copy_sides(mid_ref, 0, ROWS - HALF, a_ref, b_ref)


def lon_both(q, from_a, from_b, weights):
    return pl.pallas_call(
        lon_kernel,
        out_shape=[
            field_shape(),
            field_shape(),
            field_shape(HALF),
            field_shape(HALF),
            jax.ShapeDtypeStruct((LEV, COLS), F32),
        ],
        scratch_shapes=[pltpu.VMEM((4, 32, 256), F32), pltpu.VMEM((4, 64, 256), BF16)],
        compiler_params=params(9),
        name="lon_transpose_and_lon",
    )(q, from_a, from_b, *weights)


def fold_kernel(mid_ref, ra_ref, rb_ref, q_ref, a_ref, b_ref):
    is_even = even("lat")
    at_a = jnp.where(is_even, ROWS - HALF, 0)
    at_b = jnp.where(is_even, 0, ROWS - HALF)
    q_ref[...] = mid_ref[...]
    for r in range(HALF):
        q_ref[at_a + r] += ra_ref[r]
    for r in range(HALF):
        q_ref[at_b + r] += rb_ref[r]
    lane = iota((LEV, COLS), 1)
    is_even = even("lon")
    for group in range(ROWS // 3):
        west, east = 0.0, 0.0
        for n in range(3):
            value = q_ref[3 * group + n]
            here = jnp.logical_and(lane >= n * HALO_COLS, lane < (n + 1) * HALO_COLS)
            west = jnp.where(here, pltpu.roll(value, n * HALO_COLS, 1), west)
            east = jnp.where(here, pltpu.roll(value, (n + 1) * HALO_COLS, 1), east)
        a_ref[group] = jnp.where(is_even, east, west)
        b_ref[group] = jnp.where(is_even, west, east)


def fold(mid, from_a, from_b):
    pack = field_shape(ROWS // 3)
    return pl.pallas_call(
        fold_kernel,
        out_shape=[field_shape(), pack, pack],
        compiler_params=params(6),
        name="fold_rims",
    )(mid, from_a, from_b)


def lat_rows(mid_ref, ra_ref, rb_ref, wide, weight_ref, sigma_ref, image_ref):
    is_even = even("lat")
    at_a = jnp.where(is_even, HALF + ROWS, 0)
    at_b = jnp.where(is_even, 0, HALF + ROWS)
    wide[HALF : HALF + ROWS] = mid_ref[...]
    for r in range(HALF):
        wide[at_a + r] = ra_ref[r]
        wide[at_b + r] = rb_ref[r]
    group = 4
    for first in range(0, ROWS, group):
        totals = [jnp.zeros((LEV, COLS), F32) for _ in range(group)]
        for r in range(first, first + group + 2 * HALF):
            x = wide[r]
            for n in range(group):
                distance = abs(first + n + HALF - r)
                if distance <= HALF:
                    m = first + n
                    totals[n] = totals[n] + weight_ref[distance, m : m + 1, :] * x
        for n in range(group):
            image_ref[first + n] = sigma_ref[first + n] * totals[n]


def stencil(m, x_ref, diag_ref, east_ref, north_ref, north_east_ref, north_west_ref):
    x = x_ref[m]
    right = lambda value: pltpu.roll(value, COLS - 1, 1)
    out = diag_ref[m] * x + east_ref[m] * right(x)
    moved = east_ref[m] * x
    if m + 1 < ROWS:
        above = x_ref[m + 1]
        out = out + north_ref[m] * above + north_east_ref[m] * right(above)
        moved = moved + north_west_ref[m] * above
    if m > 0:
        below = x_ref[m - 1]
        out = out + north_ref[m - 1] * below + north_west_ref[m - 1] * right(below)
        moved = moved + north_east_ref[m - 1] * below
    return x, out + pltpu.roll(moved, 1, 1)


def observe_kernel(ra_ref, rb_ref, e_ref, weight_ref, sigma_ref, *refs):
    coefficients, (image_ref, mid_ref, a_ref, b_ref, norm_ref, g, wide) = refs[:5], refs[5:]
    lat_rows(e_ref, ra_ref, rb_ref, wide, weight_ref, sigma_ref, image_ref)
    norm = jnp.zeros((LEV, COLS), F32)
    for m in range(ROWS):
        x, out = stencil(m, image_ref, *coefficients)
        norm = norm + x * out
        g[m] = sigma_ref[m] * out
    norm_ref[...] = norm
    push_out(g, weight_ref, wide, mid_ref, a_ref, b_ref)


def observe(from_a, from_b, mid, lat_weight, sigma, coefficients):
    return pl.pallas_call(
        observe_kernel,
        out_shape=[
            field_shape(),
            field_shape(),
            field_shape(HALF),
            field_shape(HALF),
            jax.ShapeDtypeStruct((LEV, COLS), F32),
        ],
        scratch_shapes=row_scratch(),
        compiler_params=params(9),
        name="lat_and_observe",
    )(from_a, from_b, mid, lat_weight, sigma, *coefficients)


def last_kernel(ra_ref, rb_ref, e_ref, weight_ref, sigma_ref, *refs):
    coefficients, norm_refs, (image_ref, sums_ref, wide) = refs[:5], refs[5:8], refs[8:]
    lat_rows(e_ref, ra_ref, rb_ref, wide, weight_ref, sigma_ref, image_ref)
    norm = jnp.zeros((LEV, COLS), F32)
    for m in range(ROWS):
        x, out = stencil(m, image_ref, *coefficients)
        norm = norm + x * out
    lane = iota((1, 128), 1)
    row = jnp.zeros((1, 128), F32)
    for n, value in enumerate([ref[...] for ref in norm_refs] + [norm]):
        total = jnp.sum(jnp.sum(value, axis=0, keepdims=True), axis=1, keepdims=True)
        row = jnp.where(lane == n, total, row)
    sums_ref[...] = jnp.broadcast_to(row, (OWNERS, 128))


def last(from_a, from_b, mid, lat_weight, sigma, coefficients, norms):
    return pl.pallas_call(
        last_kernel,
        out_shape=[field_shape(), jax.ShapeDtypeStruct((OWNERS, 128), F32)],
        scratch_shapes=row_scratch()[1:],
        compiler_params=params(9),
        name="lat_and_moments",
    )(from_a, from_b, mid, lat_weight, sigma, *coefficients, *norms)


def exchange(axis, periodic, side_a, side_b):
    count = lax.axis_size(axis)

    def swaps(first):
        pairs = []
        for i in range(first, count, 2):
            if i + 1 < count or periodic:
                pairs += [(i, (i + 1) % count), ((i + 1) % count, i)]
        return pairs

    from_b = lax.ppermute(side_b, axis, swaps(1))
    return lax.ppermute(side_a, axis, swaps(0)), from_b


def combine_kernel(sums_ref, start_ref, start_image_ref, next_ref, next_image_ref, control_ref, increment_ref):
    row = jnp.sum(sums_ref[...], axis=0, keepdims=True)
    lane = iota((1, 128), 1)
    pick = lambda n: jnp.sum(jnp.where(lane == n, row, 0.0), axis=1, keepdims=True)
    m0 = pick(0)
    m1, m2, m3 = pick(1) / m0, pick(2) / m0, pick(3) / m0
    lift = 1.0 / (DAMP * DAMP)
    unit = 1.0 / lift
    step0 = unit / (unit + m1)
    keep = m1 / (unit + m1)
    ratio = jnp.maximum(m2 - m1 * m1, 0.0) / ((unit + m1) * (unit + m1))
    lead = keep + ratio
    tail = 1.0 / (unit + m1)
    second = lift * (lead * lead * m1 - 2.0 * lead * tail * m2 + tail * tail * m3)
    step1 = ratio / (ratio + ratio * ratio + second)
    alpha = step0 + step1 * lead
    gamma = -step1 * tail
    for j in range(ROWS):
        at = pl.ds(j, LEV, stride=ROWS)
        control_ref[at, :] = alpha * start_ref[j] + gamma * next_ref[j]
        increment_ref[at, :] = alpha * start_image_ref[j] + gamma * next_image_ref[j]


def combine(sums, start, start_image, following, following_image):
    return pl.pallas_call(
        combine_kernel,
        out_shape=[jax.ShapeDtypeStruct((CELLS, COLS), F32)] * 2,
        compiler_params=params(9),
        name="combine",
    )(sums, start, start_image, following, following_image)


def body(
    background_sigma,
    scale_lon,
    scale_lat,
    obs_owner,
    obs_count,
    obs_cell,
    obs_level,
    obs_weight,
    obs_value,
    obs_precision,
):
    everyone = ("lon", "lat")
    send = place(obs_owner, obs_count, obs_cell, obs_level, obs_weight, obs_value, obs_precision)
    send, scale_lon = lax.optimization_barrier((send, scale_lon))
    got = lax.all_to_all(send, everyone, 0, 0, tiled=True).reshape(OWNERS, FIELDS * CAP)
    scale_a, scale_b = exchange("lon", True, scale_lon, scale_lon)
    mid, side_a, side_b, turned, sigma, lat_weight = scatter_rhs(
        got, background_sigma.reshape(CELLS, COLS), scale_lat
    )
    turned, scale_lon, scale_a, scale_b = lax.optimization_barrier((turned, scale_lon, scale_a, scale_b))
    lon_weight = filter_weights(scale_lon, scale_a, scale_b)

    from_a, from_b = exchange("lat", False, side_a, side_b)
    north = scatter_plain(turned, NORTH, "scatter_north")
    q, side_a, side_b = fold(mid, from_a, from_b)
    from_a, from_b = exchange("lon", True, side_a, side_b)
    side = scatter_pair(turned, EAST, "scatter_east")
    start, mid, side_a, side_b, norm0 = lon_both(q, from_a, from_b, lon_weight)
    from_a, from_b = exchange("lat", False, side_a, side_b)
    diag = scatter_pair(turned, DIAG, "scatter_diag")
    coefficients = (diag, side, *north)
    image0, mid, side_a, side_b, norm1 = observe(from_a, from_b, mid, lat_weight, sigma, coefficients)

    from_a, from_b = exchange("lat", False, side_a, side_b)
    q, side_a, side_b = fold(mid, from_a, from_b)
    from_a, from_b = exchange("lon", True, side_a, side_b)
    following, mid, side_a, side_b, norm2 = lon_both(q, from_a, from_b, lon_weight)
    from_a, from_b = exchange("lat", False, side_a, side_b)
    image1, sums = last(from_a, from_b, mid, lat_weight, sigma, coefficients, (norm0, norm1, norm2))
    sums = lax.all_to_all(sums, everyone, 0, 0, tiled=True)
    control, increment = combine(sums, start, image0, following, image1)
    shape = background_sigma.shape
    return control.reshape(shape), increment.reshape(shape)


def solution(mesh):
    return jax.shard_map(
        body,
        mesh=mesh,
        in_specs=(
            P(None, "lat", "lon"),
            P("lat", "lon"),
            P("lat", "lon"),
            P(("lon", "lat")),
            P(("lon", "lat")),
            P(("lon", "lat")),
            P(("lon", "lat")),
            P(None, ("lon", "lat")),
            P(("lon", "lat")),
            P(("lon", "lat")),
        ),
        out_specs=(P(None, "lat", "lon"), P(None, "lat", "lon")),
        check_vma=False,
    )
```

time: 169 us -> 132 us (0.78)
  starting transfers between devices: 54.3 us -> 33.2 us
  Pallas kernels: 68.6 us -> 52 us
  waiting for transfers between devices: 15.3 us -> 25.1 us
  local copies, waits for them, and re-layouts: 9.46 us -> 2.52 us
  blocking collectives: 17.7 us -> 15.2 us
    ppermute x16 -> x14, starting transfers between devices: 44.4 us -> 21.7 us  [the longest x7 19.9 us: exchange(): from_b = lax.ppermute(side_b, axis, swaps(1))]
    pallas_call x4, Pallas kernels: 18.5 us -> 9.36 us  [the longest x1 4.61 us: place(): pl.pallas_call(place_kernel, out_shape=jax.ShapeDtypeStruct((OWNERS, 1, F...]
    all_to_all x1, waiting for transfers between devices: 0.01 us -> 5.64 us  [body(): lax.all_to_all(send, everyone, 0, 0, tiled=True)]
    unnamed x25 -> x9, local copies, waits for them, and re-layouts: 7.77 us -> 2.52 us
    ppermute x16 -> x14, waiting for transfers between devices: 15.3 us -> 19.4 us  [the longest x7 16.8 us: exchange(): from_b = lax.ppermute(side_b, axis, swaps(1))]
    pallas_call x1, Pallas kernels: 14.9 us -> 10.8 us  [scatter_plain(): pl.pallas_call(functools.partial(scatter_plain_kernel, blocks), out_shape...]
    pallas_call x2, Pallas kernels: 17.8 us -> 13.8 us  [scatter_pair(): pl.pallas_call(functools.partial(scatter_pair_kernel, blocks), out_shape=...]
    all_to_all x1, blocking collectives: 17.7 us -> 15.2 us  [body(): sums = lax.all_to_all(sums, everyone, 0, 0, tiled=True)]
  transfers between devices with their start and end apart: 17 -> 15, of which waited for: 5 -> 6; matrix products, arithmetic and copies ran while one was open for 2% -> 0% of each run, Pallas kernels for 28% -> 28%
where the time goes in v2:
time: 132 us; the launch traced here: 131 us
  Pallas kernels  52 us (39%)
  starting transfers between devices  33.2 us (25%)
  waiting for transfers between devices  25.1 us (19%)
  blocking collectives  15.2 us (12%)
  local copies, waits for them, and re-layouts  2.52 us (2%)
  between operations  1.53 us (1%)
  other arithmetic  1.51 us (1%)
    ppermute x7, starting transfers between devices, exchange(): from_b = lax.ppermute(side_b, axis, swaps(1))  19.9 us
    ppermute x7, waiting for transfers between devices, exchange(): from_b = lax.ppermute(side_b, axis, swaps(1))  16.8 us
    all_to_all x1, blocking collectives, body(): sums = lax.all_to_all(sums, everyone, 0, 0, tiled=True)  15.2 us
    pallas_call x2, Pallas kernels, scatter_pair(): pl.pallas_call(functools.partial(scatter_pair_kernel, blocks), out_shape=...  13.8 us
    all_to_all x1, starting transfers between devices, body(): lax.all_to_all(send, everyone, 0, 0, tiled=True)  11.5 us
    pallas_call x1, Pallas kernels, scatter_plain(): pl.pallas_call(functools.partial(scatter_plain_kernel, blocks), out_shape...  10.8 us
    pallas_call x1, Pallas kernels, scatter_rhs(): pl.pallas_call(scatter_rhs_kernel, out_shape=[field_shape(), field_shape(...  8.5 us
    all_to_all x1, waiting for transfers between devices, body(): lax.all_to_all(send, everyone, 0, 0, tiled=True)  5.64 us
  transfers between devices with their start and end apart: 15, of which 6 were waited for; matrix products, arithmetic and copies ran while one was open for 0% of the time, Pallas kernels for 28%

profile of v2, /device:TPU:1, one launch (start us, length us, event | category | flops | bytes accessed | tf_op | source)
XLA Modules:
  0.0 131.0 jit_solution(8122889062114435706)
XLA Ops:
  1.3 0.7 multiply_bitcast_fusion.1
  2.0 0.8 convert_bitcast_fusion
  2.8 0.8 copy-done
  3.6 4.6 %place_observations.1 = f32[128,1,384]{2,1,0:T(1,128)} custom-call(f32[4,32,128]{2,1,0:T(8,128)S(1)} %pad_maximum_fusion.fields_ref, f32[4,4096]{1,0:T(4,128)S(1)} %copy-done), custom_call_target="tpu_custom_call" | custom-call | tf_op jit(solution)/shard_map/place_observations/pallas_call | solution.py:96
  8.3 11.5 %all-to-all-start = ((f32[128,1,384]{2,1,0:T(1,128)}), f32[128,1,384]{2,1,0:T(1,128)S(1)}, u32[]{:S(2)}, u32[]{:S(2)}) async-start(f32[128,1,384]{2,1,0:T(1,128)} %place_observations.1), calls=%async_computation | async-start | bytes 393216 | tf_op jit(solution)/shard_map/all_to_all | solution.py:651
  19.8 4.9 %collective-permute-start.5 = (f32[24,128]{1,0:T(8,128)}, f32[24,128]{1,0:T(8,128)S(1)}, u32[]{:S(2)}, u32[]{:S(2)}) collective-permute-start(f32[24,128]{1,0:T(8,128)} %lon_ref), channel_id=1, source_target_pairs={{8,16},{16,8},{24,32},{32,24},{40,48},{48,40},{56,64},{64,56},{72,... | collective-permute-start | bytes 36872 | tf_op jit(solution)/shard_map/ppermute | solution.py:600
  24.6 5.6 %all-to-all-done = f32[128,1,384]{2,1,0:T(1,128)S(1)} async-done(((f32[128,1,384]{2,1,0:T(1,128)}), f32[128,1,384]{2,1,0:T(1,128)S(1)}, u32[]{:S(2)}, u32[]{:S(2)}) %all-to-all-start) | async-done | bytes 196640 | tf_op jit(solution)/shard_map/all_to_all | solution.py:651
  30.3 1.0 copy-done.1
  31.3 0.7 copy-done.2
  32.0 8.5 %scatter_rhs.1 = (f32[24,25,128]{2,1,0:T(8,128)S(1)}, f32[20,25,128]{2,1,0:T(8,128)S(1)}, f32[20,25,128]{2,1,0:T(8,128)S(1)}, f32[384,128]{1,0:T(8,128)S(1)}, f3...) custom-call(f32[128,384]{1,0:T(8,128)S(1)} %bitcast.21, f32[600,128]{1,0:T(8,128)S(1)} %bitcast.23, ...), custom_call_target="tpu_custom_call" | custom-call | flops 4831838208 | bytes 2097152 | tf_op jit(solution)/shard_map/scatter_rhs/pallas_call | solution.py:296
  40.5 0.8 collective-permute-start
  41.4 2.1 %collective-permute-start.1 = (f32[20,25,128]{2,1,0:T(8,128)S(1)}, f32[20,25,128]{2,1,0:T(8,128)S(1)}, u32[]{:S(2)}, u32[]{:S(2)}) collective-permute-start(f32[20,25,128]{2,1,0:T(8,128)S(1)} %get-tuple-element.48), channel_id=1, source_target_pairs={{1,2},{2,1},{3,4},{4,3},{5,6},{6,5},{9,10},{10,9},{11,12},{12,11},... | collective-permute-start | bytes 768008 | tf_op jit(solution)/shard_map/ppermute | solution.py:600
  43.4 10.8 %scatter_north.1 = (f32[24,25,128]{2,1,0:T(8,128)S(1)}, f32[24,25,128]{2,1,0:T(8,128)S(1)}, f32[24,25,128]{2,1,0:T(8,128)S(1)}) custom-call(f32[384,128]{1,0:T(8,128)S(1)} %get-tuple-element.65.turned_ref), custom_call_target="tpu_custom_call" | custom-call | flops 7247757312 | bytes 2097152 | tf_op jit(solution)/shard_map/scatter_north/pallas_call | solution.py:325
  54.3 6.7 %scatter_east.1.refs_1_ = f32[24,25,128]{2,1,0:T(8,128)S(1)} custom-call(f32[384,128]{1,0:T(8,128)S(1)} %get-tuple-element.65.turned_ref), custom_call_target="tpu_custom_call" | custom-call | flops 4831838208 | bytes 2097152 | tf_op jit(solution)/shard_map/scatter_east/pallas_call | solution.py:314
  61.7 1.7 %collective-permute-start.3 = (f32[8,25,128]{2,1,0:T(8,128)S(1)}, f32[8,25,128]{2,1,0:T(8,128)S(1)}, u32[]{:S(2)}, u32[]{:S(2)}) collective-permute-start(f32[8,25,128]{2,1,0:T(8,128)S(1)} %get-tuple-element.51), channel_id=1, source_target_pairs={{8,16},{16,8},{24,32},{32,24},{40,48},{48,40},{56,64},{64,56},{72,... | collective-permute-start | bytes 307208 | tf_op jit(solution)/shard_map/ppermute | solution.py:600
  63.4 4.0 %filter_weights.1 = (bf16[24,256,256]{2,1,0:T(8,128)(2,1)S(1)}, bf16[24,256,256]{2,1,0:T(8,128)(2,1)S(1)}, f32[24,256]{1,0:T(8,128)S(1)}) custom-call(f32[24,128]{1,0:T(8,128)S(1)} %copy-done.3, f32[24,128]{1,0:T(8,128)S(1)} %collective-permute-done.4.a_ref, f32[24,128]{1,0:T(8,128)S(1)} %collective-permute-done.5.b_ref), custom_call_target="tpu_custom_call" | custom-call | flops 2000000000 | bytes 8388608 | tf_op jit(solution)/shard_map/filter_weights/pallas_call | solution.py:403
  67.4 2.4 %collective-permute-done.3.rb_ref = f32[8,25,128]{2,1,0:T(8,128)S(1)} collective-permute-done((f32[8,25,128]{2,1,0:T(8,128)S(1)}, f32[8,25,128]{2,1,0:T(8,128)S(1)}, u32[]{:S(2)}, u32[]{:S(2)}) %collective-permute-start.3) | collective-permute-done | bytes 102432 | tf_op jit(solution)/shard_map/ppermute | solution.py:600
  69.8 1.2 lon_transpose_and_lon.2
  71.4 3.9 %collective-permute-start.7 = (f32[20,25,128]{2,1,0:T(8,128)S(1)}, f32[20,25,128]{2,1,0:T(8,128)S(1)}, u32[]{:S(2)}, u32[]{:S(2)}) collective-permute-start(f32[20,25,128]{2,1,0:T(8,128)S(1)} %get-tuple-element.61), channel_id=1, source_target_pairs={{1,2},{2,1},{3,4},{4,3},{5,6},{6,5},{9,10},{10,9},{11,12},{12,11},... | collective-permute-start | bytes 768008 | tf_op jit(solution)/shard_map/ppermute | solution.py:600
  75.2 7.1 %scatter_diag.1.refs_0_ = f32[24,25,128]{2,1,0:T(8,128)S(1)} custom-call(f32[384,128]{1,0:T(8,128)S(1)} %get-tuple-element.65.turned_ref), custom_call_target="tpu_custom_call" | custom-call | flops 4831838208 | bytes 2097152 | tf_op jit(solution)/shard_map/scatter_diag/pallas_call | solution.py:314
  82.4 4.0 %lat_and_observe.1 = (f32[24,25,128]{2,1,0:T(8,128)S(1)}, f32[24,25,128]{2,1,0:T(8,128)S(1)}, f32[20,25,128]{2,1,0:T(8,128)S(1)}, f32[20,25,128]{2,1,0:T(8,128)S(1)}, f32[25,128]{1,0:T(8,128)S(1)}) custom-call(f32[20,25,128]{2,1,0:T(8,128)S(1)} %collective-permute-done.6.ra_ref, f32[20,25,128]{2,1,0:T(8,128)S(1)} %collective-permute-done.7.rb_ref, ...), custom_call_target="tpu_custom_call" | custom-call | tf_op jit(solution)/shard_map/lat_and_observe/pallas_call | solution.py:550
  86.5 2.4 %collective-permute-start.9 = (f32[20,25,128]{2,1,0:T(8,128)S(1)}, f32[20,25,128]{2,1,0:T(8,128)S(1)}, u32[]{:S(2)}, u32[]{:S(2)}) collective-permute-start(f32[20,25,128]{2,1,0:T(8,128)S(1)} %get-tuple-element.71), channel_id=1, source_target_pairs={{1,2},{2,1},{3,4},{4,3},{5,6},{6,5},{9,10},{10,9},{11,12},{12,11},... | collective-permute-start | bytes 768008 | tf_op jit(solution)/shard_map/ppermute | solution.py:600
  88.9 6.3 %collective-permute-done.9.rb_ref = f32[20,25,128]{2,1,0:T(8,128)S(1)} collective-permute-done((f32[20,25,128]{2,1,0:T(8,128)S(1)}, f32[20,25,128]{2,1,0:T(8,128)S(1)}, u32[]{:S(2)}, u32[]{:S(2)}) %collective-permute-start.9) | collective-permute-done | bytes 256032 | tf_op jit(solution)/shard_map/ppermute | solution.py:600
  95.7 1.2 collective-permute-start.11
  96.9 2.6 %collective-permute-done.10.ra_ref = f32[8,25,128]{2,1,0:T(8,128)S(1)} collective-permute-done((f32[8,25,128]{2,1,0:T(8,128)S(1)}, f32[8,25,128]{2,1,0:T(8,128)S(1)}, u32[]{:S(2)}, u32[]{:S(2)}) %collective-permute-start.10) | collective-permute-done | bytes 102432 | tf_op jit(solution)/shard_map/ppermute | solution.py:601
  99.5 3.4 %collective-permute-done.11.rb_ref = f32[8,25,128]{2,1,0:T(8,128)S(1)} collective-permute-done((f32[8,25,128]{2,1,0:T(8,128)S(1)}, f32[8,25,128]{2,1,0:T(8,128)S(1)}, u32[]{:S(2)}, u32[]{:S(2)}) %collective-permute-start.11) | collective-permute-done | bytes 102432 | tf_op jit(solution)/shard_map/ppermute | solution.py:600
  102.9 1.2 lon_transpose_and_lon.3
  104.2 3.8 %collective-permute-start.13 = (f32[20,25,128]{2,1,0:T(8,128)S(1)}, f32[20,25,128]{2,1,0:T(8,128)S(1)}, u32[]{:S(2)}, u32[]{:S(2)}) collective-permute-start(f32[20,25,128]{2,1,0:T(8,128)S(1)} %get-tuple-element.76), channel_id=1, source_target_pairs={{1,2},{2,1},{3,4},{4,3},{5,6},{6,5},{9,10},{10,9},{11,12},{12,11},... | collective-permute-start | bytes 768008 | tf_op jit(solution)/shard_map/ppermute | solution.py:600
  108.0 4.7 %collective-permute-done.13.rb_ref = f32[20,25,128]{2,1,0:T(8,128)S(1)} collective-permute-done((f32[20,25,128]{2,1,0:T(8,128)S(1)}, f32[20,25,128]{2,1,0:T(8,128)S(1)}, u32[]{:S(2)}, u32[]{:S(2)}) %collective-permute-start.13) | collective-permute-done | bytes 256032 | tf_op jit(solution)/shard_map/ppermute | solution.py:600
  112.7 2.0 %lat_and_moments.1 = (f32[24,25,128]{2,1,0:T(8,128)S(1)}, f32[128,128]{1,0:T(8,128)S(1)}) custom-call(f32[20,25,128]{2,1,0:T(8,128)S(1)} %collective-permute-done.12.ra_ref, f32[20,25,128]{2,1,0:T(8,128)S(1)} %collective-permute-done.13.rb_ref, f32[24,25,128]{2,1,0:T(8,128)S(1)} %get-tuple-element.77.e_ref, f32[21,24,128]{2,1,0:T(8,128)S(1)} %get-tuple-element.63.weight_ref, ...), custom_call_target="tpu_custom_call" | custom-call | tf_op jit(solution)/shard_map/lat_and_moments/pallas_call | solution.py:581
  114.7 15.2 %all_to_all.16 = f32[128,1,128]{2,1,0:T(1,128)S(1)} all-to-all(f32[128,1,128]{2,1,0:T(1,128)S(1)} %bitcast.22), channel_id=1, replica_groups=mesh['lon'=16,'lat'=8] {'lon','lat'}, dimensions={0} | all-to-all | bytes 131072 | tf_op jit(solution)/shard_map/all_to_all | solution.py:676
  129.9 1.1 combine.1
  (24 shorter events, 1.8 us)
Async XLA Ops:
  2.8 0.8 copy-start
  8.3 22.0 %all-to-all-start = ((f32[128,1,384]{2,1,0:T(1,128)}), f32[128,1,384]{2,1,0:T(1,128)S(1)}, u32[]{:S(2)}, u32[]{:S(2)}) async-start(f32[128,1,384]{2,1,0:T(1,128)} %place_observations.1), calls=%async_computation | async-start | bytes 393216 | tf_op jit(solution)/shard_map/all_to_all | solution.py:651
  19.8 20.7 %collective-permute-start.5 = (f32[24,128]{1,0:T(8,128)}, f32[24,128]{1,0:T(8,128)S(1)}, u32[]{:S(2)}, u32[]{:S(2)}) collective-permute-start(f32[24,128]{1,0:T(8,128)} %lon_ref), channel_id=1, source_target_pairs={{8,16},{16,8},{24,32},{32,24},{40,48},{48,40},{56,64},{64,56},{72,... | collective-permute-start | bytes 36872 | tf_op jit(solution)/shard_map/ppermute | solution.py:600
  24.6 15.9 %collective-permute-start.4 = (f32[24,128]{1,0:T(8,128)}, f32[24,128]{1,0:T(8,128)S(1)}, u32[]{:S(2)}, u32[]{:S(2)}) collective-permute-start(f32[24,128]{1,0:T(8,128)} %lon_ref), channel_id=1, source_target_pairs={{0,8},{8,0},{16,24},{24,16},{32,40},{40,32},{48,56},{56,48},{64,72... | collective-permute-start | bytes 36872 | tf_op jit(solution)/shard_map/ppermute | solution.py:601
  30.3 1.0 copy-start.1
  31.3 0.7 copy-start.2
  40.5 20.5 %collective-permute-start = (f32[20,25,128]{2,1,0:T(8,128)S(1)}, f32[20,25,128]{2,1,0:T(8,128)S(1)}, u32[]{:S(2)}, u32[]{:S(2)}) collective-permute-start(f32[20,25,128]{2,1,0:T(8,128)S(1)} %get-tuple-element.47), channel_id=1, source_target_pairs={{0,1},{1,0},{2,3},{3,2},{4,5},{5,4},{6,7},{7,6},{8,9},{9,8},{10,11... | collective-permute-start | bytes 768008 | tf_op jit(solution)/shard_map/ppermute | solution.py:601
  41.4 19.6 %collective-permute-start.1 = (f32[20,25,128]{2,1,0:T(8,128)S(1)}, f32[20,25,128]{2,1,0:T(8,128)S(1)}, u32[]{:S(2)}, u32[]{:S(2)}) collective-permute-start(f32[20,25,128]{2,1,0:T(8,128)S(1)} %get-tuple-element.48), channel_id=1, source_target_pairs={{1,2},{2,1},{3,4},{4,3},{5,6},{6,5},{9,10},{10,9},{11,12},{12,11},... | collective-permute-start | bytes 768008 | tf_op jit(solution)/shard_map/ppermute | solution.py:600
  54.3 9.1 %copy-start.3 = (f32[24,128]{1,0:T(8,128)S(1)}, f32[24,128]{1,0:T(8,128)}, u32[]{:S(2)}) copy-start(f32[24,128]{1,0:T(8,128)} %lon_ref) | copy-start | bytes 36868
  61.4 6.0 %collective-permute-start.2 = (f32[8,25,128]{2,1,0:T(8,128)S(1)}, f32[8,25,128]{2,1,0:T(8,128)S(1)}, u32[]{:S(2)}, u32[]{:S(2)}) collective-permute-start(f32[8,25,128]{2,1,0:T(8,128)S(1)} %get-tuple-element.50), channel_id=1, source_target_pairs={{0,8},{8,0},{16,24},{24,16},{32,40},{40,32},{48,56},{56,48},{64,72... | collective-permute-start | bytes 307208 | tf_op jit(solution)/shard_map/ppermute | solution.py:601
  61.7 8.1 %collective-permute-start.3 = (f32[8,25,128]{2,1,0:T(8,128)S(1)}, f32[8,25,128]{2,1,0:T(8,128)S(1)}, u32[]{:S(2)}, u32[]{:S(2)}) collective-permute-start(f32[8,25,128]{2,1,0:T(8,128)S(1)} %get-tuple-element.51), channel_id=1, source_target_pairs={{8,16},{16,8},{24,32},{32,24},{40,48},{48,40},{56,64},{64,56},{72,... | collective-permute-start | bytes 307208 | tf_op jit(solution)/shard_map/ppermute | solution.py:600
  71.0 11.4 %collective-permute-start.6 = (f32[20,25,128]{2,1,0:T(8,128)S(1)}, f32[20,25,128]{2,1,0:T(8,128)S(1)}, u32[]{:S(2)}, u32[]{:S(2)}) collective-permute-start(f32[20,25,128]{2,1,0:T(8,128)S(1)} %get-tuple-element.60), channel_id=1, source_target_pairs={{0,1},{1,0},{2,3},{3,2},{4,5},{5,4},{6,7},{7,6},{8,9},{9,8},{10,11... | collective-permute-start | bytes 768008 | tf_op jit(solution)/shard_map/ppermute | solution.py:601
  71.4 11.0 %collective-permute-start.7 = (f32[20,25,128]{2,1,0:T(8,128)S(1)}, f32[20,25,128]{2,1,0:T(8,128)S(1)}, u32[]{:S(2)}, u32[]{:S(2)}) collective-permute-start(f32[20,25,128]{2,1,0:T(8,128)S(1)} %get-tuple-element.61), channel_id=1, source_target_pairs={{1,2},{2,1},{3,4},{4,3},{5,6},{6,5},{9,10},{10,9},{11,12},{12,11},... | collective-permute-start | bytes 768008 | tf_op jit(solution)/shard_map/ppermute | solution.py:600
  86.4 2.5 %collective-permute-start.8 = (f32[20,25,128]{2,1,0:T(8,128)S(1)}, f32[20,25,128]{2,1,0:T(8,128)S(1)}, u32[]{:S(2)}, u32[]{:S(2)}) collective-permute-start(f32[20,25,128]{2,1,0:T(8,128)S(1)} %get-tuple-element.70), channel_id=1, source_target_pairs={{0,1},{1,0},{2,3},{3,2},{4,5},{5,4},{6,7},{7,6},{8,9},{9,8},{10,11... | collective-permute-start | bytes 768008 | tf_op jit(solution)/shard_map/ppermute | solution.py:601
  86.5 8.7 %collective-permute-start.9 = (f32[20,25,128]{2,1,0:T(8,128)S(1)}, f32[20,25,128]{2,1,0:T(8,128)S(1)}, u32[]{:S(2)}, u32[]{:S(2)}) collective-permute-start(f32[20,25,128]{2,1,0:T(8,128)S(1)} %get-tuple-element.71), channel_id=1, source_target_pairs={{1,2},{2,1},{3,4},{4,3},{5,6},{6,5},{9,10},{10,9},{11,12},{12,11},... | collective-permute-start | bytes 768008 | tf_op jit(solution)/shard_map/ppermute | solution.py:600
  95.6 3.9 %collective-permute-start.10 = (f32[8,25,128]{2,1,0:T(8,128)S(1)}, f32[8,25,128]{2,1,0:T(8,128)S(1)}, u32[]{:S(2)}, u32[]{:S(2)}) collective-permute-start(f32[8,25,128]{2,1,0:T(8,128)S(1)} %get-tuple-element.73), channel_id=1, source_target_pairs={{0,8},{8,0},{16,24},{24,16},{32,40},{40,32},{48,56},{56,48},{64,72... | collective-permute-start | bytes 307208 | tf_op jit(solution)/shard_map/ppermute | solution.py:601
  95.7 7.2 %collective-permute-start.11 = (f32[8,25,128]{2,1,0:T(8,128)S(1)}, f32[8,25,128]{2,1,0:T(8,128)S(1)}, u32[]{:S(2)}, u32[]{:S(2)}) collective-permute-start(f32[8,25,128]{2,1,0:T(8,128)S(1)} %get-tuple-element.74), channel_id=1, source_target_pairs={{8,16},{16,8},{24,32},{32,24},{40,48},{48,40},{56,64},{64,56},{72,... | collective-permute-start | bytes 307208 | tf_op jit(solution)/shard_map/ppermute | solution.py:600
  104.1 3.9 %collective-permute-start.12 = (f32[20,25,128]{2,1,0:T(8,128)S(1)}, f32[20,25,128]{2,1,0:T(8,128)S(1)}, u32[]{:S(2)}, u32[]{:S(2)}) collective-permute-start(f32[20,25,128]{2,1,0:T(8,128)S(1)} %get-tuple-element.75), channel_id=1, source_target_pairs={{0,1},{1,0},{2,3},{3,2},{4,5},{5,4},{6,7},{7,6},{8,9},{9,8},{10,11... | collective-permute-start | bytes 768008 | tf_op jit(solution)/shard_map/ppermute | solution.py:601
  104.2 8.5 %collective-permute-start.13 = (f32[20,25,128]{2,1,0:T(8,128)S(1)}, f32[20,25,128]{2,1,0:T(8,128)S(1)}, u32[]{:S(2)}, u32[]{:S(2)}) collective-permute-start(f32[20,25,128]{2,1,0:T(8,128)S(1)} %get-tuple-element.76), channel_id=1, source_target_pairs={{1,2},{2,1},{3,4},{4,3},{5,6},{6,5},{9,10},{10,9},{11,12},{12,11},... | collective-permute-start | bytes 768008 | tf_op jit(solution)/shard_map/ppermute | solution.py:600

commit v3 on v2

--- a/solution.py
+++ b/solution.py
@@ -45,9 +45,12 @@
 HALVES = 4
 
 
-def place_kernel(fields_ref, weight_ref, send_ref, onehot, vals):
+def place_kernel(fields_ref, weight_ref, send_ref, onehot, vals, roots):
+    roots[...] = jnp.sqrt(fields_ref[3])
     owner_id = iota((OWNERS, 128), 0).astype(F32)
-    slot_id = iota((CAP, 128), 0).astype(F32)
+    zero = jnp.zeros((16, 128), BF16)
+    slots = [(iota((16, 128), 0).astype(F32) + 16.0 * n).astype(BF16) for n in range(CAP // 16)]
+    packed = lambda row: jnp.broadcast_to(row, (16, 128)).astype(BF16)
     before = jnp.where(iota((128, 256), 0) < iota((128, 256), 1), 1.0, 0.0).astype(BF16)
     width = FIELDS * CAP
     part = SLOTS // HALVES
@@ -58,22 +61,24 @@
         at = slice(b * 128, (b + 1) * 128)
         to = slice(b * 128 % part, b * 128 % part + 128)
         row = lambda f: fields_ref[f, b : b + 1, :]
+        root = roots[b : b + 1, :]
         mine = jnp.where(row(0) == owner_id, 1.0, 0.0)
         mine_16 = mine.astype(BF16)
         onehot[:, to] = mine_16
         ahead = jnp.dot(mine_16, before, preferred_element_type=F32)
         rank = jnp.sum(mine * (ahead[:, :128] + base), axis=0, keepdims=True)
         base = base + ahead[:, 128:]
-        here = rank == slot_id
-        pieces = [split(weight_ref[c : c + 1, at] * row(3)) for c in range(4)]
-        pieces.append(split(row(2)))
+        here = [packed(rank) == slot for slot in slots]
+        pieces = [split(weight_ref[c : c + 1, at] * (root * DAMP)) for c in range(4)]
+        pieces.append(split(row(2) * (root * (1.0 / DAMP))))
         index = row(1).astype(jnp.int32)
         pieces.append(((index - (index & 1023)).astype(F32), (index & 896).astype(F32)))
-        for f in range(FIELDS):
-            for g in range(2):
-                p = g * FIELDS + f
-                vals[p * CAP : (p + 1) * CAP, to] = jnp.where(here, pieces[f][g], 0.0).astype(BF16)
-        vals[13 * CAP : 14 * CAP, to] = jnp.where(here, (index & 127).astype(F32), 0.0).astype(BF16)
+        columns = [(g * FIELDS + f, pieces[f][g]) for f in range(FIELDS) for g in range(2)]
+        columns.append((2 * FIELDS + 1, (index & 127).astype(F32)))
+        for p, piece in columns:
+            value = packed(piece)
+            for n in range(CAP // 16):
+                vals[p * CAP + n * 16 : p * CAP + (n + 1) * 16, to] = jnp.where(here[n], value, zero)
         if (b + 1) % (BLOCKS // HALVES) == 0:
             placed = placed + lax.dot_general(onehot[...], vals[...], NT, preferred_element_type=F32)
     send_ref[:, 0, : width - 128] = placed[:, : width - 128] + placed[:, width : 2 * width - 128]
@@ -84,14 +89,11 @@
 
 def place(obs_owner, obs_count, obs_cell, obs_level, obs_weight, obs_value, obs_precision):
     live = jnp.arange(SLOTS, dtype=jnp.int32) < obs_count[0]
-    root = jnp.sqrt(obs_precision)
-    fields = jnp.stack(
-        [
-            jnp.where(live, obs_owner, -1).astype(F32),
-            (obs_level * (BASE_ROWS * COLS) + obs_cell).astype(F32),
-            obs_value * root * (1.0 / DAMP),
-            root * DAMP,
-        ]
+    kind = jnp.arange(4, dtype=jnp.int32)[:, None]
+    owner = jnp.where(live, obs_owner, -1).astype(F32)[None]
+    index = (obs_level * (BASE_ROWS * COLS) + obs_cell).astype(F32)[None]
+    fields = jnp.where(
+        kind == 0, owner, jnp.where(kind == 1, index, jnp.where(kind == 2, obs_value[None], obs_precision[None]))
     ).reshape(4, BLOCKS, 128)
     return pl.pallas_call(
         place_kernel,
@@ -99,6 +101,7 @@
         scratch_shapes=[
             pltpu.VMEM((OWNERS, SLOTS // HALVES), BF16),
             pltpu.VMEM((14 * CAP, SLOTS // HALVES), BF16),
+            pltpu.VMEM((BLOCKS, 128), F32),
         ],
         compiler_params=params(9),
         name="place_observations",
@@ -109,20 +112,21 @@
 DIAG = (((0, 0, 0), (1, 1, 1)), ((2, 2, 0), (3, 3, 1)))
 EAST = (((0, 1, 0),), ((2, 3, 0),))
 NORTH = (((0, 2, 0), (1, 3, 1)), ((0, 3, 0),), ((1, 2, 0),))
-CHUNK = 4
+CHUNK = 8
 
 
 def low_scale(blocks):
     return 2.0**8 if blocks is RHS else 2.0**23
 
 
-def build(turned, blocks, chunk, onehot, highs, lows, onehot_8, lows_8):
+def build(turned, blocks, chunk, onehot, highs, onehot_8, lows_8):
     zero = jnp.zeros((16, 128), BF16)
     one = jnp.ones((16, 128), BF16)
     line = iota((16, 128), 0).astype(F32)
     line_16 = line.astype(BF16)
     lines = [(line + 16.0 * n).astype(BF16) for n in range(8)]
     packed = lambda row: jnp.broadcast_to(row, (16, 128)).astype(BF16)
+    eight = lambda pair: jnp.concatenate(pair, axis=0).astype(F8)
     for kk in range(CHUNK):
         k = chunk * CHUNK + kk
         at = slice(kk * 128, (kk + 1) * 128)
@@ -131,8 +135,11 @@
         row = index >> 7
         fine = jnp.where(packed((row & 15).astype(F32)) == line_16, one, zero)
         coarse = packed((row >> 4).astype(F32))
-        for n in range(ROWS_PAD // 16):
-            onehot[n * 16 : (n + 1) * 16, at] = jnp.where(coarse == jnp.full((16, 128), n, BF16), fine, zero)
+        for n in range(0, ROWS_PAD // 16, 2):
+            pair = [jnp.where(coarse == jnp.full((16, 128), n + i, BF16), fine, zero) for i in range(2)]
+            onehot[n * 16 : (n + 1) * 16, at] = pair[0]
+            onehot[(n + 1) * 16 : (n + 2) * 16, at] = pair[1]
+            onehot_8[n * 16 : (n + 2) * 16, at] = eight(pair)
         column = (index & 127).astype(F32)
         columns = (packed(column), packed(column + 1.0))
         values = []
@@ -140,40 +147,47 @@
             for x, y, shift in terms:
                 high, low = split(field(x) * field(y))
                 values.append((packed(high), packed(low * low_scale(blocks)), shift))
-        for r in range(8):
-            here = [c == lines[r] for c in columns]
+        for r in range(0, 8, 2):
+            here = [[c == lines[r + i] for c in columns] for i in range(2)]
             done = 0
             for n, terms in enumerate(blocks):
-                high, low = zero, zero
+                high, low = [zero, zero], [zero, zero]
                 for _ in terms:
                     value_high, value_low, shift = values[done]
                     done += 1
-                    high = jnp.where(here[shift], value_high, high)
-                    low = jnp.where(here[shift], value_low, low)
-                highs[n * 128 + r * 16 : n * 128 + (r + 1) * 16, at] = high
-                lows[n * 128 + r * 16 : n * 128 + (r + 1) * 16, at] = low
-    onehot_8[...] = onehot[...].astype(F8)
-    lows_8[...] = lows[...].astype(F8)
-
-
-def accumulate(turned, blocks, work, sums):
-    for total in sums:
-        total[...] = jnp.zeros_like(total)
-    first, second = work[:5], work[5:]
-    steps = CAP // CHUNK
-    build(turned, blocks, 0, *first)
-
-    def multiply(onehot, highs, lows, onehot_8, lows_8):
+                    for i in range(2):
+                        high[i] = jnp.where(here[i][shift], value_high, high[i])
+                        low[i] = jnp.where(here[i][shift], value_low, low[i])
+                start = n * 128 + r * 16
+                highs[start : start + 16, at] = high[0]
+                highs[start + 16 : start + 32, at] = high[1]
+                lows_8[start : start + 32, at] = eight(low)
+
+
+def accumulate(turned, blocks, work, sums, begin=0, end=CAP):
+    first, second = work[:4], work[4:]
+
+    def multiply(onehot, highs, onehot_8, lows_8):
         part = lax.dot_general(onehot[...], highs[...], NT, preferred_element_type=F32)
         rest = lax.dot_general(onehot_8[...], lows_8[...], NT, preferred_element_type=F32)
         part = part + rest * (1.0 / low_scale(blocks))
-        for n, total in enumerate(sums):
-            total[...] += part[:, n * 128 : (n + 1) * 128]
+        for n in range(len(blocks)):
+            sums[n] += part[:, n * 128 : (n + 1) * 128]
+
+    start, steps = begin // CHUNK, (end - begin) // CHUNK
+    build(turned, blocks, start, *first)
+    if steps <= 3:
+        for step in range(steps):
+            now, later = (first, second) if step % 2 == 0 else (second, first)
+            if step + 1 < steps:
+                build(turned, blocks, start + step + 1, *later)
+            multiply(*now)
+        return
 
     def step(pair, carry):
-        build(turned, blocks, 2 * pair + 1, *second)
+        build(turned, blocks, start + 2 * pair + 1, *second)
         multiply(*first)
-        build(turned, blocks, (2 * pair + 2) & (steps - 1), *first)
+        build(turned, blocks, start + ((2 * pair + 2) & (steps - 1)), *first)
         multiply(*second)
         return carry
 
@@ -184,16 +198,16 @@
     return ref[pl.ds(j, LEV, stride=rows), :]
 
 
-def base_row(total, j):
-    return row_of(total, j, BASE_ROWS)
-
-
-def two_rows(sums, j):
+def base_row(sums, n, j):
+    return sums[n, pl.ds(j, LEV, stride=BASE_ROWS), :]
+
+
+def two_rows(sums, n, j):
     if j == 0:
-        return base_row(sums[0], 0)
+        return base_row(sums, n, 0)
     if j == BASE_ROWS:
-        return base_row(sums[1], j - 1)
-    return base_row(sums[0], j) + base_row(sums[1], j - 1)
+        return base_row(sums, n + 1, j - 1)
+    return base_row(sums, n, j) + base_row(sums, n + 1, j - 1)
 
 
 def even(axis):
@@ -204,8 +218,8 @@
     is_even = even("lat")
     at_a, at_b = jnp.where(is_even, low, top), jnp.where(is_even, top, low)
     for r in range(HALF):
-        a_ref[r] = source_ref[at_a + r]
-        b_ref[r] = source_ref[at_b + r]
+        a_ref[r * LEV : (r + 1) * LEV, :] = source_ref[at_a + r]
+        b_ref[r * LEV : (r + 1) * LEV, :] = source_ref[at_b + r]
 
 
 def push_rows(g_ref, weight_ref, wide):
@@ -229,11 +243,11 @@
 
 
 def scatter_rhs_kernel(
-    got_ref, sigma_ref, lat_ref, mid_ref, a_ref, b_ref, turned_ref, sigma_rows_ref, lat_weight_ref, *refs
+    got_ref, local_ref, mid_ref, a_ref, b_ref, turned_ref, sigma_rows_ref, lat_weight_ref, *refs
 ):
-    work, sums, (g, wide) = refs[:10], refs[10:12], refs[12:]
+    work, (sums, g, wide) = refs[:8], refs[8:]
     turned_ref[...] = got_ref[...].T
-    scale = lat_ref[...]
+    scale = local_ref[CELLS:, :]
     factor = -0.5 / (scale * scale)
     norm = jnp.ones_like(factor)
     for d in range(1, HALF + 1):
@@ -244,28 +258,35 @@
     lat_weight_ref[0] = inverse
     for d in range(1, HALF + 1):
         lat_weight_ref[d] = lat_weight_ref[d] * inverse
+    sums[...] = jnp.zeros_like(sums)
     accumulate(turned_ref, RHS, work, sums)
     for j in range(ROWS):
-        sigma = row_of(sigma_ref, j)
+        sigma = row_of(local_ref, j)
         sigma_rows_ref[j] = sigma
-        g[j] = sigma * two_rows(sums, j)
+        g[j] = sigma * two_rows(sums, 0, j)
     push_out(g, lat_weight_ref, wide, mid_ref, a_ref, b_ref)
 
 
-def scatter_pair_kernel(blocks, turned_ref, out_ref, *refs):
-    work, sums = refs[:10], refs[10:]
-    accumulate(turned_ref, blocks, work, sums)
+OPERATOR = DIAG + EAST + NORTH
+CUTS = (0, 16, 32, CAP)
+
+
+def operator_kernel(begin, end, turned_ref, *refs):
+    refs = list(refs)
+    before_ref = refs.pop(0) if begin > 0 else None
+    if end < CAP:
+        sums, work = refs[0], refs[1:]
+    else:
+        outs, sums, work = refs[:5], refs[5], refs[6:]
+    sums[...] = jnp.zeros_like(sums) if begin == 0 else before_ref[...]
+    accumulate(turned_ref, OPERATOR, work, sums, begin, end)
+    if end < CAP:
+        return
     for j in range(ROWS):
-        out_ref[j] = two_rows(sums, j)
-
-
-def scatter_plain_kernel(blocks, turned_ref, *refs):
-    count = len(blocks)
-    outs, work, sums = refs[:count], refs[count : count + 10], refs[count + 10 :]
-    accumulate(turned_ref, blocks, work, sums)
-    for j in range(ROWS):
-        for out_ref, total in zip(outs, sums):
-            out_ref[j] = base_row(total, j) if j < BASE_ROWS else jnp.zeros((LEV, COLS), F32)
+        outs[0][j] = two_rows(sums, 0, j)
+        outs[1][j] = two_rows(sums, 2, j)
+        for n in range(3):
+            outs[2 + n][j] = base_row(sums, 4 + n, j) if j < BASE_ROWS else jnp.zeros((LEV, COLS), F32)
 
 
 def field_shape(rows=ROWS):
@@ -276,60 +297,60 @@
     return [
         pltpu.VMEM((ROWS_PAD, CHUNK * 128), BF16),
         pltpu.VMEM((count * 128, CHUNK * 128), BF16),
-        pltpu.VMEM((count * 128, CHUNK * 128), BF16),
         pltpu.VMEM((ROWS_PAD, CHUNK * 128), F8),
         pltpu.VMEM((count * 128, CHUNK * 128), F8),
-    ] * 2 + [pltpu.VMEM((ROWS_PAD, 128), F32)] * count
+    ] * 2
+
+
+def rim_shape():
+    return jax.ShapeDtypeStruct((HALF * LEV, COLS), F32)
+
+
+def sums_shape(count):
+    return (count, ROWS_PAD, COLS)
 
 
 def row_scratch():
     return [pltpu.VMEM((ROWS, LEV, COLS), F32), pltpu.VMEM((ROWS + 2 * HALF, LEV, COLS), F32)]
 
 
-def scatter_cost(count):
+def scatter_cost(count, slots=CAP):
     return pl.CostEstimate(
-        flops=4 * ROWS_PAD * OWNERS * CAP * 128 * count, bytes_accessed=2 * 1024 * 1024, transcendentals=0
+        flops=4 * ROWS_PAD * OWNERS * slots * 128 * count, bytes_accessed=2 * 1024 * 1024, transcendentals=0
     )
 
 
-def scatter_rhs(got, sigma, scale_lat):
+def scatter_rhs(got, local):
     return pl.pallas_call(
         scatter_rhs_kernel,
         out_shape=[
             field_shape(),
-            field_shape(HALF),
-            field_shape(HALF),
+            rim_shape(),
+            rim_shape(),
             jax.ShapeDtypeStruct((FIELDS * CAP, OWNERS), F32),
             field_shape(),
             jax.ShapeDtypeStruct((HALF + 1, ROWS, COLS), F32),
         ],
-        scratch_shapes=scatter_scratch(2) + row_scratch(),
+        scratch_shapes=scatter_scratch(2) + [pltpu.VMEM(sums_shape(2), F32)] + row_scratch(),
         compiler_params=params(9),
         cost_estimate=scatter_cost(2),
         name="scatter_rhs",
-    )(got, sigma, scale_lat)
-
-
-def scatter_pair(turned, blocks, name):
-    return pl.pallas_call(
-        functools.partial(scatter_pair_kernel, blocks),
-        out_shape=field_shape(),
-        scratch_shapes=scatter_scratch(2),
-        compiler_params=params(9),
-        cost_estimate=scatter_cost(2),
-        name=name,
-    )(turned)
-
-
-def scatter_plain(turned, blocks, name):
-    return pl.pallas_call(
-        functools.partial(scatter_plain_kernel, blocks),
-        out_shape=[field_shape()] * len(blocks),
-        scratch_shapes=scatter_scratch(len(blocks)),
-        compiler_params=params(9),
-        cost_estimate=scatter_cost(len(blocks)),
-        name=name,
-    )(turned)
+    )(got, local)
+
+
+def scatter_operator(turned, part, *before):
+    begin, end = CUTS[part], CUTS[part + 1]
+    count = len(OPERATOR)
+    final = end == CAP
+    running = jax.ShapeDtypeStruct(sums_shape(count), F32)
+    return pl.pallas_call(
+        functools.partial(operator_kernel, begin, end),
+        out_shape=[field_shape()] * 5 if final else running,
+        scratch_shapes=([pltpu.VMEM(sums_shape(count), F32)] if final else []) + scatter_scratch(count),
+        compiler_params=params(18),
+        cost_estimate=scatter_cost(count, end - begin),
+        name="scatter_operator",
+    )(turned, *before)
 
 
 NEAR_TILE = tuple(range(0, 160, 16)) + (224, 240)
@@ -454,8 +475,8 @@
         out_shape=[
             field_shape(),
             field_shape(),
-            field_shape(HALF),
-            field_shape(HALF),
+            rim_shape(),
+            rim_shape(),
             jax.ShapeDtypeStruct((LEV, COLS), F32),
         ],
         scratch_shapes=[pltpu.VMEM((4, 32, 256), F32), pltpu.VMEM((4, 64, 256), BF16)],
@@ -470,9 +491,9 @@
     at_b = jnp.where(is_even, 0, ROWS - HALF)
     q_ref[...] = mid_ref[...]
     for r in range(HALF):
-        q_ref[at_a + r] += ra_ref[r]
+        q_ref[at_a + r] += ra_ref[r * LEV : (r + 1) * LEV, :]
     for r in range(HALF):
-        q_ref[at_b + r] += rb_ref[r]
+        q_ref[at_b + r] += rb_ref[r * LEV : (r + 1) * LEV, :]
     lane = iota((LEV, COLS), 1)
     is_even = even("lon")
     for group in range(ROWS // 3):
@@ -502,8 +523,8 @@
     at_b = jnp.where(is_even, 0, HALF + ROWS)
     wide[HALF : HALF + ROWS] = mid_ref[...]
     for r in range(HALF):
-        wide[at_a + r] = ra_ref[r]
-        wide[at_b + r] = rb_ref[r]
+        wide[at_a + r] = ra_ref[r * LEV : (r + 1) * LEV, :]
+        wide[at_b + r] = rb_ref[r * LEV : (r + 1) * LEV, :]
     group = 4
     for first in range(0, ROWS, group):
         totals = [jnp.zeros((LEV, COLS), F32) for _ in range(group)]
@@ -552,8 +573,8 @@
         out_shape=[
             field_shape(),
             field_shape(),
-            field_shape(HALF),
-            field_shape(HALF),
+            rim_shape(),
+            rim_shape(),
             jax.ShapeDtypeStruct((LEV, COLS), F32),
         ],
         scratch_shapes=row_scratch(),
@@ -650,21 +671,19 @@
     send, scale_lon = lax.optimization_barrier((send, scale_lon))
     got = lax.all_to_all(send, everyone, 0, 0, tiled=True).reshape(OWNERS, FIELDS * CAP)
     scale_a, scale_b = exchange("lon", True, scale_lon, scale_lon)
-    mid, side_a, side_b, turned, sigma, lat_weight = scatter_rhs(
-        got, background_sigma.reshape(CELLS, COLS), scale_lat
-    )
+    local = jnp.concatenate([background_sigma.reshape(CELLS, COLS), scale_lat], axis=0)
+    mid, side_a, side_b, turned, sigma, lat_weight = scatter_rhs(got, local)
     turned, scale_lon, scale_a, scale_b = lax.optimization_barrier((turned, scale_lon, scale_a, scale_b))
     lon_weight = filter_weights(scale_lon, scale_a, scale_b)
 
     from_a, from_b = exchange("lat", False, side_a, side_b)
-    north = scatter_plain(turned, NORTH, "scatter_north")
+    sums = scatter_operator(turned, 0)
     q, side_a, side_b = fold(mid, from_a, from_b)
     from_a, from_b = exchange("lon", True, side_a, side_b)
-    side = scatter_pair(turned, EAST, "scatter_east")
+    sums = scatter_operator(turned, 1, sums)
     start, mid, side_a, side_b, norm0 = lon_both(q, from_a, from_b, lon_weight)
     from_a, from_b = exchange("lat", False, side_a, side_b)
-    diag = scatter_pair(turned, DIAG, "scatter_diag")
-    coefficients = (diag, side, *north)
+    coefficients = scatter_operator(turned, 2, sums)
     image0, mid, side_a, side_b, norm1 = observe(from_a, from_b, mid, lat_weight, sigma, coefficients)
 
     from_a, from_b = exchange("lat", False, side_a, side_b)

time: 132 us -> 122 us (0.924)
  Pallas kernels: 52 us -> 45.3 us
  waiting for transfers between devices: 25.1 us -> 22 us
  local copies, waits for them, and re-layouts: 2.52 us -> 0.85 us
    pallas_call x7, Pallas kernels: 39.6 us -> 33.2 us  [the longest x3 19.4 us: scatter_operator(): pl.pallas_call(functools.partial(operator_kernel, begin, end), out_shape=...]
    ppermute x7, waiting for transfers between devices: 16.8 us -> 14.8 us  [exchange(): from_b = lax.ppermute(side_b, axis, swaps(1))]
    unnamed x9 -> x5, local copies, waits for them, and re-layouts: 2.52 us -> 0.85 us
    another operation x3 -> x0, other arithmetic: 1.51 us -> none  [place(): jnp.stack([jnp.where(live, obs_owner, -1).astype(F32), (obs_level * (BASE...]
  transfers between devices with their start and end apart: 15 -> 15, of which waited for: 6 -> 6; matrix products, arithmetic and copies ran while one was open for 0% -> 1% of each run, Pallas kernels for 28% -> 26%
where the time goes in v3:
time: 122 us
  Pallas kernels  45.3 us (37%)
  starting transfers between devices  34.1 us (28%)
  waiting for transfers between devices  22 us (18%)
  blocking collectives  15.2 us (12%)
  other arithmetic  2.59 us (2%)
  between operations  1.53 us (1%)
    ppermute x7, starting transfers between devices, exchange(): from_b = lax.ppermute(side_b, axis, swaps(1))  20.8 us
    pallas_call x3, Pallas kernels, scatter_operator(): pl.pallas_call(functools.partial(operator_kernel, begin, end), out_shape=...  19.4 us
    all_to_all x1, blocking collectives, body(): sums = lax.all_to_all(sums, everyone, 0, 0, tiled=True)  15.2 us
    ppermute x7, waiting for transfers between devices, exchange(): from_b = lax.ppermute(side_b, axis, swaps(1))  14.8 us
    all_to_all x1, starting transfers between devices, body(): lax.all_to_all(send, everyone, 0, 0, tiled=True)  11.5 us
    pallas_call x1, Pallas kernels, scatter_rhs(): pl.pallas_call(scatter_rhs_kernel, out_shape=[field_shape(), rim_shape(),...  7.67 us
    all_to_all x1, waiting for transfers between devices, body(): lax.all_to_all(send, everyone, 0, 0, tiled=True)  4.63 us
    pallas_call x1, Pallas kernels, place(): pl.pallas_call(place_kernel, out_shape=jax.ShapeDtypeStruct((OWNERS, 1, F...  4.44 us
  transfers between devices with their start and end apart: 15, of which 6 were waited for; matrix products, arithmetic and copies ran while one was open for 1% of the time, Pallas kernels for 26%

profile of v3, /device:TPU:1, one launch (start us, length us, event | category | flops | bytes accessed | tf_op | source)
XLA Modules:
  0.0 121.7 jit_solution(6576461852241214165)
XLA Ops:
  1.3 0.8 convert_bitcast_fusion
  2.1 0.8 select_select_fusion.fields_ref
  2.9 0.8 copy-done
  3.7 4.4 %place_observations.1 = f32[128,1,384]{2,1,0:T(1,128)} custom-call(f32[4,32,128]{2,1,0:T(8,128)S(1)} %select_select_fusion.fields_ref, f32[4,4096]{1,0:T(4,128)S(1)} %copy-done), custom_call_target="tpu_custom_call" | custom-call | tf_op jit(solution)/shard_map/place_observations/pallas_call | solution.py:98
  8.2 11.5 %all-to-all-start = ((f32[128,1,384]{2,1,0:T(1,128)}), f32[128,1,384]{2,1,0:T(1,128)S(1)}, u32[]{:S(2)}, u32[]{:S(2)}) async-start(f32[128,1,384]{2,1,0:T(1,128)} %place_observations.1), calls=%async_computation | async-start | bytes 393216 | tf_op jit(solution)/shard_map/all_to_all | solution.py:672
  19.7 4.9 %collective-permute-start.5 = (f32[24,128]{1,0:T(8,128)}, f32[24,128]{1,0:T(8,128)S(1)}, u32[]{:S(2)}, u32[]{:S(2)}) collective-permute-start(f32[24,128]{1,0:T(8,128)} %lon_ref), channel_id=1, source_target_pairs={{8,16},{16,8},{24,32},{32,24},{40,48},{48,40},{56,64},{64,56},{72,... | collective-permute-start | bytes 36872 | tf_op jit(solution)/shard_map/ppermute | solution.py:621
  24.6 1.0 pad_maximum_fusion.local_ref
  25.6 4.6 %all-to-all-done = f32[128,1,384]{2,1,0:T(1,128)S(1)} async-done(((f32[128,1,384]{2,1,0:T(1,128)}), f32[128,1,384]{2,1,0:T(1,128)S(1)}, u32[]{:S(2)}, u32[]{:S(2)}) %all-to-all-start) | async-done | bytes 196640 | tf_op jit(solution)/shard_map/all_to_all | solution.py:672
  30.2 7.7 %scatter_rhs.1 = (f32[24,25,128]{2,1,0:T(8,128)S(1)}, f32[500,128]{1,0:T(8,128)S(1)}, f32[500,128]{1,0:T(8,128)S(1)}, f32[384,128]{1,0:T(8,128)S(1)}, f32[24,25,...) custom-call(f32[128,384]{1,0:T(8,128)S(1)} %bitcast.19, f32[624,128]{1,0:T(8,128)S(1)} %pad_maximum_fusion.local_ref), custom_call_target="tpu_custom_call" | custom-call | flops 4831838208 | bytes 2097152 | tf_op jit(solution)/shard_map/scatter_rhs/pallas_call | solution.py:324
  37.9 0.8 collective-permute-start
  38.8 2.3 %collective-permute-start.1 = (f32[500,128]{1,0:T(8,128)S(1)}, f32[500,128]{1,0:T(8,128)S(1)}, u32[]{:S(2)}, u32[]{:S(2)}) collective-permute-start(f32[500,128]{1,0:T(8,128)S(1)} %get-tuple-element.50), channel_id=1, source_target_pairs={{1,2},{2,1},{3,4},{4,3},{5,6},{6,5},{9,10},{10,9},{11,12},{12,11},... | collective-permute-start | bytes 768008 | tf_op jit(solution)/shard_map/ppermute | solution.py:621
  41.0 4.6 %scatter_operator.3.refs_0_ = f32[7,576,128]{2,1,0:T(8,128)S(1)} custom-call(f32[384,128]{1,0:T(8,128)S(1)} %get-tuple-element.67.turned_ref), custom_call_target="tpu_custom_call" | custom-call | flops 4227858432 | bytes 2097152 | tf_op jit(solution)/shard_map/scatter_operator/pallas_call | solution.py:346
  45.6 4.7 %scatter_operator.4.refs_0_ = f32[7,576,128]{2,1,0:T(8,128)S(1)} custom-call(f32[384,128]{1,0:T(8,128)S(1)} %get-tuple-element.67.turned_ref, f32[7,576,128]{2,1,0:T(8,128)S(1)} %scatter_operator.3.refs_0_), custom_call_target="tpu_custom_call" | custom-call | flops 4227858432 | bytes 2097152 | tf_op jit(solution)/shard_map/scatter_operator/pallas_call | solution.py:346
  50.3 0.4 fold_rims.2
  51.1 1.7 %collective-permute-start.3 = (f32[8,25,128]{2,1,0:T(8,128)S(1)}, f32[8,25,128]{2,1,0:T(8,128)S(1)}, u32[]{:S(2)}, u32[]{:S(2)}) collective-permute-start(f32[8,25,128]{2,1,0:T(8,128)S(1)} %get-tuple-element.53), channel_id=1, source_target_pairs={{8,16},{16,8},{24,32},{32,24},{40,48},{48,40},{56,64},{64,56},{72,... | collective-permute-start | bytes 307208 | tf_op jit(solution)/shard_map/ppermute | solution.py:621
  52.7 4.0 %filter_weights.1 = (bf16[24,256,256]{2,1,0:T(8,128)(2,1)S(1)}, bf16[24,256,256]{2,1,0:T(8,128)(2,1)S(1)}, f32[24,256]{1,0:T(8,128)S(1)}) custom-call(f32[24,128]{1,0:T(8,128)S(1)} %copy-done.1, f32[24,128]{1,0:T(8,128)S(1)} %collective-permute-done.4.a_ref, f32[24,128]{1,0:T(8,128)S(1)} %collective-permute-done.5.b_ref), custom_call_target="tpu_custom_call" | custom-call | flops 2000000000 | bytes 8388608 | tf_op jit(solution)/shard_map/filter_weights/pallas_call | solution.py:424
  56.8 2.4 %collective-permute-done.3.rb_ref = f32[8,25,128]{2,1,0:T(8,128)S(1)} collective-permute-done((f32[8,25,128]{2,1,0:T(8,128)S(1)}, f32[8,25,128]{2,1,0:T(8,128)S(1)}, u32[]{:S(2)}, u32[]{:S(2)}) %collective-permute-start.3) | collective-permute-done | bytes 102432 | tf_op jit(solution)/shard_map/ppermute | solution.py:621
  59.1 1.2 %lon_transpose_and_lon.2 = (f32[24,25,128]{2,1,0:T(8,128)S(1)}, f32[24,25,128]{2,1,0:T(8,128)S(1)}, f32[500,128]{1,0:T(8,128)S(1)}, f32[500,128]{1,0:T(8,128)S(1)}, f32[25,128]{1,0:T(8,128)S(1)}) custom-call(f32[24,25,128]{2,1,0:T(8,128)S(1)} %get-tuple-element.51.q_ref, f32[8,25,128]{2,1,0:T(8,128)S(1)} %collective-permute-done.2.ra_ref, ...), custom_call_target="tpu_custom_call" | custom-call | tf_op jit(solution)/shard_map/lon_transpose_and_lon/pallas_call | solution.py:473
  60.7 4.1 %collective-permute-start.7 = (f32[500,128]{1,0:T(8,128)S(1)}, f32[500,128]{1,0:T(8,128)S(1)}, u32[]{:S(2)}, u32[]{:S(2)}) collective-permute-start(f32[500,128]{1,0:T(8,128)S(1)} %get-tuple-element.63), channel_id=1, source_target_pairs={{1,2},{2,1},{3,4},{4,3},{5,6},{6,5},{9,10},{10,9},{11,12},{12,11},... | collective-permute-start | bytes 768008 | tf_op jit(solution)/shard_map/ppermute | solution.py:621
  64.8 10.2 %scatter_operator.5 = (f32[24,25,128]{2,1,0:T(8,128)S(1)}, f32[24,25,128]{2,1,0:T(8,128)S(1)}, f32[24,25,128]{2,1,0:T(8,128)S(1)}, f32[24,25,128]{2,1,0:T(8,128)S(1)}, f32[24,25,128]{2,1,0:T(8,128)S(1)}) custom-call(f32[384,128]{1,0:T(8,128)S(1)} %get-tuple-element.67.turned_ref, f32[7,576,128]{2,1,0:T(8,128)S(1)} %scatter_operator.4.refs_0_), custom_call_target="tpu_custom_call" | custom-call | flops 8455716864 | bytes 2097152 | tf_op jit(solution)/shard_map/scatter_operator/pallas_call | solution.py:346
  75.0 3.7 %lat_and_observe.1 = (f32[24,25,128]{2,1,0:T(8,128)S(1)}, f32[24,25,128]{2,1,0:T(8,128)S(1)}, f32[500,128]{1,0:T(8,128)S(1)}, f32[500,128]{1,0:T(8,128)S(1)}, f32[25,128]{1,0:T(8,128)S(1)}) custom-call(f32[500,128]{1,0:T(8,128)S(1)} %collective-permute-done.6.ra_ref, f32[500,128]{1,0:T(8,128)S(1)} %collective-permute-done.7.rb_ref, ...), custom_call_target="tpu_custom_call" | custom-call | tf_op jit(solution)/shard_map/lat_and_observe/pallas_call | solution.py:571
  78.8 2.4 %collective-permute-start.9 = (f32[500,128]{1,0:T(8,128)S(1)}, f32[500,128]{1,0:T(8,128)S(1)}, u32[]{:S(2)}, u32[]{:S(2)}) collective-permute-start(f32[500,128]{1,0:T(8,128)S(1)} %get-tuple-element.75), channel_id=1, source_target_pairs={{1,2},{2,1},{3,4},{4,3},{5,6},{6,5},{9,10},{10,9},{11,12},{12,11},... | collective-permute-start | bytes 768008 | tf_op jit(solution)/shard_map/ppermute | solution.py:621
  81.2 5.2 %collective-permute-done.9.rb_ref = f32[500,128]{1,0:T(8,128)S(1)} collective-permute-done((f32[500,128]{1,0:T(8,128)S(1)}, f32[500,128]{1,0:T(8,128)S(1)}, u32[]{:S(2)}, u32[]{:S(2)}) %collective-permute-start.9) | collective-permute-done | bytes 256032 | tf_op jit(solution)/shard_map/ppermute | solution.py:621
  86.9 1.2 collective-permute-start.11
  88.1 2.6 %collective-permute-done.10.ra_ref = f32[8,25,128]{2,1,0:T(8,128)S(1)} collective-permute-done((f32[8,25,128]{2,1,0:T(8,128)S(1)}, f32[8,25,128]{2,1,0:T(8,128)S(1)}, u32[]{:S(2)}, u32[]{:S(2)}) %collective-permute-start.10) | collective-permute-done | bytes 102432 | tf_op jit(solution)/shard_map/ppermute | solution.py:622
  90.7 3.4 %collective-permute-done.11.rb_ref = f32[8,25,128]{2,1,0:T(8,128)S(1)} collective-permute-done((f32[8,25,128]{2,1,0:T(8,128)S(1)}, f32[8,25,128]{2,1,0:T(8,128)S(1)}, u32[]{:S(2)}, u32[]{:S(2)}) %collective-permute-start.11) | collective-permute-done | bytes 102432 | tf_op jit(solution)/shard_map/ppermute | solution.py:621
  94.2 1.2 %lon_transpose_and_lon.3 = (f32[24,25,128]{2,1,0:T(8,128)S(1)}, f32[24,25,128]{2,1,0:T(8,128)S(1)}, f32[500,128]{1,0:T(8,128)S(1)}, f32[500,128]{1,0:T(8,128)S(1)}, f32[25,128]{1,0:T(8,128)S(1)}) custom-call(f32[24,25,128]{2,1,0:T(8,128)S(1)} %get-tuple-element.76.q_ref, f32[8,25,128]{2,1,0:T(8,128)S(1)} %collective-permute-done.10.ra_ref, ...), custom_call_target="tpu_custom_call" | custom-call | tf_op jit(solution)/shard_map/lon_transpose_and_lon/pallas_call | solution.py:473
  95.5 4.3 %collective-permute-start.13 = (f32[500,128]{1,0:T(8,128)S(1)}, f32[500,128]{1,0:T(8,128)S(1)}, u32[]{:S(2)}, u32[]{:S(2)}) collective-permute-start(f32[500,128]{1,0:T(8,128)S(1)} %get-tuple-element.80), channel_id=1, source_target_pairs={{1,2},{2,1},{3,4},{4,3},{5,6},{6,5},{9,10},{10,9},{11,12},{12,11},... | collective-permute-start | bytes 768008 | tf_op jit(solution)/shard_map/ppermute | solution.py:621
  99.8 3.7 %collective-permute-done.13.rb_ref = f32[500,128]{1,0:T(8,128)S(1)} collective-permute-done((f32[500,128]{1,0:T(8,128)S(1)}, f32[500,128]{1,0:T(8,128)S(1)}, u32[]{:S(2)}, u32[]{:S(2)}) %collective-permute-start.13) | collective-permute-done | bytes 256032 | tf_op jit(solution)/shard_map/ppermute | solution.py:621
  103.6 1.8 %lat_and_moments.1 = (f32[24,25,128]{2,1,0:T(8,128)S(1)}, f32[128,128]{1,0:T(8,128)S(1)}) custom-call(f32[500,128]{1,0:T(8,128)S(1)} %collective-permute-done.12.ra_ref, f32[500,128]{1,0:T(8,128)S(1)} %collective-permute-done.13.rb_ref, f32[24,25,128]{2,1,0:T(8,128)S(1)} %get-tuple-element.81.e_ref, f32[21,24,128]{2,1,0:T(8,128)S(1)} %get-tuple-element.65.weight_ref, ...), custom_call_target="tpu_custom_call" | custom-call | tf_op jit(solution)/shard_map/lat_and_moments/pallas_call | solution.py:602
  105.3 15.2 %all_to_all.16 = f32[128,1,128]{2,1,0:T(1,128)S(1)} all-to-all(f32[128,1,128]{2,1,0:T(1,128)S(1)} %bitcast.20), channel_id=1, replica_groups=mesh['lon'=16,'lat'=8] {'lon','lat'}, dimensions={0} | all-to-all | bytes 131072 | tf_op jit(solution)/shard_map/all_to_all | solution.py:695
  120.5 1.1 combine.1
  (22 shorter events, 1.4 us)
Async XLA Ops:
  2.9 0.8 copy-start
  8.2 22.0 %all-to-all-start = ((f32[128,1,384]{2,1,0:T(1,128)}), f32[128,1,384]{2,1,0:T(1,128)S(1)}, u32[]{:S(2)}, u32[]{:S(2)}) async-start(f32[128,1,384]{2,1,0:T(1,128)} %place_observations.1), calls=%async_computation | async-start | bytes 393216 | tf_op jit(solution)/shard_map/all_to_all | solution.py:672
  19.7 18.2 %collective-permute-start.5 = (f32[24,128]{1,0:T(8,128)}, f32[24,128]{1,0:T(8,128)S(1)}, u32[]{:S(2)}, u32[]{:S(2)}) collective-permute-start(f32[24,128]{1,0:T(8,128)} %lon_ref), channel_id=1, source_target_pairs={{8,16},{16,8},{24,32},{32,24},{40,48},{48,40},{56,64},{64,56},{72,... | collective-permute-start | bytes 36872 | tf_op jit(solution)/shard_map/ppermute | solution.py:621
  24.6 13.4 %collective-permute-start.4 = (f32[24,128]{1,0:T(8,128)}, f32[24,128]{1,0:T(8,128)S(1)}, u32[]{:S(2)}, u32[]{:S(2)}) collective-permute-start(f32[24,128]{1,0:T(8,128)} %lon_ref), channel_id=1, source_target_pairs={{0,8},{8,0},{16,24},{24,16},{32,40},{40,32},{48,56},{56,48},{64,72... | collective-permute-start | bytes 36872 | tf_op jit(solution)/shard_map/ppermute | solution.py:622
  37.9 12.4 %collective-permute-start = (f32[500,128]{1,0:T(8,128)S(1)}, f32[500,128]{1,0:T(8,128)S(1)}, u32[]{:S(2)}, u32[]{:S(2)}) collective-permute-start(f32[500,128]{1,0:T(8,128)S(1)} %get-tuple-element.49), channel_id=1, source_target_pairs={{0,1},{1,0},{2,3},{3,2},{4,5},{5,4},{6,7},{7,6},{8,9},{9,8},{10,11... | collective-permute-start | bytes 768008 | tf_op jit(solution)/shard_map/ppermute | solution.py:622
  38.8 11.6 %collective-permute-start.1 = (f32[500,128]{1,0:T(8,128)S(1)}, f32[500,128]{1,0:T(8,128)S(1)}, u32[]{:S(2)}, u32[]{:S(2)}) collective-permute-start(f32[500,128]{1,0:T(8,128)S(1)} %get-tuple-element.50), channel_id=1, source_target_pairs={{1,2},{2,1},{3,4},{4,3},{5,6},{6,5},{9,10},{10,9},{11,12},{12,11},... | collective-permute-start | bytes 768008 | tf_op jit(solution)/shard_map/ppermute | solution.py:621
  45.6 7.1 %copy-start.1 = (f32[24,128]{1,0:T(8,128)S(1)}, f32[24,128]{1,0:T(8,128)}, u32[]{:S(2)}) copy-start(f32[24,128]{1,0:T(8,128)} %lon_ref) | copy-start | bytes 36868
  50.7 6.0 %collective-permute-start.2 = (f32[8,25,128]{2,1,0:T(8,128)S(1)}, f32[8,25,128]{2,1,0:T(8,128)S(1)}, u32[]{:S(2)}, u32[]{:S(2)}) collective-permute-start(f32[8,25,128]{2,1,0:T(8,128)S(1)} %get-tuple-element.52), channel_id=1, source_target_pairs={{0,8},{8,0},{16,24},{24,16},{32,40},{40,32},{48,56},{56,48},{64,72... | collective-permute-start | bytes 307208 | tf_op jit(solution)/shard_map/ppermute | solution.py:622
  51.1 8.1 %collective-permute-start.3 = (f32[8,25,128]{2,1,0:T(8,128)S(1)}, f32[8,25,128]{2,1,0:T(8,128)S(1)}, u32[]{:S(2)}, u32[]{:S(2)}) collective-permute-start(f32[8,25,128]{2,1,0:T(8,128)S(1)} %get-tuple-element.53), channel_id=1, source_target_pairs={{8,16},{16,8},{24,32},{32,24},{40,48},{48,40},{56,64},{64,56},{72,... | collective-permute-start | bytes 307208 | tf_op jit(solution)/shard_map/ppermute | solution.py:621
  60.4 14.7 %collective-permute-start.6 = (f32[500,128]{1,0:T(8,128)S(1)}, f32[500,128]{1,0:T(8,128)S(1)}, u32[]{:S(2)}, u32[]{:S(2)}) collective-permute-start(f32[500,128]{1,0:T(8,128)S(1)} %get-tuple-element.62), channel_id=1, source_target_pairs={{0,1},{1,0},{2,3},{3,2},{4,5},{5,4},{6,7},{7,6},{8,9},{9,8},{10,11... | collective-permute-start | bytes 768008 | tf_op jit(solution)/shard_map/ppermute | solution.py:622
  60.7 14.3 %collective-permute-start.7 = (f32[500,128]{1,0:T(8,128)S(1)}, f32[500,128]{1,0:T(8,128)S(1)}, u32[]{:S(2)}, u32[]{:S(2)}) collective-permute-start(f32[500,128]{1,0:T(8,128)S(1)} %get-tuple-element.63), channel_id=1, source_target_pairs={{1,2},{2,1},{3,4},{4,3},{5,6},{6,5},{9,10},{10,9},{11,12},{12,11},... | collective-permute-start | bytes 768008 | tf_op jit(solution)/shard_map/ppermute | solution.py:621
  78.7 2.5 %collective-permute-start.8 = (f32[500,128]{1,0:T(8,128)S(1)}, f32[500,128]{1,0:T(8,128)S(1)}, u32[]{:S(2)}, u32[]{:S(2)}) collective-permute-start(f32[500,128]{1,0:T(8,128)S(1)} %get-tuple-element.74), channel_id=1, source_target_pairs={{0,1},{1,0},{2,3},{3,2},{4,5},{5,4},{6,7},{7,6},{8,9},{9,8},{10,11... | collective-permute-start | bytes 768008 | tf_op jit(solution)/shard_map/ppermute | solution.py:622
  78.8 7.6 %collective-permute-start.9 = (f32[500,128]{1,0:T(8,128)S(1)}, f32[500,128]{1,0:T(8,128)S(1)}, u32[]{:S(2)}, u32[]{:S(2)}) collective-permute-start(f32[500,128]{1,0:T(8,128)S(1)} %get-tuple-element.75), channel_id=1, source_target_pairs={{1,2},{2,1},{3,4},{4,3},{5,6},{6,5},{9,10},{10,9},{11,12},{12,11},... | collective-permute-start | bytes 768008 | tf_op jit(solution)/shard_map/ppermute | solution.py:621
  86.8 3.9 %collective-permute-start.10 = (f32[8,25,128]{2,1,0:T(8,128)S(1)}, f32[8,25,128]{2,1,0:T(8,128)S(1)}, u32[]{:S(2)}, u32[]{:S(2)}) collective-permute-start(f32[8,25,128]{2,1,0:T(8,128)S(1)} %get-tuple-element.77), channel_id=1, source_target_pairs={{0,8},{8,0},{16,24},{24,16},{32,40},{40,32},{48,56},{56,48},{64,72... | collective-permute-start | bytes 307208 | tf_op jit(solution)/shard_map/ppermute | solution.py:622
  86.9 7.2 %collective-permute-start.11 = (f32[8,25,128]{2,1,0:T(8,128)S(1)}, f32[8,25,128]{2,1,0:T(8,128)S(1)}, u32[]{:S(2)}, u32[]{:S(2)}) collective-permute-start(f32[8,25,128]{2,1,0:T(8,128)S(1)} %get-tuple-element.78), channel_id=1, source_target_pairs={{8,16},{16,8},{24,32},{32,24},{40,48},{48,40},{56,64},{64,56},{72,... | collective-permute-start | bytes 307208 | tf_op jit(solution)/shard_map/ppermute | solution.py:621
  95.4 4.4 %collective-permute-start.12 = (f32[500,128]{1,0:T(8,128)S(1)}, f32[500,128]{1,0:T(8,128)S(1)}, u32[]{:S(2)}, u32[]{:S(2)}) collective-permute-start(f32[500,128]{1,0:T(8,128)S(1)} %get-tuple-element.79), channel_id=1, source_target_pairs={{0,1},{1,0},{2,3},{3,2},{4,5},{5,4},{6,7},{7,6},{8,9},{9,8},{10,11... | collective-permute-start | bytes 768008 | tf_op jit(solution)/shard_map/ppermute | solution.py:622
  95.5 8.1 %collective-permute-start.13 = (f32[500,128]{1,0:T(8,128)S(1)}, f32[500,128]{1,0:T(8,128)S(1)}, u32[]{:S(2)}, u32[]{:S(2)}) collective-permute-start(f32[500,128]{1,0:T(8,128)S(1)} %get-tuple-element.80), channel_id=1, source_target_pairs={{1,2},{2,1},{3,4},{4,3},{5,6},{6,5},{9,10},{10,9},{11,12},{12,11},... | collective-permute-start | bytes 768008 | tf_op jit(solution)/shard_map/ppermute | solution.py:621

commit v4 on v3

--- a/solution.py
+++ b/solution.py
@@ -268,7 +268,7 @@
 
 
 OPERATOR = DIAG + EAST + NORTH
-CUTS = (0, 16, 32, CAP)
+CUTS = (0, 16, 40, CAP)
 
 
 def operator_kernel(begin, end, turned_ref, *refs):

time: 122 us -> 121 us (level)
  transfers between devices with their start and end apart: 15 -> 15, of which waited for: 6 -> 6; matrix products, arithmetic and copies ran while one was open for 1% -> 1% of each run, Pallas kernels for 26% -> 25%
where the time goes in v4:
time: 121 us
  Pallas kernels  44.2 us (37%)
  starting transfers between devices  34.2 us (28%)
  waiting for transfers between devices  22 us (18%)
  blocking collectives  15.2 us (13%)
  other arithmetic  2.59 us (2%)
  between operations  1.53 us (1%)
    ppermute x7, starting transfers between devices, exchange(): from_b = lax.ppermute(side_b, axis, swaps(1))  20.8 us
    pallas_call x3, Pallas kernels, scatter_operator(): pl.pallas_call(functools.partial(operator_kernel, begin, end), out_shape=...  18.3 us
    all_to_all x1, blocking collectives, body(): sums = lax.all_to_all(sums, everyone, 0, 0, tiled=True)  15.2 us
    ppermute x7, waiting for transfers between devices, exchange(): from_b = lax.ppermute(side_b, axis, swaps(1))  14.8 us
    all_to_all x1, starting transfers between devices, body(): lax.all_to_all(send, everyone, 0, 0, tiled=True)  11.5 us
    pallas_call x1, Pallas kernels, scatter_rhs(): pl.pallas_call(scatter_rhs_kernel, out_shape=[field_shape(), rim_shape(),...  7.67 us
    all_to_all x1, waiting for transfers between devices, body(): lax.all_to_all(send, everyone, 0, 0, tiled=True)  4.63 us
    pallas_call x1, Pallas kernels, place(): pl.pallas_call(place_kernel, out_shape=jax.ShapeDtypeStruct((OWNERS, 1, F...  4.44 us
  transfers between devices with their start and end apart: 15, of which 6 were waited for; matrix products, arithmetic and copies ran while one was open for 1% of the time, Pallas kernels for 25%

profile of v4, /device:TPU:1, one launch (start us, length us, event | category | flops | bytes accessed | tf_op | source)
XLA Modules:
  0.0 120.5 jit_solution(2504852164336784303)
XLA Ops:
  1.3 0.8 convert_bitcast_fusion
  2.1 0.8 select_select_fusion.fields_ref
  2.9 0.8 copy-done
  3.7 4.4 %place_observations.1 = f32[128,1,384]{2,1,0:T(1,128)} custom-call(f32[4,32,128]{2,1,0:T(8,128)S(1)} %select_select_fusion.fields_ref, f32[4,4096]{1,0:T(4,128)S(1)} %copy-done), custom_call_target="tpu_custom_call" | custom-call | tf_op jit(solution)/shard_map/place_observations/pallas_call | solution.py:98
  8.2 11.5 %all-to-all-start = ((f32[128,1,384]{2,1,0:T(1,128)}), f32[128,1,384]{2,1,0:T(1,128)S(1)}, u32[]{:S(2)}, u32[]{:S(2)}) async-start(f32[128,1,384]{2,1,0:T(1,128)} %place_observations.1), calls=%async_computation | async-start | bytes 393216 | tf_op jit(solution)/shard_map/all_to_all | solution.py:672
  19.7 4.9 %collective-permute-start.5 = (f32[24,128]{1,0:T(8,128)}, f32[24,128]{1,0:T(8,128)S(1)}, u32[]{:S(2)}, u32[]{:S(2)}) collective-permute-start(f32[24,128]{1,0:T(8,128)} %lon_ref), channel_id=1, source_target_pairs={{8,16},{16,8},{24,32},{32,24},{40,48},{48,40},{56,64},{64,56},{72,... | collective-permute-start | bytes 36872 | tf_op jit(solution)/shard_map/ppermute | solution.py:621
  24.6 1.0 pad_maximum_fusion.local_ref
  25.6 4.6 %all-to-all-done = f32[128,1,384]{2,1,0:T(1,128)S(1)} async-done(((f32[128,1,384]{2,1,0:T(1,128)}), f32[128,1,384]{2,1,0:T(1,128)S(1)}, u32[]{:S(2)}, u32[]{:S(2)}) %all-to-all-start) | async-done | bytes 196640 | tf_op jit(solution)/shard_map/all_to_all | solution.py:672
  30.2 7.7 %scatter_rhs.1 = (f32[24,25,128]{2,1,0:T(8,128)S(1)}, f32[500,128]{1,0:T(8,128)S(1)}, f32[500,128]{1,0:T(8,128)S(1)}, f32[384,128]{1,0:T(8,128)S(1)}, f32[24,25,...) custom-call(f32[128,384]{1,0:T(8,128)S(1)} %bitcast.19, f32[624,128]{1,0:T(8,128)S(1)} %pad_maximum_fusion.local_ref), custom_call_target="tpu_custom_call" | custom-call | flops 4831838208 | bytes 2097152 | tf_op jit(solution)/shard_map/scatter_rhs/pallas_call | solution.py:324
  37.9 0.8 collective-permute-start
  38.8 2.3 %collective-permute-start.1 = (f32[500,128]{1,0:T(8,128)S(1)}, f32[500,128]{1,0:T(8,128)S(1)}, u32[]{:S(2)}, u32[]{:S(2)}) collective-permute-start(f32[500,128]{1,0:T(8,128)S(1)} %get-tuple-element.50), channel_id=1, source_target_pairs={{1,2},{2,1},{3,4},{4,3},{5,6},{6,5},{9,10},{10,9},{11,12},{12,11},... | collective-permute-start | bytes 768008 | tf_op jit(solution)/shard_map/ppermute | solution.py:621
  41.0 4.6 %scatter_operator.3.refs_0_ = f32[7,576,128]{2,1,0:T(8,128)S(1)} custom-call(f32[384,128]{1,0:T(8,128)S(1)} %get-tuple-element.67.turned_ref), custom_call_target="tpu_custom_call" | custom-call | flops 4227858432 | bytes 2097152 | tf_op jit(solution)/shard_map/scatter_operator/pallas_call | solution.py:346
  45.6 6.7 %scatter_operator.4.refs_0_ = f32[7,576,128]{2,1,0:T(8,128)S(1)} custom-call(f32[384,128]{1,0:T(8,128)S(1)} %get-tuple-element.67.turned_ref, f32[7,576,128]{2,1,0:T(8,128)S(1)} %scatter_operator.3.refs_0_), custom_call_target="tpu_custom_call" | custom-call | flops 6341787648 | bytes 2097152 | tf_op jit(solution)/shard_map/scatter_operator/pallas_call | solution.py:346
  52.4 0.4 fold_rims.2
  53.2 1.7 %collective-permute-start.3 = (f32[8,25,128]{2,1,0:T(8,128)S(1)}, f32[8,25,128]{2,1,0:T(8,128)S(1)}, u32[]{:S(2)}, u32[]{:S(2)}) collective-permute-start(f32[8,25,128]{2,1,0:T(8,128)S(1)} %get-tuple-element.53), channel_id=1, source_target_pairs={{8,16},{16,8},{24,32},{32,24},{40,48},{48,40},{56,64},{64,56},{72,... | collective-permute-start | bytes 307208 | tf_op jit(solution)/shard_map/ppermute | solution.py:621
  54.8 4.0 %filter_weights.1 = (bf16[24,256,256]{2,1,0:T(8,128)(2,1)S(1)}, bf16[24,256,256]{2,1,0:T(8,128)(2,1)S(1)}, f32[24,256]{1,0:T(8,128)S(1)}) custom-call(f32[24,128]{1,0:T(8,128)S(1)} %copy-done.1, f32[24,128]{1,0:T(8,128)S(1)} %collective-permute-done.4.a_ref, f32[24,128]{1,0:T(8,128)S(1)} %collective-permute-done.5.b_ref), custom_call_target="tpu_custom_call" | custom-call | flops 2000000000 | bytes 8388608 | tf_op jit(solution)/shard_map/filter_weights/pallas_call | solution.py:424
  58.8 2.4 %collective-permute-done.3.rb_ref = f32[8,25,128]{2,1,0:T(8,128)S(1)} collective-permute-done((f32[8,25,128]{2,1,0:T(8,128)S(1)}, f32[8,25,128]{2,1,0:T(8,128)S(1)}, u32[]{:S(2)}, u32[]{:S(2)}) %collective-permute-start.3) | collective-permute-done | bytes 102432 | tf_op jit(solution)/shard_map/ppermute | solution.py:621
  61.2 1.2 %lon_transpose_and_lon.2 = (f32[24,25,128]{2,1,0:T(8,128)S(1)}, f32[24,25,128]{2,1,0:T(8,128)S(1)}, f32[500,128]{1,0:T(8,128)S(1)}, f32[500,128]{1,0:T(8,128)S(1)}, f32[25,128]{1,0:T(8,128)S(1)}) custom-call(f32[24,25,128]{2,1,0:T(8,128)S(1)} %get-tuple-element.51.q_ref, f32[8,25,128]{2,1,0:T(8,128)S(1)} %collective-permute-done.2.ra_ref, ...), custom_call_target="tpu_custom_call" | custom-call | tf_op jit(solution)/shard_map/lon_transpose_and_lon/pallas_call | solution.py:473
  62.8 4.1 %collective-permute-start.7 = (f32[500,128]{1,0:T(8,128)S(1)}, f32[500,128]{1,0:T(8,128)S(1)}, u32[]{:S(2)}, u32[]{:S(2)}) collective-permute-start(f32[500,128]{1,0:T(8,128)S(1)} %get-tuple-element.63), channel_id=1, source_target_pairs={{1,2},{2,1},{3,4},{4,3},{5,6},{6,5},{9,10},{10,9},{11,12},{12,11},... | collective-permute-start | bytes 768008 | tf_op jit(solution)/shard_map/ppermute | solution.py:621
  66.9 6.9 %scatter_operator.5 = (f32[24,25,128]{2,1,0:T(8,128)S(1)}, f32[24,25,128]{2,1,0:T(8,128)S(1)}, f32[24,25,128]{2,1,0:T(8,128)S(1)}, f32[24,25,128]{2,1,0:T(8,128)S(1)}, f32[24,25,128]{2,1,0:T(8,128)S(1)}) custom-call(f32[384,128]{1,0:T(8,128)S(1)} %get-tuple-element.67.turned_ref, f32[7,576,128]{2,1,0:T(8,128)S(1)} %scatter_operator.4.refs_0_), custom_call_target="tpu_custom_call" | custom-call | flops 6341787648 | bytes 2097152 | tf_op jit(solution)/shard_map/scatter_operator/pallas_call | solution.py:346
  73.9 3.7 %lat_and_observe.1 = (f32[24,25,128]{2,1,0:T(8,128)S(1)}, f32[24,25,128]{2,1,0:T(8,128)S(1)}, f32[500,128]{1,0:T(8,128)S(1)}, f32[500,128]{1,0:T(8,128)S(1)}, f32[25,128]{1,0:T(8,128)S(1)}) custom-call(f32[500,128]{1,0:T(8,128)S(1)} %collective-permute-done.6.ra_ref, f32[500,128]{1,0:T(8,128)S(1)} %collective-permute-done.7.rb_ref, ...), custom_call_target="tpu_custom_call" | custom-call | tf_op jit(solution)/shard_map/lat_and_observe/pallas_call | solution.py:571
  77.7 2.4 %collective-permute-start.9 = (f32[500,128]{1,0:T(8,128)S(1)}, f32[500,128]{1,0:T(8,128)S(1)}, u32[]{:S(2)}, u32[]{:S(2)}) collective-permute-start(f32[500,128]{1,0:T(8,128)S(1)} %get-tuple-element.75), channel_id=1, source_target_pairs={{1,2},{2,1},{3,4},{4,3},{5,6},{6,5},{9,10},{10,9},{11,12},{12,11},... | collective-permute-start | bytes 768008 | tf_op jit(solution)/shard_map/ppermute | solution.py:621
  80.1 5.2 %collective-permute-done.9.rb_ref = f32[500,128]{1,0:T(8,128)S(1)} collective-permute-done((f32[500,128]{1,0:T(8,128)S(1)}, f32[500,128]{1,0:T(8,128)S(1)}, u32[]{:S(2)}, u32[]{:S(2)}) %collective-permute-start.9) | collective-permute-done | bytes 256032 | tf_op jit(solution)/shard_map/ppermute | solution.py:621
  85.8 1.2 collective-permute-start.11
  87.0 2.6 %collective-permute-done.10.ra_ref = f32[8,25,128]{2,1,0:T(8,128)S(1)} collective-permute-done((f32[8,25,128]{2,1,0:T(8,128)S(1)}, f32[8,25,128]{2,1,0:T(8,128)S(1)}, u32[]{:S(2)}, u32[]{:S(2)}) %collective-permute-start.10) | collective-permute-done | bytes 102432 | tf_op jit(solution)/shard_map/ppermute | solution.py:622
  89.6 3.4 %collective-permute-done.11.rb_ref = f32[8,25,128]{2,1,0:T(8,128)S(1)} collective-permute-done((f32[8,25,128]{2,1,0:T(8,128)S(1)}, f32[8,25,128]{2,1,0:T(8,128)S(1)}, u32[]{:S(2)}, u32[]{:S(2)}) %collective-permute-start.11) | collective-permute-done | bytes 102432 | tf_op jit(solution)/shard_map/ppermute | solution.py:621
  93.0 1.2 %lon_transpose_and_lon.3 = (f32[24,25,128]{2,1,0:T(8,128)S(1)}, f32[24,25,128]{2,1,0:T(8,128)S(1)}, f32[500,128]{1,0:T(8,128)S(1)}, f32[500,128]{1,0:T(8,128)S(1)}, f32[25,128]{1,0:T(8,128)S(1)}) custom-call(f32[24,25,128]{2,1,0:T(8,128)S(1)} %get-tuple-element.76.q_ref, f32[8,25,128]{2,1,0:T(8,128)S(1)} %collective-permute-done.10.ra_ref, ...), custom_call_target="tpu_custom_call" | custom-call | tf_op jit(solution)/shard_map/lon_transpose_and_lon/pallas_call | solution.py:473
  94.3 4.3 %collective-permute-start.13 = (f32[500,128]{1,0:T(8,128)S(1)}, f32[500,128]{1,0:T(8,128)S(1)}, u32[]{:S(2)}, u32[]{:S(2)}) collective-permute-start(f32[500,128]{1,0:T(8,128)S(1)} %get-tuple-element.80), channel_id=1, source_target_pairs={{1,2},{2,1},{3,4},{4,3},{5,6},{6,5},{9,10},{10,9},{11,12},{12,11},... | collective-permute-start | bytes 768008 | tf_op jit(solution)/shard_map/ppermute | solution.py:621
  98.7 3.7 %collective-permute-done.13.rb_ref = f32[500,128]{1,0:T(8,128)S(1)} collective-permute-done((f32[500,128]{1,0:T(8,128)S(1)}, f32[500,128]{1,0:T(8,128)S(1)}, u32[]{:S(2)}, u32[]{:S(2)}) %collective-permute-start.13) | collective-permute-done | bytes 256032 | tf_op jit(solution)/shard_map/ppermute | solution.py:621
  102.4 1.8 %lat_and_moments.1 = (f32[24,25,128]{2,1,0:T(8,128)S(1)}, f32[128,128]{1,0:T(8,128)S(1)}) custom-call(f32[500,128]{1,0:T(8,128)S(1)} %collective-permute-done.12.ra_ref, f32[500,128]{1,0:T(8,128)S(1)} %collective-permute-done.13.rb_ref, f32[24,25,128]{2,1,0:T(8,128)S(1)} %get-tuple-element.81.e_ref, f32[21,24,128]{2,1,0:T(8,128)S(1)} %get-tuple-element.65.weight_ref, ...), custom_call_target="tpu_custom_call" | custom-call | tf_op jit(solution)/shard_map/lat_and_moments/pallas_call | solution.py:602
  104.2 15.2 %all_to_all.16 = f32[128,1,128]{2,1,0:T(1,128)S(1)} all-to-all(f32[128,1,128]{2,1,0:T(1,128)S(1)} %bitcast.20), channel_id=1, replica_groups=mesh['lon'=16,'lat'=8] {'lon','lat'}, dimensions={0} | all-to-all | bytes 131072 | tf_op jit(solution)/shard_map/all_to_all | solution.py:695
  119.4 1.1 combine.1
  (22 shorter events, 1.4 us)
Async XLA Ops:
  2.9 0.8 copy-start
  8.2 22.0 %all-to-all-start = ((f32[128,1,384]{2,1,0:T(1,128)}), f32[128,1,384]{2,1,0:T(1,128)S(1)}, u32[]{:S(2)}, u32[]{:S(2)}) async-start(f32[128,1,384]{2,1,0:T(1,128)} %place_observations.1), calls=%async_computation | async-start | bytes 393216 | tf_op jit(solution)/shard_map/all_to_all | solution.py:672
  19.7 18.2 %collective-permute-start.5 = (f32[24,128]{1,0:T(8,128)}, f32[24,128]{1,0:T(8,128)S(1)}, u32[]{:S(2)}, u32[]{:S(2)}) collective-permute-start(f32[24,128]{1,0:T(8,128)} %lon_ref), channel_id=1, source_target_pairs={{8,16},{16,8},{24,32},{32,24},{40,48},{48,40},{56,64},{64,56},{72,... | collective-permute-start | bytes 36872 | tf_op jit(solution)/shard_map/ppermute | solution.py:621
  24.6 13.4 %collective-permute-start.4 = (f32[24,128]{1,0:T(8,128)}, f32[24,128]{1,0:T(8,128)S(1)}, u32[]{:S(2)}, u32[]{:S(2)}) collective-permute-start(f32[24,128]{1,0:T(8,128)} %lon_ref), channel_id=1, source_target_pairs={{0,8},{8,0},{16,24},{24,16},{32,40},{40,32},{48,56},{56,48},{64,72... | collective-permute-start | bytes 36872 | tf_op jit(solution)/shard_map/ppermute | solution.py:622
  37.9 14.5 %collective-permute-start = (f32[500,128]{1,0:T(8,128)S(1)}, f32[500,128]{1,0:T(8,128)S(1)}, u32[]{:S(2)}, u32[]{:S(2)}) collective-permute-start(f32[500,128]{1,0:T(8,128)S(1)} %get-tuple-element.49), channel_id=1, source_target_pairs={{0,1},{1,0},{2,3},{3,2},{4,5},{5,4},{6,7},{7,6},{8,9},{9,8},{10,11... | collective-permute-start | bytes 768008 | tf_op jit(solution)/shard_map/ppermute | solution.py:622
  38.8 13.6 %collective-permute-start.1 = (f32[500,128]{1,0:T(8,128)S(1)}, f32[500,128]{1,0:T(8,128)S(1)}, u32[]{:S(2)}, u32[]{:S(2)}) collective-permute-start(f32[500,128]{1,0:T(8,128)S(1)} %get-tuple-element.50), channel_id=1, source_target_pairs={{1,2},{2,1},{3,4},{4,3},{5,6},{6,5},{9,10},{10,9},{11,12},{12,11},... | collective-permute-start | bytes 768008 | tf_op jit(solution)/shard_map/ppermute | solution.py:621
  45.6 9.2 %copy-start.1 = (f32[24,128]{1,0:T(8,128)S(1)}, f32[24,128]{1,0:T(8,128)}, u32[]{:S(2)}) copy-start(f32[24,128]{1,0:T(8,128)} %lon_ref) | copy-start | bytes 36868
  52.8 6.0 %collective-permute-start.2 = (f32[8,25,128]{2,1,0:T(8,128)S(1)}, f32[8,25,128]{2,1,0:T(8,128)S(1)}, u32[]{:S(2)}, u32[]{:S(2)}) collective-permute-start(f32[8,25,128]{2,1,0:T(8,128)S(1)} %get-tuple-element.52), channel_id=1, source_target_pairs={{0,8},{8,0},{16,24},{24,16},{32,40},{40,32},{48,56},{56,48},{64,72... | collective-permute-start | bytes 307208 | tf_op jit(solution)/shard_map/ppermute | solution.py:622
  53.2 8.1 %collective-permute-start.3 = (f32[8,25,128]{2,1,0:T(8,128)S(1)}, f32[8,25,128]{2,1,0:T(8,128)S(1)}, u32[]{:S(2)}, u32[]{:S(2)}) collective-permute-start(f32[8,25,128]{2,1,0:T(8,128)S(1)} %get-tuple-element.53), channel_id=1, source_target_pairs={{8,16},{16,8},{24,32},{32,24},{40,48},{48,40},{56,64},{64,56},{72,... | collective-permute-start | bytes 307208 | tf_op jit(solution)/shard_map/ppermute | solution.py:621
  62.4 11.4 %collective-permute-start.6 = (f32[500,128]{1,0:T(8,128)S(1)}, f32[500,128]{1,0:T(8,128)S(1)}, u32[]{:S(2)}, u32[]{:S(2)}) collective-permute-start(f32[500,128]{1,0:T(8,128)S(1)} %get-tuple-element.62), channel_id=1, source_target_pairs={{0,1},{1,0},{2,3},{3,2},{4,5},{5,4},{6,7},{7,6},{8,9},{9,8},{10,11... | collective-permute-start | bytes 768008 | tf_op jit(solution)/shard_map/ppermute | solution.py:622
  62.8 11.1 %collective-permute-start.7 = (f32[500,128]{1,0:T(8,128)S(1)}, f32[500,128]{1,0:T(8,128)S(1)}, u32[]{:S(2)}, u32[]{:S(2)}) collective-permute-start(f32[500,128]{1,0:T(8,128)S(1)} %get-tuple-element.63), channel_id=1, source_target_pairs={{1,2},{2,1},{3,4},{4,3},{5,6},{6,5},{9,10},{10,9},{11,12},{12,11},... | collective-permute-start | bytes 768008 | tf_op jit(solution)/shard_map/ppermute | solution.py:621
  77.6 2.5 %collective-permute-start.8 = (f32[500,128]{1,0:T(8,128)S(1)}, f32[500,128]{1,0:T(8,128)S(1)}, u32[]{:S(2)}, u32[]{:S(2)}) collective-permute-start(f32[500,128]{1,0:T(8,128)S(1)} %get-tuple-element.74), channel_id=1, source_target_pairs={{0,1},{1,0},{2,3},{3,2},{4,5},{5,4},{6,7},{7,6},{8,9},{9,8},{10,11... | collective-permute-start | bytes 768008 | tf_op jit(solution)/shard_map/ppermute | solution.py:622
  77.7 7.6 %collective-permute-start.9 = (f32[500,128]{1,0:T(8,128)S(1)}, f32[500,128]{1,0:T(8,128)S(1)}, u32[]{:S(2)}, u32[]{:S(2)}) collective-permute-start(f32[500,128]{1,0:T(8,128)S(1)} %get-tuple-element.75), channel_id=1, source_target_pairs={{1,2},{2,1},{3,4},{4,3},{5,6},{6,5},{9,10},{10,9},{11,12},{12,11},... | collective-permute-start | bytes 768008 | tf_op jit(solution)/shard_map/ppermute | solution.py:621
  85.7 3.9 %collective-permute-start.10 = (f32[8,25,128]{2,1,0:T(8,128)S(1)}, f32[8,25,128]{2,1,0:T(8,128)S(1)}, u32[]{:S(2)}, u32[]{:S(2)}) collective-permute-start(f32[8,25,128]{2,1,0:T(8,128)S(1)} %get-tuple-element.77), channel_id=1, source_target_pairs={{0,8},{8,0},{16,24},{24,16},{32,40},{40,32},{48,56},{56,48},{64,72... | collective-permute-start | bytes 307208 | tf_op jit(solution)/shard_map/ppermute | solution.py:622
  85.8 7.2 %collective-permute-start.11 = (f32[8,25,128]{2,1,0:T(8,128)S(1)}, f32[8,25,128]{2,1,0:T(8,128)S(1)}, u32[]{:S(2)}, u32[]{:S(2)}) collective-permute-start(f32[8,25,128]{2,1,0:T(8,128)S(1)} %get-tuple-element.78), channel_id=1, source_target_pairs={{8,16},{16,8},{24,32},{32,24},{40,48},{48,40},{56,64},{64,56},{72,... | collective-permute-start | bytes 307208 | tf_op jit(solution)/shard_map/ppermute | solution.py:621
  94.2 4.4 %collective-permute-start.12 = (f32[500,128]{1,0:T(8,128)S(1)}, f32[500,128]{1,0:T(8,128)S(1)}, u32[]{:S(2)}, u32[]{:S(2)}) collective-permute-start(f32[500,128]{1,0:T(8,128)S(1)} %get-tuple-element.79), channel_id=1, source_target_pairs={{0,1},{1,0},{2,3},{3,2},{4,5},{5,4},{6,7},{7,6},{8,9},{9,8},{10,11... | collective-permute-start | bytes 768008 | tf_op jit(solution)/shard_map/ppermute | solution.py:622
  94.3 8.1 %collective-permute-start.13 = (f32[500,128]{1,0:T(8,128)S(1)}, f32[500,128]{1,0:T(8,128)S(1)}, u32[]{:S(2)}, u32[]{:S(2)}) collective-permute-start(f32[500,128]{1,0:T(8,128)S(1)} %get-tuple-element.80), channel_id=1, source_target_pairs={{1,2},{2,1},{3,4},{4,3},{5,6},{6,5},{9,10},{10,9},{11,12},{12,11},... | collective-permute-start | bytes 768008 | tf_op jit(solution)/shard_map/ppermute | solution.py:621
